TPU v7x, 32 devices: a whole 2x2x4 slice. The times are simulated.
32 devices in a mesh: slab: 8 (over z, y), snap: 4 (over x, core).
Axes of the slice: x: 2, y: 2, z: 4, core: 2. Of those that a mesh axis runs over, the one named last changes fastest.
Arguments:
- flow: bfloat16 [64, 3, 16, 64, 128], P('snap', None, 'slab'), may hold values from -127 to 127
- large_scale: bfloat16 [3, 16, 64, 128], P(None, 'slab'), may hold values from -6 to 6
- modulation: float32 [64, 64], replicated, may hold values from -15 to 15
- metric: float32 [4, 16, 64, 128], P(None, 'slab'), may hold values from -0.5 to 9.6
Outputs:
- whitened: float32 [64, 3, 16, 64, 128], P(None, None, 'slab', 'snap')
All inputs are finite; a program needn't handle non-finite values.
Results may differ from a plain program's by a relative error of at most 0.0003.
Values may be sent and summed in bfloat16 or wider, within the bound.
No kernel may reach another device: no remote copies, remote signals or barrier semaphores. Data moves between devices by JAX's collectives and lax.ppermute only.
A program may use at most 64 MiB of HBM per device.

v0:
```python
import jax
import jax.numpy as jnp
from jax import lax
from jax.sharding import PartitionSpec as P

NSITER = 6


def with_halo(block, sides, width):
    for axis, dim in sides:
        count = lax.axis_size(axis)
        forward = [(i, i + 1) for i in range(count - 1)]
        backward = [(target, source) for source, target in forward]
        low = lax.ppermute(
            lax.slice_in_dim(block, block.shape[dim] - width, None, axis=dim), axis, forward
        )
        high = lax.ppermute(lax.slice_in_dim(block, 0, width, axis=dim), axis, backward)
        block = jnp.concatenate([low, block, high], axis=dim)
    return block


def vorticity(velocity, metric):
    metric_x = metric[0]
    shear_xy = metric[1]
    metric_y = metric[2]
    metric_z = metric[3]

    def along_x(values):
        return 0.5 * (values[..., 1:-1, 2:, :] - values[..., 1:-1, :-2, :])

    def along_y(values):
        return 0.5 * (values[..., 2:, 1:-1, :] - values[..., :-2, 1:-1, :])

    def along_z(values):
        center = values[..., 1:-1, 1:-1, :]
        return 0.5 * (jnp.roll(center, -1, -1) - jnp.roll(center, 1, -1))

    def slope_x(values):
        return metric_x * along_x(values) + shear_xy * along_y(values)

    def slope_y(values):
        return metric_y * along_y(values)

    def slope_z(values):
        return metric_z * along_z(values)

    stream = velocity[..., 0, :, :, :]
    normal = velocity[..., 1, :, :, :]
    spanwise = velocity[..., 2, :, :, :]
    around_x = slope_y(spanwise) - slope_z(normal)
    around_y = slope_z(stream) - slope_x(spanwise)
    around_z = slope_x(normal) - slope_y(stream)
    return jnp.stack([around_x, around_y, around_z], axis=-4)


def wrap_columns(values):
    return jnp.concatenate([values[..., -1:, :], values, values[..., :1, :]], axis=-2)


def whitening(correlation):
    identity = jnp.eye(correlation.shape[0], dtype=correlation.dtype)
    frob_scale = jnp.sqrt(jnp.sum(correlation * correlation) + 1e-06)
    approx = correlation / frob_scale
    inverse = identity
    for repeat in range(NSITER):
        factor = 0.5 * (3.0 * identity - jnp.dot(inverse, approx, precision=lax.Precision.HIGHEST))
        approx = jnp.dot(approx, factor, precision=lax.Precision.HIGHEST)
        inverse = jnp.dot(factor, inverse, precision=lax.Precision.HIGHEST)
    return inverse / jnp.sqrt(frob_scale)


def inner_rows(left_rows, right_rows):
    return lax.dot_general(
        left_rows,
        right_rows,
        (((1,), (1,)), ((), ())),
        precision=lax.Precision.HIGHEST,
        preferred_element_type=jnp.float32,
    )


def planes_padded(flow, large_scale):
    joined = jnp.concatenate([flow, large_scale[None]], axis=0)
    return with_halo(joined, (("slab", 2),), 1)


def per_device(flow, large_scale, modulation, metric):
    snap_count = lax.axis_size("snap")
    slab_count = lax.axis_size("slab")
    own_snaps = flow.shape[0]
    block_cols = flow.shape[3] // snap_count
    snap_index = lax.axis_index("snap")
    mod_ext = jnp.concatenate([modulation[:, -1:], modulation, modulation[:, :1]], axis=1)
    padded = planes_padded(flow, large_scale)
    large_ext = wrap_columns(padded[own_snaps].astype(jnp.float32))
    mod_mine = lax.dynamic_slice_in_dim(mod_ext, snap_index * own_snaps, own_snaps, 0)
    velocity = (
        wrap_columns(padded[:own_snaps].astype(jnp.float32))
        + mod_mine[:, None, None, :, None] * large_ext[None]
    )
    local_fields = vorticity(velocity, metric)
    pieces = local_fields.reshape(
        own_snaps, 3, local_fields.shape[2], snap_count, block_cols, local_fields.shape[4]
    )
    fields = lax.all_to_all(pieces, "snap", split_axis=3, concat_axis=0, tiled=True)[:, :, :, 0]
    snapshot_rows = fields.reshape(fields.shape[0], -1)
    gram_local = inner_rows(snapshot_rows, snapshot_rows)
    gram_total = lax.psum(gram_local, ("slab", "snap"))
    correlation = gram_total / (snapshot_rows.shape[1] * slab_count * snap_count)
    weights = whitening(correlation)
    result = jnp.dot(weights, snapshot_rows, precision=lax.Precision.HIGHEST)
    return result.reshape(fields.shape)


def solution(mesh):
    return jax.shard_map(
        per_device,
        mesh=mesh,
        in_specs=(
            P("snap", None, "slab", None, None),
            P(None, "slab", None, None),
            P(),
            P(None, "slab", None, None),
        ),
        out_specs=P(None, None, "slab", "snap", None),
        check_vma=False,
    )
```

profile of v0, /device:TPU:0, one launch (start us, length us, event | category | flops | bytes accessed | tf_op | source)
XLA Modules:
  0.0 152.2 jit_solution(17694933197023606983)
XLA Ops:
  0.0 0.0 copy-start
  0.0 2.8 %fusion.20 = (bf16[17,3,1,64,128]{4,3,2,1,0:T(8,128)(2,1)}, bf16[17,3,1,64,128]{4,3,2,1,0:T(8,128)(2,1)}) fusion(bf16[16,3,2,64,128]{4,3,2,1,0:T(8,128)(2,1)} %param.4, bf16[1,3,2,64,128]{4,3,2,1,0:T(8,128)(2,1)} %bitcast.83), kind=kLoop, calls=%fused_computation.43 | loop fusion | flops 835584 | bytes 3342336 | tf_op jit(solution)/shard_map/concatenate | solution.py:83
  2.9 4.9 %collective-permute-start = (bf16[17,3,1,64,128]{4,3,2,1,0:T(8,128)(2,1)}, bf16[17,3,1,64,128]{4,3,2,1,0:T(8,128)(2,1)S(1)}, u32[]{:S(2)}, u32[]{:S(2)}) collective-permute-start(bf16[17,3,1,64,128]{4,3,2,1,0:T(8,128)(2,1)} %get-tuple-element.20), channel_id=1, source_target_pairs={{0,4},{4,8},{8,12},{12,16},{16,20},{20,24},{24,28},{1,5},{5,9},{9,... | collective-permute-start | bytes 2506760 | tf_op jit(solution)/shard_map/ppermute | solution.py:14
  7.8 1.3 collective-permute-start.1
  9.1 0.0 copy-done.2
  9.1 0.1 fusion.34
  9.2 0.1 fusion.25
  9.2 1.0 multiply_bitcast_fusion.2
  10.2 33.6 %collective-permute-done = bf16[17,3,1,64,128]{4,3,2,1,0:T(8,128)(2,1)S(1)} collective-permute-done((bf16[17,3,1,64,128]{4,3,2,1,0:T(8,128)(2,1)}, bf16[17,3,1,64,128]{4,3,2,1,0:T(8,128)(2,1)S(1)}, u32[]{:S(2)}, u32[]{:S(2)}) %collective-permute-start) | collective-permute-done | bytes 835616 | tf_op jit(solution)/shard_map/ppermute | solution.py:14
  43.8 0.0 collective-permute-done.1
  43.8 0.0 copy-done
  43.8 0.0 copy-done.1
  43.8 0.5 pad_maximum_fusion
  44.3 0.7 slice_convert_fusion
  45.1 0.1 fusion.28
  45.3 1.5 maximum_add_fusion
  46.8 0.5 slice_bitcast_fusion.2
  47.2 0.9 fusion.29
  48.1 0.8 fusion.30
  48.9 0.6 fusion.10
  49.6 1.7 %fusion.18 = (f32[16,2,64,128]{3,2,1,0:T(8,128)S(1)}, f32[16,2,64,128]{3,2,1,0:T(8,128)S(1)}) fusion(f32[16,2,64,1]{3,2,1,0:T(8,128)S(1)} %get-tuple-element.13, f32[16,2,64,127]{3,2,1,0:T(8,128)S(1)} %get-tuple-element.15, f32[16,2,64,127]{3,2,1,0:T(8,128)S(1)} %get-tuple-element.14, f32[16,2,64,1]{3,2,1,0:T(8,128)S(1)} %get-tuple-element.12, ...), kind=kLoop, calls=%fused_computation.40 | loop fusion | flops 4194304 | bytes 10747904 | tf_op jit(solution)/shard_map/sub | solution.py:50
  51.2 0.3 pad_maximum_fusion.1
  51.6 0.5 copy.16
  52.0 40.3 %all_to_all.15 = f32[16,3,2,4,16,128]{5,4,2,1,0,3:T(8,128)} all-to-all(f32[16,3,2,4,16,128]{5,4,2,1,0,3:T(8,128)S(1)} %copy.16), channel_id=1, replica_groups=mesh['slab'=8,'snap'=4] {'snap'}, dimensions={3} | all-to-all | bytes 6291456 | tf_op jit(solution)/shard_map/all_to_all | solution.py:105
  92.3 2.8 %reshape_squeeze.3 = f32[64,12288]{1,0:T(8,128)S(1)} reshape(f32[4,16,3,2,1,16,128]{6,5,3,2,1,0,4:T(8,128)} %bitcast.79) | data formatting | bytes 6291456 | tf_op jit(solution)/shard_map/reshape;squeeze | solution.py:106
  95.1 2.6 %fusion.35 = f32[64,64]{1,0:T(8,128)S(1)} fusion(f32[64,12288]{1,0:T(8,128)S(1)} %reshape_squeeze.3), kind=kOutput, calls=%fused_computation.71 | convolution fusion | flops 603979776 | bytes 3162112 | tf_op jit(solution)/shard_map/dot_general | solution.py:73
  97.7 41.6 %psum.7 = f32[64,64]{1,0:T(8,128)S(1)} all-reduce(f32[64,64]{1,0:T(8,128)S(1)} %fusion.35), channel_id=1, replica_groups=mesh['slab'=8,'snap'=4] {'slab','snap'}, use_global_device_ids=true, to_apply=%region_0.1 | all-reduce | flops 4096 | bytes 32768 | tf_op jit(solution)/shard_map/psum | solution.py:108
  139.3 0.6 multiply_reduce_fusion
  140.6 0.2 fusion.8
  140.8 0.2 fusion.23
  141.0 0.1 fusion.22
  141.1 0.2 fusion.7
  141.3 0.2 fusion.37
  141.5 0.2 fusion.36
  141.6 0.2 fusion.6
  141.8 0.2 fusion.39
  142.0 0.2 fusion.38
  142.2 0.2 fusion.5
  142.3 0.2 fusion.41
  142.5 0.2 fusion.40
  142.7 0.2 fusion.4
  142.8 0.2 fusion.42
  143.0 0.2 fusion.43
  143.2 0.6 copy.19
  143.7 0.2 fusion.3
  143.9 0.2 fusion.2
  144.1 4.6 %fusion = f32[64,3,2,16,128]{4,0,3,2,1:T(8,128)S(1)} fusion(f32[64,64,1,1,1]{1,0,4,3,2:T(8,128)S(1)} %fusion.2, f32[3,2,16,128,64]{3,2,1,0,4:T(8,128)S(1)} %bitcast.78), kind=kOutput, calls=%fused_computation.4 | convolution fusion | flops 603979776 | bytes 6307840 | tf_op jit(solution)/shard_map/dot_general | solution.py:111
  148.7 3.5 %copy.14 = f32[64,3,2,16,128]{4,3,2,1,0:T(8,128)} copy(f32[64,3,2,16,128]{4,0,3,2,1:T(8,128)S(1)} %fusion) | data formatting | bytes 6291456 | tf_op jit(solution)/shard_map/dot_general | solution.py:111
  (5 shorter events, 0.1 us)
Async XLA Ops:
  0.0 43.8 %copy-start = (bf16[16,3,2,64,128]{4,3,2,1,0:T(8,128)(2,1)S(1)}, bf16[16,3,2,64,128]{4,3,2,1,0:T(8,128)(2,1)}, u32[]{:S(2)}) copy-start(bf16[16,3,2,64,128]{4,3,2,1,0:T(8,128)(2,1)} %param.4) | copy-start | bytes 4718596
  0.0 43.8 %copy-start.1 = (bf16[3,2,64,128]{3,2,1,0:T(8,128)(2,1)S(1)}, bf16[3,2,64,128]{3,2,1,0:T(8,128)(2,1)}, u32[]{:S(2)}) copy-start(bf16[3,2,64,128]{3,2,1,0:T(8,128)(2,1)} %param.5) | copy-start | bytes 294916
  0.0 9.1 %copy-start.2 = (f32[64,64]{1,0:T(8,128)S(1)}, f32[64,64]{1,0:T(8,128)}, u32[]{:S(2)}) copy-start(f32[64,64]{1,0:T(8,128)} %param.6) | copy-start | bytes 49156
  2.9 40.9 %collective-permute-start = (bf16[17,3,1,64,128]{4,3,2,1,0:T(8,128)(2,1)}, bf16[17,3,1,64,128]{4,3,2,1,0:T(8,128)(2,1)S(1)}, u32[]{:S(2)}, u32[]{:S(2)}) collective-permute-start(bf16[17,3,1,64,128]{4,3,2,1,0:T(8,128)(2,1)} %get-tuple-element.20), channel_id=1, source_target_pairs={{0,4},{4,8},{8,12},{12,16},{16,20},{20,24},{24,28},{1,5},{5,9},{9,... | collective-permute-start | bytes 2506760 | tf_op jit(solution)/shard_map/ppermute | solution.py:14
  7.8 36.0 %collective-permute-start.1 = (bf16[17,3,1,64,128]{4,3,2,1,0:T(8,128)(2,1)}, bf16[17,3,1,64,128]{4,3,2,1,0:T(8,128)(2,1)S(1)}, u32[]{:S(2)}, u32[]{:S(2)}) collective-permute-start(bf16[17,3,1,64,128]{4,3,2,1,0:T(8,128)(2,1)} %get-tuple-element.21), channel_id=1, source_target_pairs={{4,0},{8,4},{12,8},{16,12},{20,16},{24,20},{28,24},{5,1},{9,5},{13... | collective-permute-start | bytes 2506760 | tf_op jit(solution)/shard_map/ppermute | solution.py:17
where the time goes:
time: 153 us; the launch traced here: 152 us
  blocking collectives  81.8 us (53%)
  waiting for transfers between devices  33.6 us (22%)
  matrix products  9.95 us (7%)
  other arithmetic  9.88 us (6%)
  local copies, waits for them, and re-layouts  9.73 us (6%)
  starting transfers between devices  6.21 us (4%)
    psum x1, blocking collectives, per_device(): gram_total = lax.psum(gram_local, ('slab', 'snap'))  41.6 us
    all_to_all x1, blocking collectives, per_device(): lax.all_to_all(pieces, 'snap', split_axis=3, concat_axis=0, tiled=True)  40.3 us
    ppermute x1, waiting for transfers between devices, with_halo(): lax.ppermute(lax.slice_in_dim(block, block.shape[dim] - width, None, axis...  33.6 us
    ppermute x1, starting transfers between devices, with_halo(): lax.ppermute(lax.slice_in_dim(block, block.shape[dim] - width, None, axis...  4.91 us
    dot_general x1, matrix products, per_device(): result = jnp.dot(weights, snapshot_rows, precision=lax.Precision.HIGHEST)  4.62 us
    dot_general x1, local copies, waits for them, and re-layouts, per_device(): result = jnp.dot(weights, snapshot_rows, precision=lax.Precision.HIGHEST)  3.49 us
  transfers between devices with their start and end apart: 2, of which 1 were waited for; matrix products, arithmetic and copies ran while one was open for 1% of the time, Pallas kernels for 0%

commit v1 on v0

v1 whole, which is shorter than its diff:
```python
import functools

import jax
import jax.numpy as jnp
from jax import lax
from jax.experimental import pallas as pl
from jax.experimental.pallas import tpu as pltpu
from jax.sharding import PartitionSpec as P

NSITER = 6
CORES = 2
VMEM_BYTES = 48 * 1024 * 1024


def pack_kernel(chips, planes, cols, where, flow, large, *refs):
    outs, flat = refs[:-1], refs[-1]
    outs = list(outs)
    snaps, width = flow.shape[0], flow.shape[3]
    extra = outs[0].shape[2] - cols
    own = [outs.pop(0) for _ in range(planes)]
    own_edge = outs.pop(0)
    own_other = outs.pop(0)
    away = [[outs.pop(0) for _ in range(planes)] for _ in range(chips - 1)]
    away_edge = [outs.pop(0) for _ in range(chips - 1)]
    chip, core = where[0], where[1]

    def column(col):
        return flat[pl.ds(col, snaps, stride=width), :].astype(jnp.bfloat16)

    def wrapped(col):
        return lax.rem(col + width, width)

    for plane in range(planes):
        for snap in range(snaps):
            flat[pl.ds(snap * width, width), :] = flow[snap, 0, plane].astype(jnp.float32)
        for step in range(chips):
            base = lax.rem(chip + step, chips) * (CORES * cols)
            for part in range(CORES):
                start = base + part * cols
                target = own[plane] if step == 0 else away[step - 1][plane]
                for col in range(cols):
                    target[0, part, col] = column(start + col)
                if step == 0:
                    rows = large[0, plane, pl.ds(pl.multiple_of(start, 8), cols), :]
                    if cols < extra * snaps:
                        rows = jnp.concatenate([rows] * (extra * snaps // cols), axis=0)
                    for piece in range(extra):
                        target[0, part, cols + piece] = rows[piece * snaps : (piece + 1) * snaps]
                else:
                    edge = away_edge[step - 1]
                    edge[0, part, 2 * plane] = column(wrapped(start - 1))
                    edge[0, part, 2 * plane + 1] = column(wrapped(start + cols))
        mine = chip * (CORES * cols) + core * cols
        own_edge[0, 2 * plane] = column(wrapped(mine - 1))
        own_edge[0, 2 * plane + 1] = column(wrapped(mine + cols))
        other = chip * (CORES * cols) + (1 - core) * cols
        for col in range(cols + 2):
            own_other[0, plane, col] = column(wrapped(other + col - 1))


def pack(flow, large, where, chips, cols):
    snaps, comps, planes, width, depth = flow.shape
    extra = -(-cols // snaps)
    kind = flow.dtype
    shapes = [(comps, CORES, cols + extra, snaps, depth)] * planes
    shapes += [(comps, 2 * planes, snaps, depth), (comps, planes, cols + 2, snaps, depth)]
    shapes += [(comps, CORES, cols, snaps, depth)] * (planes * (chips - 1))
    shapes += [(comps, CORES, 2 * planes, snaps, depth)] * (chips - 1)

    def spec(shape):
        tail = len(shape) - 1
        return pl.BlockSpec((1,) + shape[1:], lambda comp: (comp,) + (0,) * tail)

    outs = pl.pallas_call(
        functools.partial(pack_kernel, chips, planes, cols),
        grid=(comps,),
        in_specs=[
            pl.BlockSpec(memory_space=pltpu.SMEM),
            pl.BlockSpec((snaps, 1, planes, width, depth), lambda comp: (0, comp, 0, 0, 0)),
            pl.BlockSpec((1, planes, width, depth), lambda comp: (comp, 0, 0, 0)),
        ],
        out_specs=[spec(shape) for shape in shapes],
        out_shape=[jax.ShapeDtypeStruct(shape, kind) for shape in shapes],
        scratch_shapes=[pltpu.VMEM((snaps * width, depth), jnp.float32)],
        compiler_params=pltpu.CompilerParams(vmem_limit_bytes=VMEM_BYTES),
        name="pack",
    )(where, flow, large)
    outs = list(outs)
    own = [outs.pop(0) for _ in range(planes)]
    own_edge, own_other = outs.pop(0), outs.pop(0)
    away = [[outs.pop(0) for _ in range(planes)] for _ in range(chips - 1)]
    return own, own_edge, own_other, away, outs


def load_field(refs, where, field, wide, sems, chips, planes, cols, snaps):
    refs = list(refs)
    chip, core = where[0], where[1]
    copies = []

    def copy(source, target):
        copies.append(pltpu.make_async_copy(source, target, sems.at[0]))

    def rows(step, part):
        owner = lax.rem(chip + chips - step, chips) * CORES + part
        return pl.ds(pl.multiple_of(owner * snaps, snaps), snaps)

    own = [refs.pop(0) for _ in range(planes)]
    own_edge, own_other = refs.pop(0), refs.pop(0)
    own_low, own_high, own_low_other, own_high_other = [refs.pop(0) for _ in range(4)]
    mine, theirs = rows(0, core), rows(0, 1 - core)
    middle = pl.ds(1, cols)
    for plane in range(planes):
        copy(own[plane].at[:, core, pl.ds(0, cols)], field.at[:, plane + 1, middle, mine])
        copy(own_edge.at[:, 2 * plane], field.at[:, plane + 1, 0, mine])
        copy(own_edge.at[:, 2 * plane + 1], field.at[:, plane + 1, cols + 1, mine])
        copy(own_other.at[:, plane], field.at[:, plane + 1, :, theirs])
    for target, near, far in ((0, own_low, own_low_other), (planes + 1, own_high, own_high_other)):
        copy(near.at[:, core, pl.ds(0, cols)], field.at[:, target, middle, mine])
        copy(far.at[:, pl.ds(0, cols)], field.at[:, target, middle, theirs])
    extra = wide.shape[2]
    copy(own_low.at[:, core, pl.ds(cols, extra)], wide.at[0])
    copy(own_high.at[:, core, pl.ds(cols, extra)], wide.at[1])
    for step in range(1, chips):
        mine, theirs = rows(step, core), rows(step, 1 - core)
        for plane in range(planes):
            near, far = refs.pop(0), refs.pop(0)
            copy(near.at[:, core], field.at[:, plane + 1, middle, mine])
            copy(far, field.at[:, plane + 1, middle, theirs])
        near, far = refs.pop(0), refs.pop(0)
        for plane in range(planes):
            for side, col in ((0, 0), (1, cols + 1)):
                copy(near.at[:, core, 2 * plane + side], field.at[:, plane + 1, col, mine])
                copy(far.at[:, 2 * plane + side], field.at[:, plane + 1, col, theirs])
        for target in (0, planes + 1):
            near, far = refs.pop(0), refs.pop(0)
            copy(near.at[:, core], field.at[:, target, middle, mine])
            copy(far, field.at[:, target, middle, theirs])
    assert not refs
    for item in copies:
        item.start()
    return copies


def field_kernel(chips, where, metric, large, amplitude, *refs):
    refs, (parts, gram, field, wide, coef, total, sems) = refs[:-7], refs[-7:]
    comps, planes, cols, depth = large.shape[0], metric.shape[1], metric.shape[2], metric.shape[3]
    everyone = field.shape[3]
    snaps = everyone // (chips * CORES)
    for item in load_field(refs, where, field, wide, sems, chips, planes, cols, snaps):
        item.wait()

    def along_z(values):
        return pltpu.roll(values, depth - 1, 1) - pltpu.roll(values, 1, 1)

    def halo(side, comp):
        rows = [wide[side, comp, piece] for piece in range(wide.shape[2])]
        return jnp.concatenate(rows, axis=0).astype(jnp.float32)[:cols]

    for plane in range(planes):
        half_x, half_shear, half_y, half_z = [0.5 * metric[k, plane] for k in range(4)]

        def at(comp, index):
            if index < 0:
                return halo(0, comp)
            if index == planes:
                return halo(1, comp)
            return large[comp, index, 1 : cols + 1]

        step_y = [at(comp, plane + 1) - at(comp, plane - 1) for comp in range(comps)]
        step_z = [along_z(at(comp, plane)) for comp in range(2)]
        after = [large[comp, plane, 2 : cols + 2] for comp in (1, 2)]
        before = [large[comp, plane, 0:cols] for comp in (1, 2)]
        rows = [
            half_x,
            half_shear,
            half_y,
            half_z,
            half_y * step_y[2] - half_z * step_z[1],
            half_z * step_z[0] - half_shear * step_y[2],
            half_shear * step_y[1] - half_y * step_y[0],
            half_x * after[0],
            half_x * before[0],
            half_x * after[1],
            half_x * before[1],
        ]
        for index, value in enumerate(rows):
            coef[plane, index] = value

    total[...] = jnp.zeros_like(total)
    tile = 16
    pairs = cols // 2

    def body(item, carry):
        plane = item // pairs
        first = (item % pairs) * 2
        for sub in range(2):
            col = first + sub
            row = [
                jnp.broadcast_to(coef[plane, index, pl.ds(col, 1), :], (tile, depth))
                for index in range(11)
            ]
            gx, shear, gy, gz, ax, ay, az, v_after, v_before, w_after, w_before = row
            for group in range(everyone // tile):
                span = pl.ds(group * tile, tile)

                def get(comp, plane_at, col_at):
                    return field[comp, plane_at, col_at, span, :].astype(jnp.float32)

                mod_before = amplitude[col, span, :]
                mod_here = amplitude[col + 1, span, :]
                mod_after = amplitude[col + 2, span, :]
                dy_u, dy_v, dy_w = [
                    get(comp, plane + 2, col + 1) - get(comp, plane, col + 1) for comp in range(3)
                ]
                dz_u, dz_v = [along_z(get(comp, plane + 1, col + 1)) for comp in range(2)]
                dx_v, dx_w = [
                    get(comp, plane + 1, col + 2) - get(comp, plane + 1, col) for comp in (1, 2)
                ]
                around_x = gy * dy_w - gz * dz_v + mod_here * ax
                around_y = (
                    gz * dz_u - gx * dx_w - shear * dy_w + mod_here * ay
                    - (mod_after * w_after - mod_before * w_before)
                )
                around_z = (
                    gx * dx_v + shear * dy_v - gy * dy_u + mod_here * az
                    + (mod_after * v_after - mod_before * v_before)
                )
                for comp, value in enumerate((around_x, around_y, around_z)):
                    top = value.astype(jnp.bfloat16)
                    rest = (value - top.astype(jnp.float32)).astype(jnp.bfloat16)
                    parts[comp, plane, col, span, :] = top
                    parts[comp, plane, col, pl.ds(everyone + group * tile, tile), :] = rest
        for comp in range(3):
            both = jnp.concatenate(
                [parts[comp, plane, first], parts[comp, plane, first + 1]], axis=1
            )
            total[...] += lax.dot_general(
                both, both, (((1,), (1,)), ((), ())), preferred_element_type=jnp.float32
            )
        return carry

    lax.fori_loop(0, planes * pairs, body, 0)
    gram[...] = (
        total[:everyone, :everyone]
        + total[everyone:, everyone:]
        + (total[:everyone, everyone:] + total[everyone:, :everyone])
    )


def field_and_gram(where, metric, large, amplitude, arrays, chips, snaps):
    comps = large.shape[0]
    _, planes, cols, depth = metric.shape
    everyone = snaps * chips * CORES
    extra = -(-cols // snaps)
    whole = pl.BlockSpec(memory_space=pltpu.VMEM)
    return pl.pallas_call(
        functools.partial(field_kernel, chips),
        in_specs=[pl.BlockSpec(memory_space=pltpu.SMEM), whole, whole, whole]
        + [pl.BlockSpec(memory_space=pl.ANY)] * len(arrays),
        out_specs=[whole, whole],
        out_shape=[
            jax.ShapeDtypeStruct((comps, planes, cols, 2 * everyone, depth), jnp.bfloat16),
            jax.ShapeDtypeStruct((everyone, everyone), jnp.float32),
        ],
        scratch_shapes=[
            pltpu.VMEM((comps, planes + 2, cols + 2, everyone, depth), jnp.bfloat16),
            pltpu.VMEM((2, comps, extra, snaps, depth), jnp.bfloat16),
            pltpu.VMEM((planes, 11, cols, depth), jnp.float32),
            pltpu.VMEM((2 * everyone, 2 * everyone), jnp.float32),
            pltpu.SemaphoreType.DMA((1,)),
        ],
        compiler_params=pltpu.CompilerParams(vmem_limit_bytes=VMEM_BYTES),
        name="field_and_gram",
    )(where, metric, large, amplitude, *arrays)


def whiten_kernel(count, gram, parts, out, left):
    everyone = gram.shape[0]
    cols = parts.shape[2]

    @pl.when((pl.program_id(0) == 0) & (pl.program_id(1) == 0))
    def _():
        def dot(a, b):
            return jnp.dot(
                a, b, precision=lax.Precision.HIGHEST, preferred_element_type=jnp.float32
            )

        correlation = gram[...] / count
        frob_scale = jnp.sqrt(jnp.sum(correlation * correlation, keepdims=True) + 1e-06)
        approx = correlation / frob_scale
        row = lax.broadcasted_iota(jnp.int32, (everyone, everyone), 0)
        col = lax.broadcasted_iota(jnp.int32, (everyone, everyone), 1)
        diagonal = jnp.where(row == col, 3.0, 0.0)
        factor = 0.5 * (diagonal - approx)
        inverse = factor
        for _ in range(1, NSITER):
            approx = dot(approx, factor)
            factor = 0.5 * (diagonal - dot(inverse, approx))
            inverse = dot(factor, inverse)
        weights = inverse / jnp.sqrt(frob_scale)
        top = weights.astype(jnp.bfloat16)
        rest = (weights - top.astype(jnp.float32)).astype(jnp.bfloat16)
        left[:, :everyone] = top
        left[:, everyone : 2 * everyone] = top
        left[:, 2 * everyone : 3 * everyone] = rest
        left[:, 3 * everyone :] = rest

    depth = out.shape[-1]
    flat = out.reshape(everyone * cols, depth)
    mix = left[...]
    for first in range(0, cols, 2):
        both = jnp.concatenate([parts[0, 0, first], parts[0, 0, first + 1]], axis=1)
        both = jnp.concatenate([both, both], axis=0)
        mixed = jnp.dot(mix, both, preferred_element_type=jnp.float32)
        for sub in range(2):
            flat[pl.ds(first + sub, everyone, stride=cols), :] = mixed[
                :, sub * depth : (sub + 1) * depth
            ]


def whiten(gram, parts, count):
    everyone = gram.shape[0]
    comps, planes, cols, _, depth = parts.shape
    out = pl.pallas_call(
        functools.partial(whiten_kernel, count),
        grid=(comps, planes),
        in_specs=[
            pl.BlockSpec((everyone, everyone), lambda comp, plane: (0, 0)),
            pl.BlockSpec(
                (1, 1, cols, 2 * everyone, depth), lambda comp, plane: (comp, plane, 0, 0, 0)
            ),
        ],
        out_specs=pl.BlockSpec(
            (everyone, 1, 1, cols, depth), lambda comp, plane: (0, comp, plane, 0, 0)
        ),
        out_shape=jax.ShapeDtypeStruct((everyone, comps, planes, cols, depth), jnp.float32),
        scratch_shapes=[pltpu.VMEM((everyone, 4 * everyone), jnp.bfloat16)],
        compiler_params=pltpu.CompilerParams(vmem_limit_bytes=VMEM_BYTES),
        name="whiten",
    )(gram, parts)
    return out


def to_chip(array, step):
    count = lax.axis_size("snap")
    pairs = [(i, (i + step * CORES) % count) for i in range(count)]
    return lax.ppermute(array, "snap", pairs)


def to_core(array):
    return lax.ppermute(array, "snap", [(i, i ^ 1) for i in range(lax.axis_size("snap"))])


def to_slab(array, step):
    count = lax.axis_size("slab")
    pairs = [(i, i + step) for i in range(count) if 0 <= i + step < count]
    return lax.ppermute(array, "slab", pairs)


def all_sum(value):
    for axis in ("snap", "slab"):
        count = lax.axis_size(axis)
        if count & (count - 1):
            value = lax.psum(value, axis)
            continue
        stride = 1
        while stride < count:
            pairs = [(i, i ^ stride) for i in range(count)]
            value = value + lax.ppermute(value, axis, pairs)
            stride *= 2
    return value


def per_device(flow, large_scale, modulation, metric):
    snap_count = lax.axis_size("snap")
    slab_count = lax.axis_size("slab")
    snaps, comps, planes, width, depth = flow.shape
    chips = snap_count // CORES
    cols = width // snap_count
    place = lax.axis_index("snap")
    chip, core = place // CORES, place % CORES
    where = jnp.stack([chip, core]).astype(jnp.int32)

    def half(array, axis):
        return lax.dynamic_index_in_dim(array, 1 - core, axis, keepdims=False)

    own, own_edge, own_other, away, away_edge = pack(flow, large_scale, where, chips, cols)
    own_low = to_slab(own[-1], 1)
    own_high = to_slab(own[0], -1)
    arrays = own + [own_edge, to_core(own_other)]
    arrays += [own_low, own_high, to_core(half(own_low, 1)), to_core(half(own_high, 1))]
    for step in range(1, chips):
        here = [to_chip(item, step) for item in away[step - 1]]
        edge = to_chip(away_edge[step - 1], step)
        low, high = to_slab(here[-1], 1), to_slab(here[0], -1)
        for item in here + [edge, low, high]:
            arrays += [item, to_core(half(item, 1))]

    first = place * cols
    def window(array, axis):
        padded = jnp.concatenate(
            [
                lax.slice_in_dim(array, width - 1, width, axis=axis),
                array,
                lax.slice_in_dim(array, 0, 1, axis=axis),
            ],
            axis=axis,
        )
        return lax.dynamic_slice_in_dim(padded, first, cols + 2, axis)

    large = window(large_scale, 2).astype(jnp.float32)
    amplitude = window(modulation, 1).T[:, :, None]
    amplitude = jnp.broadcast_to(amplitude, amplitude.shape[:2] + (depth,))
    metric_mine = lax.dynamic_slice_in_dim(metric, first, cols, 2)
    parts, gram = field_and_gram(where, metric_mine, large, amplitude, arrays, chips, snaps)
    gram = all_sum(gram)
    return whiten(gram, parts, float(comps * planes * slab_count * width * depth))


def solution(mesh):
    return jax.shard_map(
        per_device,
        mesh=mesh,
        in_specs=(
            P("snap", None, "slab", None, None),
            P(None, "slab", None, None),
            P(),
            P(None, "slab", None, None),
        ),
        out_specs=P(None, None, "slab", "snap", None),
        check_vma=False,
    )
```

time: 153 us -> 87.7 us (0.57)
  blocking collectives: 81.8 us -> 0 us
  starting transfers between devices: 6.21 us -> 25.5 us
  Pallas kernels: 0 us -> 18.9 us
  matrix products: 9.95 us -> 0 us
  other arithmetic: 9.88 us -> 1.71 us
  local copies, waits for them, and re-layouts: 9.73 us -> 6.75 us
    psum x1 -> x0, blocking collectives: 41.6 us -> none  [per_device(): gram_total = lax.psum(gram_local, ('slab', 'snap'))]
    all_to_all x1 -> x0, blocking collectives: 40.3 us -> none  [per_device(): lax.all_to_all(pieces, 'snap', split_axis=3, concat_axis=0, tiled=True)]
    ppermute x2 -> x20, starting transfers between devices: 6.21 us -> 25.5 us  [the longest x4 10.9 us: to_slab(): return lax.ppermute(array, 'slab', pairs)]
    pallas_call x0 -> x3, Pallas kernels: none -> 18.9 us  [the longest x1 8.36 us: field_and_gram(): pl.pallas_call(functools.partial(field_kernel, chips), in_specs=[pl.Block...]
    dot_general x19 -> x0, matrix products: 9.95 us -> none  [the longest x1 4.62 us: per_device(): result = jnp.dot(weights, snapshot_rows, precision=lax.Precision.HIGHEST)]
    unnamed x7 -> x10, local copies, waits for them, and re-layouts: 0.57 us -> 4.22 us
    dot_general x1 -> x0, local copies, waits for them, and re-layouts: 3.49 us -> none  [per_device(): result = jnp.dot(weights, snapshot_rows, precision=lax.Precision.HIGHEST)]
    concatenate x4 -> x0, other arithmetic: 3.44 us -> none  [the longest x1 2.84 us: planes_padded(): joined = jnp.concatenate([flow, large_scale[None]], axis=0)]
  transfers between devices with their start and end apart: 2 -> 20, of which waited for: 1 -> 11; matrix products, arithmetic and copies ran while one was open for 1% -> 5% of each run, Pallas kernels for 0% -> 0%
where the time goes in v1:
time: 87.7 us; the launch traced here: 87.2 us
  waiting for transfers between devices  34.2 us (39%)
  starting transfers between devices  25.5 us (29%)
  Pallas kernels  18.9 us (22%)
  local copies, waits for them, and re-layouts  6.75 us (8%)
  other arithmetic  1.71 us (2%)
    ppermute x4, waiting for transfers between devices, to_slab(): return lax.ppermute(array, 'slab', pairs)  16 us
    ppermute x4, starting transfers between devices, to_slab(): return lax.ppermute(array, 'slab', pairs)  10.9 us
    ppermute x5, waiting for transfers between devices, all_sum(): value = value + lax.ppermute(value, axis, pairs)  10.4 us
    pallas_call x1, Pallas kernels, field_and_gram(): pl.pallas_call(functools.partial(field_kernel, chips), in_specs=[pl.Block...  8.36 us
    ppermute x5, starting transfers between devices, all_sum(): value = value + lax.ppermute(value, axis, pairs)  7.85 us
    ppermute x3, waiting for transfers between devices, to_chip(): return lax.ppermute(array, 'snap', pairs)  7.28 us
    pallas_call x1, Pallas kernels, whiten(): pl.pallas_call(functools.partial(whiten_kernel, count), grid=(comps, plan...  6 us
    ppermute x3, starting transfers between devices, to_chip(): return lax.ppermute(array, 'snap', pairs)  4.97 us
  transfers between devices with their start and end apart: 20, of which 11 were waited for; matrix products, arithmetic and copies ran while one was open for 5% of the time, Pallas kernels for 0%

profile of v1, /device:TPU:0, one launch (start us, length us, event | category | flops | bytes accessed | tf_op | source)
XLA Modules:
  0.0 87.2 jit_solution(16098332915379218412)
XLA Ops:
  0.0 0.1 pad_add_fusion.where
  0.1 1.4 %copy-done.2 = bf16[16,3,2,64,128]{4,3,2,1,0:T(8,128)(2,1)S(1)} copy-done((bf16[16,3,2,64,128]{4,3,2,1,0:T(8,128)(2,1)S(1)}, bf16[16,3,2,64,128]{4,3,2,1,0:T(8,128)(2,1)}, u32[]{:S(2)}) %copy-start.2) | copy-done | bytes 1572888
  1.5 0.9 %copy-done.3 = bf16[3,2,64,128]{3,2,1,0:T(8,128)(2,1)S(1)} copy-done((bf16[3,2,64,128]{3,2,1,0:T(8,128)(2,1)S(1)}, bf16[3,2,64,128]{3,2,1,0:T(8,128)(2,1)}, u32[]{:S(2)}) %copy-start.3) | copy-done | bytes 98328
  2.4 4.6 %pack.1 = (bf16[3,2,17,16,128]{4,3,2,1,0:T(8,128)(2,1)S(1)}, bf16[3,2,17,16,128]{4,3,2,1,0:T(8,128)(2,1)S(1)}, bf16[3,4,16,128]{3,2,1,0:T(8,128)(2,1)S(1)}, bf16...) custom-call(s32[2]{0:T(128)S(1)} %pad_add_fusion.where, ...), custom_call_target="tpu_custom_call" | custom-call | tf_op jit(solution)/shard_map/pack/pallas_call | solution.py:74
  7.0 2.9 %collective-permute-start.9 = (bf16[3,2,4,16,128]{4,3,2,1,0:T(8,128)(2,1)S(1)}, bf16[3,2,4,16,128]{4,3,2,1,0:T(8,128)(2,1)S(1)}, u32[]{:S(2)}, u32[]{:S(2)}) collective-permute-start(bf16[3,2,4,16,128]{4,3,2,1,0:T(8,128)(2,1)S(1)} %get-tuple-element.20), channel_id=1, source_target_pairs={{0,2},{1,3},{2,0},{3,1},{4,6},{5,7},{6,4},{7,5},{8,10},{9,11},{10,... | collective-permute-start | bytes 294920 | tf_op jit(solution)/shard_map/ppermute | solution.py:347
  9.9 0.0 collective-permute-start.5
  9.9 2.0 %collective-permute-start.7 = (bf16[3,2,16,16,128]{4,3,2,1,0:T(8,128)(2,1)}, bf16[3,2,16,16,128]{4,3,2,1,0:T(8,128)(2,1)S(1)}, u32[]{:S(2)}, u32[]{:S(2)}) collective-permute-start(bf16[3,2,16,16,128]{4,3,2,1,0:T(8,128)(2,1)} %get-tuple-element.19), channel_id=1, source_target_pairs={{0,2},{1,3},{2,0},{3,1},{4,6},{5,7},{6,4},{7,5},{8,10},{9,11},{10,... | collective-permute-start | bytes 1179656 | tf_op jit(solution)/shard_map/ppermute | solution.py:347
  11.9 1.3 %collective-permute-start.2 = (bf16[3,2,17,16,128]{4,3,2,1,0:T(8,128)(2,1)S(1)}, bf16[3,2,17,16,128]{4,3,2,1,0:T(8,128)(2,1)S(1)}, u32[]{:S(2)}, u32[]{:S(2)}) collective-permute-start(bf16[3,2,17,16,128]{4,3,2,1,0:T(8,128)(2,1)S(1)} %get-tuple-element.14.refs_0_), channel_id=1, source_target_pairs={{4,0},{8,4},{12,8},{16,12},{20,16},{24,20},{28,24},{5,1},{9,5},{13... | collective-permute-start | bytes 1253384 | tf_op jit(solution)/shard_map/ppermute | solution.py:357
  13.2 4.6 %collective-permute-start.1 = (bf16[3,2,17,16,128]{4,3,2,1,0:T(8,128)(2,1)S(1)}, bf16[3,2,17,16,128]{4,3,2,1,0:T(8,128)(2,1)S(1)}, u32[]{:S(2)}, u32[]{:S(2)}) collective-permute-start(bf16[3,2,17,16,128]{4,3,2,1,0:T(8,128)(2,1)S(1)} %get-tuple-element.15.refs_1_), channel_id=1, source_target_pairs={{0,4},{4,8},{8,12},{12,16},{16,20},{20,24},{24,28},{1,5},{5,9},{9,... | collective-permute-start | bytes 1253384 | tf_op jit(solution)/shard_map/ppermute | solution.py:357
  17.8 1.5 %fusion.5 = (f32[64,1]{1,0:T(8,128)}, f32[64,1]{1,0:T(8,128)}) fusion(f32[64,64]{1,0:T(8,128)} %param.6), kind=kLoop, calls=%fused_computation.19 | loop fusion | bytes 1024 | tf_op jit(solution)/shard_map/slice | solution.py:403
  19.3 0.6 fusion.4
  19.9 0.9 %fusion.3 = f32[18,64]{0,1:T(8,128)S(1)} fusion(s32[]{:T(128)S(6)} %select_n.33, f32[64,1]{1,0:T(8,128)} %get-tuple-element.26, f32[64,64]{1,0:T(8,128)} %param.6, f32[64,1]{1,0:T(8,128)} %get-tuple-element.25), kind=kLoop, calls=%fused_computation.14 | loop fusion | flops 2304 | bytes 21508 | tf_op jit(solution)/shard_map/transpose | solution.py:412
  20.8 0.1 copy.5
  20.9 0.0 collective-permute-done.9.refs_12_
  20.9 0.0 collective-permute-start
  21.0 1.2 %collective-permute-done.5.refs_8_ = bf16[3,2,16,16,128]{4,3,2,1,0:T(8,128)(2,1)S(1)} collective-permute-done((bf16[3,2,16,16,128]{4,3,2,1,0:T(8,128)(2,1)}, bf16[3,2,16,16,128]{4,3,2,1,0:T(8,128)(2,1)S(1)}, u32[]{:S(2)}, u32[]{:S(2)}) %collective-permute-start.5) | collective-permute-done | bytes 393248 | tf_op jit(solution)/shard_map/ppermute | solution.py:347
  22.2 1.3 %collective-permute-start.13 = (bf16[3,2,16,16,128]{4,3,2,1,0:T(8,128)(2,1)S(1)}, bf16[3,2,16,16,128]{4,3,2,1,0:T(8,128)(2,1)S(1)}, u32[]{:S(2)}, u32[]{:S(2)}) collective-permute-start(bf16[3,2,16,16,128]{4,3,2,1,0:T(8,128)(2,1)S(1)} %collective-permute-done.5.refs_8_), channel_id=1, source_target_pairs={{4,0},{8,4},{12,8},{16,12},{20,16},{24,20},{28,24},{5,1},{9,5},{13... | collective-permute-start | bytes 1179656 | tf_op jit(solution)/shard_map/ppermute | solution.py:357
  23.5 6.1 %collective-permute-done.7.refs_10_ = bf16[3,2,16,16,128]{4,3,2,1,0:T(8,128)(2,1)S(1)} collective-permute-done((bf16[3,2,16,16,128]{4,3,2,1,0:T(8,128)(2,1)}, bf16[3,2,16,16,128]{4,3,2,1,0:T(8,128)(2,1)S(1)}, u32[]{:S(2)}, u32[]{:S(2)}) %collective-permute-start.7) | collective-permute-done | bytes 393248 | tf_op jit(solution)/shard_map/ppermute | solution.py:347
  29.6 3.8 %collective-permute-start.11 = (bf16[3,2,16,16,128]{4,3,2,1,0:T(8,128)(2,1)S(1)}, bf16[3,2,16,16,128]{4,3,2,1,0:T(8,128)(2,1)S(1)}, u32[]{:S(2)}, u32[]{:S(2)}) collective-permute-start(bf16[3,2,16,16,128]{4,3,2,1,0:T(8,128)(2,1)S(1)} %collective-permute-done.7.refs_10_), channel_id=1, source_target_pairs={{0,4},{4,8},{8,12},{12,16},{16,20},{20,24},{24,28},{1,5},{5,9},{9,... | collective-permute-start | bytes 1179656 | tf_op jit(solution)/shard_map/ppermute | solution.py:357
  33.4 0.0 collective-permute-done.2.refs_5_
  33.4 0.1 collective-permute-start.10
  33.5 8.3 %collective-permute-done.1.refs_4_ = bf16[3,2,17,16,128]{4,3,2,1,0:T(8,128)(2,1)S(1)} collective-permute-done((bf16[3,2,17,16,128]{4,3,2,1,0:T(8,128)(2,1)S(1)}, bf16[3,2,17,16,128]{4,3,2,1,0:T(8,128)(2,1)S(1)}, u32[]{:S(2)}, u32[]{:S(2)}) %collective-permute-start.1) | collective-permute-done | bytes 417824 | tf_op jit(solution)/shard_map/ppermute | solution.py:357
  41.8 0.0 collective-permute-start.6
  41.8 0.0 collective-permute-done.13.refs_16_
  41.8 0.6 collective-permute-start.8
  42.4 7.7 %collective-permute-done.11.refs_14_ = bf16[3,2,16,16,128]{4,3,2,1,0:T(8,128)(2,1)S(1)} collective-permute-done((bf16[3,2,16,16,128]{4,3,2,1,0:T(8,128)(2,1)S(1)}, bf16[3,2,16,16,128]{4,3,2,1,0:T(8,128)(2,1)S(1)}, u32[]{:S(2)}, u32[]{:S(2)}) %collective-permute-start.11) | collective-permute-done | bytes 393248 | tf_op jit(solution)/shard_map/ppermute | solution.py:357
  50.1 0.0 collective-permute-start.4
  50.1 0.0 collective-permute-done.10.refs_13_
  50.2 0.6 collective-permute-start.3
  50.7 0.1 collective-permute-start.14
  50.8 0.4 collective-permute-start.12
  51.2 0.7 fusion.2.large
  52.0 0.1 collective-permute-done.14.refs_17_
  52.2 0.3 collective-permute-done.12.refs_15_
  52.4 0.2 broadcast_in_dim.2.amplitude
  52.6 8.4 %field_and_gram.1 = (bf16[3,2,16,128,128]{4,3,2,1,0:T(8,128)(2,1)}, f32[64,64]{1,0:T(8,128)S(1)}) custom-call(s32[2]{0:T(128)S(1)} %pad_add_fusion.where, f32[4,2,16,128]{3,2,1,0:T(8,128)S(1)} %constant_dynamic-slice_fusion.metric, f32[3,2,18,128]{3,2,1,0:T(8,128)S(1)} %fusion.2.large, f32[18,64,128]{2,1,0:T(8,128)S(1)} %broadcast_in_dim.2.amplitude, ...), custom_call_target="tpu_custom_call" | custom-call | tf_op jit(solution)/shard_map/field_and_gram/pallas_call | solution.py:256
  61.0 0.4 collective-permute-start.15
  61.4 0.9 %collective-permute-done.15 = f32[64,64]{1,0:T(8,128)S(1)} collective-permute-done((f32[64,64]{1,0:T(8,128)S(1)}, f32[64,64]{1,0:T(8,128)S(1)}, u32[]{:S(2)}, u32[]{:S(2)}) %collective-permute-start.15) | collective-permute-done | bytes 16416 | tf_op jit(solution)/shard_map/ppermute | solution.py:369
  62.3 0.5 collective-permute-start.16
  62.8 3.4 %collective-permute-done.16 = f32[64,64]{1,0:T(8,128)S(1)} collective-permute-done((f32[64,64]{1,0:T(8,128)S(1)}, f32[64,64]{1,0:T(8,128)S(1)}, u32[]{:S(2)}, u32[]{:S(2)}) %collective-permute-start.16) | collective-permute-done | bytes 16416 | tf_op jit(solution)/shard_map/ppermute | solution.py:369
  66.2 2.5 %collective-permute-start.17 = (f32[64,64]{1,0:T(8,128)S(1)}, f32[64,64]{1,0:T(8,128)S(1)}, u32[]{:S(2)}, u32[]{:S(2)}) collective-permute-start(f32[64,64]{1,0:T(8,128)S(1)} %add.45), channel_id=1, source_target_pairs={{0,4},{4,0},{8,12},{12,8},{16,20},{20,16},{24,28},{28,24},{1,5},{5... | collective-permute-start | bytes 49160 | tf_op jit(solution)/shard_map/ppermute | solution.py:369
  68.7 1.9 %collective-permute-done.17 = f32[64,64]{1,0:T(8,128)S(1)} collective-permute-done((f32[64,64]{1,0:T(8,128)S(1)}, f32[64,64]{1,0:T(8,128)S(1)}, u32[]{:S(2)}, u32[]{:S(2)}) %collective-permute-start.17) | collective-permute-done | bytes 16416 | tf_op jit(solution)/shard_map/ppermute | solution.py:369
  70.6 1.6 %collective-permute-start.18 = (f32[64,64]{1,0:T(8,128)S(1)}, f32[64,64]{1,0:T(8,128)S(1)}, u32[]{:S(2)}, u32[]{:S(2)}) collective-permute-start(f32[64,64]{1,0:T(8,128)S(1)} %add.46), channel_id=1, source_target_pairs={{0,8},{4,12},{8,0},{12,4},{16,24},{20,28},{24,16},{28,20},{1,9},{5... | collective-permute-start | bytes 49160 | tf_op jit(solution)/shard_map/ppermute | solution.py:369
  72.2 2.3 %collective-permute-done.18 = f32[64,64]{1,0:T(8,128)S(1)} collective-permute-done((f32[64,64]{1,0:T(8,128)S(1)}, f32[64,64]{1,0:T(8,128)S(1)}, u32[]{:S(2)}, u32[]{:S(2)}) %collective-permute-start.18) | collective-permute-done | bytes 16416 | tf_op jit(solution)/shard_map/ppermute | solution.py:369
  74.5 2.9 %collective-permute-start.19 = (f32[64,64]{1,0:T(8,128)S(1)}, f32[64,64]{1,0:T(8,128)S(1)}, u32[]{:S(2)}, u32[]{:S(2)}) collective-permute-start(f32[64,64]{1,0:T(8,128)S(1)} %add.47), channel_id=1, source_target_pairs={{0,16},{4,20},{8,24},{12,28},{16,0},{20,4},{24,8},{28,12},{1,17},{... | collective-permute-start | bytes 49160 | tf_op jit(solution)/shard_map/ppermute | solution.py:369
  77.4 1.9 %collective-permute-done.19 = f32[64,64]{1,0:T(8,128)S(1)} collective-permute-done((f32[64,64]{1,0:T(8,128)S(1)}, f32[64,64]{1,0:T(8,128)S(1)}, u32[]{:S(2)}, u32[]{:S(2)}) %collective-permute-start.19) | collective-permute-done | bytes 16416 | tf_op jit(solution)/shard_map/ppermute | solution.py:369
  79.3 1.9 %copy-done.1 = bf16[3,2,16,128,128]{4,3,2,1,0:T(8,128)(2,1)S(1)} copy-done((bf16[3,2,16,128,128]{4,3,2,1,0:T(8,128)(2,1)S(1)}, bf16[3,2,16,128,128]{4,3,2,1,0:T(8,128)(2,1)}, u32[]{:S(2)}) %copy-start.1) | copy-done | bytes 3145752
  81.2 6.0 %whiten.1 = f32[64,3,2,16,128]{4,3,2,1,0:T(8,128)} custom-call(f32[64,64]{1,0:T(8,128)S(1)} %add.48.gram, bf16[3,2,16,128,128]{4,3,2,1,0:T(8,128)(2,1)S(1)} %copy-done.1), custom_call_target="tpu_custom_call" | custom-call | tf_op jit(solution)/shard_map/whiten/pallas_call | solution.py:324
  (25 shorter events, 0.2 us)
Async XLA Ops:
  0.0 51.2 %copy-start = (f32[4,2,64,128]{3,2,1,0:T(8,128)S(1)}, f32[4,2,64,128]{3,2,1,0:T(8,128)}, u32[]{:S(2)}) copy-start(f32[4,2,64,128]{3,2,1,0:T(8,128)} %param.7) | copy-start | bytes 786436
  0.1 1.4 %copy-start.2 = (bf16[16,3,2,64,128]{4,3,2,1,0:T(8,128)(2,1)S(1)}, bf16[16,3,2,64,128]{4,3,2,1,0:T(8,128)(2,1)}, u32[]{:S(2)}) copy-start(bf16[16,3,2,64,128]{4,3,2,1,0:T(8,128)(2,1)} %flow.1) | copy-start | bytes 4718596
  1.5 0.9 %copy-start.3 = (bf16[3,2,64,128]{3,2,1,0:T(8,128)(2,1)S(1)}, bf16[3,2,64,128]{3,2,1,0:T(8,128)(2,1)}, u32[]{:S(2)}) copy-start(bf16[3,2,64,128]{3,2,1,0:T(8,128)(2,1)} %large.1) | copy-start | bytes 294916
  2.4 48.8 %copy-start.4 = (bf16[3,2,64,128]{3,2,1,0:T(8,128)(2,1)S(1)}, bf16[3,2,64,128]{3,2,1,0:T(8,128)(2,1)}, u32[]{:S(2)}) copy-start(bf16[3,2,64,128]{3,2,1,0:T(8,128)(2,1)} %large.1) | copy-start | bytes 294916
  7.0 13.9 %collective-permute-start.9 = (bf16[3,2,4,16,128]{4,3,2,1,0:T(8,128)(2,1)S(1)}, bf16[3,2,4,16,128]{4,3,2,1,0:T(8,128)(2,1)S(1)}, u32[]{:S(2)}, u32[]{:S(2)}) collective-permute-start(bf16[3,2,4,16,128]{4,3,2,1,0:T(8,128)(2,1)S(1)} %get-tuple-element.20), channel_id=1, source_target_pairs={{0,2},{1,3},{2,0},{3,1},{4,6},{5,7},{6,4},{7,5},{8,10},{9,11},{10,... | collective-permute-start | bytes 294920 | tf_op jit(solution)/shard_map/ppermute | solution.py:347
  9.9 12.3 %collective-permute-start.5 = (bf16[3,2,16,16,128]{4,3,2,1,0:T(8,128)(2,1)}, bf16[3,2,16,16,128]{4,3,2,1,0:T(8,128)(2,1)S(1)}, u32[]{:S(2)}, u32[]{:S(2)}) collective-permute-start(bf16[3,2,16,16,128]{4,3,2,1,0:T(8,128)(2,1)} %get-tuple-element.18), channel_id=1, source_target_pairs={{0,2},{1,3},{2,0},{3,1},{4,6},{5,7},{6,4},{7,5},{8,10},{9,11},{10,... | collective-permute-start | bytes 1179656 | tf_op jit(solution)/shard_map/ppermute | solution.py:347
  9.9 19.6 %collective-permute-start.7 = (bf16[3,2,16,16,128]{4,3,2,1,0:T(8,128)(2,1)}, bf16[3,2,16,16,128]{4,3,2,1,0:T(8,128)(2,1)S(1)}, u32[]{:S(2)}, u32[]{:S(2)}) collective-permute-start(bf16[3,2,16,16,128]{4,3,2,1,0:T(8,128)(2,1)} %get-tuple-element.19), channel_id=1, source_target_pairs={{0,2},{1,3},{2,0},{3,1},{4,6},{5,7},{6,4},{7,5},{8,10},{9,11},{10,... | collective-permute-start | bytes 1179656 | tf_op jit(solution)/shard_map/ppermute | solution.py:347
  11.9 21.4 %collective-permute-start.2 = (bf16[3,2,17,16,128]{4,3,2,1,0:T(8,128)(2,1)S(1)}, bf16[3,2,17,16,128]{4,3,2,1,0:T(8,128)(2,1)S(1)}, u32[]{:S(2)}, u32[]{:S(2)}) collective-permute-start(bf16[3,2,17,16,128]{4,3,2,1,0:T(8,128)(2,1)S(1)} %get-tuple-element.14.refs_0_), channel_id=1, source_target_pairs={{4,0},{8,4},{12,8},{16,12},{20,16},{24,20},{28,24},{5,1},{9,5},{13... | collective-permute-start | bytes 1253384 | tf_op jit(solution)/shard_map/ppermute | solution.py:357
  13.2 28.5 %collective-permute-start.1 = (bf16[3,2,17,16,128]{4,3,2,1,0:T(8,128)(2,1)S(1)}, bf16[3,2,17,16,128]{4,3,2,1,0:T(8,128)(2,1)S(1)}, u32[]{:S(2)}, u32[]{:S(2)}) collective-permute-start(bf16[3,2,17,16,128]{4,3,2,1,0:T(8,128)(2,1)S(1)} %get-tuple-element.15.refs_1_), channel_id=1, source_target_pairs={{0,4},{4,8},{8,12},{12,16},{16,20},{20,24},{24,28},{1,5},{5,9},{9,... | collective-permute-start | bytes 1253384 | tf_op jit(solution)/shard_map/ppermute | solution.py:357
  20.9 29.8 %collective-permute-start = (bf16[3,2,18,16,128]{4,3,2,1,0:T(8,128)(2,1)S(1)}, bf16[3,2,18,16,128]{4,3,2,1,0:T(8,128)(2,1)S(1)}, u32[]{:S(2)}, u32[]{:S(2)}) collective-permute-start(bf16[3,2,18,16,128]{4,3,2,1,0:T(8,128)(2,1)S(1)} %get-tuple-element.17), channel_id=1, source_target_pairs={{0,1},{1,0},{2,3},{3,2},{4,5},{5,4},{6,7},{7,6},{8,9},{9,8},{10,11... | collective-permute-start | bytes 1327112 | tf_op jit(solution)/shard_map/ppermute | solution.py:351
  22.2 19.6 %collective-permute-start.13 = (bf16[3,2,16,16,128]{4,3,2,1,0:T(8,128)(2,1)S(1)}, bf16[3,2,16,16,128]{4,3,2,1,0:T(8,128)(2,1)S(1)}, u32[]{:S(2)}, u32[]{:S(2)}) collective-permute-start(bf16[3,2,16,16,128]{4,3,2,1,0:T(8,128)(2,1)S(1)} %collective-permute-done.5.refs_8_), channel_id=1, source_target_pairs={{4,0},{8,4},{12,8},{16,12},{20,16},{24,20},{28,24},{5,1},{9,5},{13... | collective-permute-start | bytes 1179656 | tf_op jit(solution)/shard_map/ppermute | solution.py:357
  29.6 20.5 %collective-permute-start.11 = (bf16[3,2,16,16,128]{4,3,2,1,0:T(8,128)(2,1)S(1)}, bf16[3,2,16,16,128]{4,3,2,1,0:T(8,128)(2,1)S(1)}, u32[]{:S(2)}, u32[]{:S(2)}) collective-permute-start(bf16[3,2,16,16,128]{4,3,2,1,0:T(8,128)(2,1)S(1)} %collective-permute-done.7.refs_10_), channel_id=1, source_target_pairs={{0,4},{4,8},{8,12},{12,16},{16,20},{20,24},{24,28},{1,5},{5,9},{9,... | collective-permute-start | bytes 1179656 | tf_op jit(solution)/shard_map/ppermute | solution.py:357
  33.4 16.8 %collective-permute-start.10 = (bf16[3,4,16,128]{3,2,1,0:T(8,128)(2,1)S(1)}, bf16[3,4,16,128]{3,2,1,0:T(8,128)(2,1)S(1)}, u32[]{:S(2)}, u32[]{:S(2)}) collective-permute-start(bf16[3,4,16,128]{3,2,1,0:T(8,128)(2,1)S(1)} %dynamic-slice_bitcast_fusion.6), channel_id=1, source_target_pairs={{0,1},{1,0},{2,3},{3,2},{4,5},{5,4},{6,7},{7,6},{8,9},{9,8},{10,11... | collective-permute-start | bytes 147464 | tf_op jit(solution)/shard_map/ppermute | solution.py:351
  41.8 9.0 %collective-permute-start.6 = (bf16[3,16,16,128]{3,2,1,0:T(8,128)(2,1)S(1)}, bf16[3,16,16,128]{3,2,1,0:T(8,128)(2,1)S(1)}, u32[]{:S(2)}, u32[]{:S(2)}) collective-permute-start(bf16[3,16,16,128]{3,2,1,0:T(8,128)(2,1)S(1)} %dynamic-slice_bitcast_fusion.5), channel_id=1, source_target_pairs={{0,1},{1,0},{2,3},{3,2},{4,5},{5,4},{6,7},{7,6},{8,9},{9,8},{10,11... | collective-permute-start | bytes 589832 | tf_op jit(solution)/shard_map/ppermute | solution.py:351
  41.8 10.2 %collective-permute-start.8 = (bf16[3,16,16,128]{3,2,1,0:T(8,128)(2,1)S(1)}, bf16[3,16,16,128]{3,2,1,0:T(8,128)(2,1)S(1)}, u32[]{:S(2)}, u32[]{:S(2)}) collective-permute-start(bf16[3,16,16,128]{3,2,1,0:T(8,128)(2,1)S(1)} %dynamic-slice_bitcast_fusion.4), channel_id=1, source_target_pairs={{0,1},{1,0},{2,3},{3,2},{4,5},{5,4},{6,7},{7,6},{8,9},{9,8},{10,11... | collective-permute-start | bytes 589832 | tf_op jit(solution)/shard_map/ppermute | solution.py:351
  50.1 1.9 %collective-permute-start.4 = (bf16[3,17,16,128]{3,2,1,0:T(8,128)(2,1)S(1)}, bf16[3,17,16,128]{3,2,1,0:T(8,128)(2,1)S(1)}, u32[]{:S(2)}, u32[]{:S(2)}) collective-permute-start(bf16[3,17,16,128]{3,2,1,0:T(8,128)(2,1)S(1)} %dynamic-slice_bitcast_fusion), channel_id=1, source_target_pairs={{0,1},{1,0},{2,3},{3,2},{4,5},{5,4},{6,7},{7,6},{8,9},{9,8},{10,11... | collective-permute-start | bytes 626696 | tf_op jit(solution)/shard_map/ppermute | solution.py:351
  50.2 1.9 %collective-permute-start.3 = (bf16[3,17,16,128]{3,2,1,0:T(8,128)(2,1)S(1)}, bf16[3,17,16,128]{3,2,1,0:T(8,128)(2,1)S(1)}, u32[]{:S(2)}, u32[]{:S(2)}) collective-permute-start(bf16[3,17,16,128]{3,2,1,0:T(8,128)(2,1)S(1)} %dynamic-slice_bitcast_fusion.1), channel_id=1, source_target_pairs={{0,1},{1,0},{2,3},{3,2},{4,5},{5,4},{6,7},{7,6},{8,9},{9,8},{10,11... | collective-permute-start | bytes 626696 | tf_op jit(solution)/shard_map/ppermute | solution.py:351
  50.7 1.4 %collective-permute-start.14 = (bf16[3,16,16,128]{3,2,1,0:T(8,128)(2,1)S(1)}, bf16[3,16,16,128]{3,2,1,0:T(8,128)(2,1)S(1)}, u32[]{:S(2)}, u32[]{:S(2)}) collective-permute-start(bf16[3,16,16,128]{3,2,1,0:T(8,128)(2,1)S(1)} %dynamic-slice_bitcast_fusion.2), channel_id=1, source_target_pairs={{0,1},{1,0},{2,3},{3,2},{4,5},{5,4},{6,7},{7,6},{8,9},{9,8},{10,11... | collective-permute-start | bytes 589832 | tf_op jit(solution)/shard_map/ppermute | solution.py:351
  50.8 1.6 %collective-permute-start.12 = (bf16[3,16,16,128]{3,2,1,0:T(8,128)(2,1)S(1)}, bf16[3,16,16,128]{3,2,1,0:T(8,128)(2,1)S(1)}, u32[]{:S(2)}, u32[]{:S(2)}) collective-permute-start(bf16[3,16,16,128]{3,2,1,0:T(8,128)(2,1)S(1)} %dynamic-slice_bitcast_fusion.3), channel_id=1, source_target_pairs={{0,1},{1,0},{2,3},{3,2},{4,5},{5,4},{6,7},{7,6},{8,9},{9,8},{10,11... | collective-permute-start | bytes 589832 | tf_op jit(solution)/shard_map/ppermute | solution.py:351
  61.0 1.3 %collective-permute-start.15 = (f32[64,64]{1,0:T(8,128)S(1)}, f32[64,64]{1,0:T(8,128)S(1)}, u32[]{:S(2)}, u32[]{:S(2)}) collective-permute-start(f32[64,64]{1,0:T(8,128)S(1)} %get-tuple-element.21), channel_id=1, source_target_pairs={{0,1},{1,0},{2,3},{3,2},{4,5},{5,4},{6,7},{7,6},{8,9},{9,8},{10,11... | collective-permute-start | bytes 49160 | tf_op jit(solution)/shard_map/ppermute | solution.py:369
  62.3 3.9 %collective-permute-start.16 = (f32[64,64]{1,0:T(8,128)S(1)}, f32[64,64]{1,0:T(8,128)S(1)}, u32[]{:S(2)}, u32[]{:S(2)}) collective-permute-start(f32[64,64]{1,0:T(8,128)S(1)} %add.44), channel_id=1, source_target_pairs={{0,2},{1,3},{2,0},{3,1},{4,6},{5,7},{6,4},{7,5},{8,10},{9,11},{10,... | collective-permute-start | bytes 49160 | tf_op jit(solution)/shard_map/ppermute | solution.py:369
  66.2 4.4 %collective-permute-start.17 = (f32[64,64]{1,0:T(8,128)S(1)}, f32[64,64]{1,0:T(8,128)S(1)}, u32[]{:S(2)}, u32[]{:S(2)}) collective-permute-start(f32[64,64]{1,0:T(8,128)S(1)} %add.45), channel_id=1, source_target_pairs={{0,4},{4,0},{8,12},{12,8},{16,20},{20,16},{24,28},{28,24},{1,5},{5... | collective-permute-start | bytes 49160 | tf_op jit(solution)/shard_map/ppermute | solution.py:369
  70.6 3.9 %collective-permute-start.18 = (f32[64,64]{1,0:T(8,128)S(1)}, f32[64,64]{1,0:T(8,128)S(1)}, u32[]{:S(2)}, u32[]{:S(2)}) collective-permute-start(f32[64,64]{1,0:T(8,128)S(1)} %add.46), channel_id=1, source_target_pairs={{0,8},{4,12},{8,0},{12,4},{16,24},{20,28},{24,16},{28,20},{1,9},{5... | collective-permute-start | bytes 49160 | tf_op jit(solution)/shard_map/ppermute | solution.py:369
  74.5 4.8 %collective-permute-start.19 = (f32[64,64]{1,0:T(8,128)S(1)}, f32[64,64]{1,0:T(8,128)S(1)}, u32[]{:S(2)}, u32[]{:S(2)}) collective-permute-start(f32[64,64]{1,0:T(8,128)S(1)} %add.47), channel_id=1, source_target_pairs={{0,16},{4,20},{8,24},{12,28},{16,0},{20,4},{24,8},{28,12},{1,17},{... | collective-permute-start | bytes 49160 | tf_op jit(solution)/shard_map/ppermute | solution.py:369
  79.3 1.9 %copy-start.1 = (bf16[3,2,16,128,128]{4,3,2,1,0:T(8,128)(2,1)S(1)}, bf16[3,2,16,128,128]{4,3,2,1,0:T(8,128)(2,1)}, u32[]{:S(2)}) copy-start(bf16[3,2,16,128,128]{4,3,2,1,0:T(8,128)(2,1)} %get-tuple-element.22.parts) | copy-start | bytes 9437188

commit v2 on v0

v2 whole, which is shorter than its diff:
```python
import functools

import jax
import jax.numpy as jnp
from jax import lax
from jax.experimental import pallas as pl
from jax.experimental.pallas import tpu as pltpu
from jax.sharding import PartitionSpec as P

NSITER = 6
CORES = 2
VMEM_BYTES = 16 * 1024 * 1024


def whereabouts():
    place = lax.axis_index("snap")
    return lax.div(place, CORES), lax.rem(place, CORES)


def pack_columns(flow, flat, plane):
    snaps, width = flow.shape[0], flow.shape[3]
    pitch = width + 1
    for snap in range(snaps):
        flat[pl.ds(snap * pitch, width), :] = flow[snap, 0, plane].astype(jnp.float32)

    def column(col):
        return flat[pl.ds(col, snaps, stride=pitch), :].astype(jnp.bfloat16)

    return column


def pack_own_kernel(planes, cols, flow, large, *refs):
    own, (flat, near, large_rows, sem) = refs[:-4], refs[-4:]
    snaps = flow.shape[0]
    extra = own[0].shape[2] - cols
    chip, _ = whereabouts()
    comp = pl.program_id(0)
    fetch = pltpu.make_async_copy(large.at[comp], near, sem.at[0])
    fetch.start()
    for plane in range(planes):
        column = pack_columns(flow, flat, plane)
        for part in range(CORES):
            start = chip * (CORES * cols) + part * cols
            for col in range(cols):
                own[plane][0, part, col] = column(start + col)
    fetch.wait()
    large_rows[...] = near[...].astype(jnp.float32)
    for plane in range(planes):
        for part in range(CORES):
            start = chip * (CORES * cols) + part * cols
            rows = large_rows[plane, pl.ds(pl.multiple_of(start, 8), cols), :]
            if cols < extra * snaps:
                rows = jnp.concatenate([rows] * (extra * snaps // cols), axis=0)
            for piece in range(extra):
                tile = rows[piece * snaps : (piece + 1) * snaps]
                own[plane][0, part, cols + piece] = tile.astype(jnp.bfloat16)


def pack_away_kernel(chips, planes, cols, flow, first, *refs):
    outs, flat = list(refs[:-1]), refs[-1]
    width = flow.shape[3]
    own_edge, own_other = outs.pop(0), outs.pop(0)
    mine, other = outs[: chips - 1], outs[chips - 1 :]
    chip, core = whereabouts()
    for plane in range(planes):
        column = pack_columns(flow, flat, plane)

        def window(target, start):
            target[0, plane, 0] = column(lax.rem(start - 1 + width, width))
            for col in range(cols):
                target[0, plane, col + 1] = column(start + col)
            target[0, plane, cols + 1] = column(lax.rem(start + cols, width))

        for step in range(1, chips):
            base = lax.rem(chip + step, chips) * (CORES * cols)
            window(other[step - 1], base + (1 - core) * cols)
            window(mine[step - 1], base + core * cols)
        base = chip * (CORES * cols)
        window(own_other, base + (1 - core) * cols)
        start = base + core * cols
        own_edge[0, 2 * plane] = column(lax.rem(start - 1 + width, width))
        own_edge[0, 2 * plane + 1] = column(lax.rem(start + cols, width))


def pack(flow, large, chips, cols):
    snaps, comps, planes, width, depth = flow.shape
    extra = -(-cols // snaps)

    def spec(shape):
        tail = len(shape) - 1
        return pl.BlockSpec((1,) + shape[1:], lambda comp: (comp,) + (0,) * tail)

    def call(kernel, shapes, second, scratch, name):
        return list(
            pl.pallas_call(
                kernel,
                grid=(comps,),
                in_specs=[
                    pl.BlockSpec((snaps, 1, planes, width, depth), lambda comp: (0, comp, 0, 0, 0)),
                    pl.BlockSpec(memory_space=pl.ANY),
                ],
                out_specs=[spec(shape) for shape in shapes],
                out_shape=[jax.ShapeDtypeStruct(shape, flow.dtype) for shape in shapes],
                scratch_shapes=[pltpu.VMEM((snaps * (width + 1), depth), jnp.float32)] + scratch,
                compiler_params=pltpu.CompilerParams(vmem_limit_bytes=VMEM_BYTES),
                name=name,
            )(flow, second)
        )

    own = call(
        functools.partial(pack_own_kernel, planes, cols),
        [(comps, CORES, cols + extra, snaps, depth)] * planes,
        large,
        [
            pltpu.VMEM((planes, width, depth), large.dtype),
            pltpu.VMEM((planes, width, depth), jnp.float32),
            pltpu.SemaphoreType.DMA((1,)),
        ],
        "pack_own",
    )
    window = (comps, planes, cols + 2, snaps, depth)
    outs = call(
        functools.partial(pack_away_kernel, chips, planes, cols),
        [(comps, 2 * planes, snaps, depth)] + [window] * (2 * chips - 1),
        own[0],
        [],
        "pack_away",
    )
    return own, outs[0], outs[1], outs[2 : chips + 1], outs[chips + 1 :]


def fetch_all(views, slots, sem):
    copies = [pltpu.make_async_copy(view, slot, sem) for view, slot in zip(views, slots)]
    for item in copies:
        item.start()
    for item in copies:
        item.wait()


def coefficients(own, low, high, metric, large, coef, first):
    comps, (_, planes, cols, depth) = 3, metric.shape
    width = large.shape[2]

    def rolled(comp, plane):
        if plane < 0 or plane == planes:
            near = low if plane < 0 else high
            rows = [near[comp, piece] for piece in range(cols, near.shape[1])]
            return jnp.concatenate(rows, axis=0).astype(jnp.float32)[:cols]
        values = large[comp, plane].astype(jnp.float32)
        return pltpu.roll(values, lax.rem(width + 1 - first, width), 0)

    def at(comp, plane):
        values = rolled(comp, plane)
        return values if plane in (-1, planes) else values[1 : cols + 1]

    for plane in range(planes):
        half_x, half_shear, half_y, half_z = [0.5 * metric[k, plane] for k in range(4)]
        step_y = [at(comp, plane + 1) - at(comp, plane - 1) for comp in range(comps)]
        step_z = [along_z(at(comp, plane)) for comp in range(2)]
        after = [rolled(comp, plane)[2 : cols + 2] for comp in (1, 2)]
        before = [rolled(comp, plane)[:cols] for comp in (1, 2)]
        rows = [
            half_x,
            half_shear,
            half_y,
            half_z,
            half_y * step_y[2] - half_z * step_z[1],
            half_z * step_z[0] - half_shear * step_y[2],
            half_shear * step_y[1] - half_y * step_y[0],
            half_x * after[0],
            half_x * before[0],
            half_x * after[1],
            half_x * before[1],
        ]
        for index, value in enumerate(rows):
            coef[plane, index] = value


def along_z(values):
    depth = values.shape[-1]
    return pltpu.roll(values, depth - 1, 1) - pltpu.roll(values, 1, 1)


def curl(get, row, mods, plane, col):
    def value(comp, plane_at, col_at):
        return get(comp, plane_at, col_at).astype(jnp.float32)

    gx, shear, gy, gz, ax, ay, az, v_after, v_before, w_after, w_before = row
    mod_before, mod_here, mod_after = mods
    dy_u, dy_v, dy_w = [value(k, plane + 1, col) - value(k, plane - 1, col) for k in range(3)]
    dz_u, dz_v = [along_z(value(k, plane, col)) for k in range(2)]
    dx_v, dx_w = [value(k, plane, col + 1) - value(k, plane, col - 1) for k in (1, 2)]
    around_x = gy * dy_w - gz * dz_v + mod_here * ax
    around_y = (
        gz * dz_u - gx * dx_w - shear * dy_w + mod_here * ay
        - (mod_after * w_after - mod_before * w_before)
    )
    around_z = (
        gx * dx_v + shear * dy_v - gy * dy_u + mod_here * az
        + (mod_after * v_after - mod_before * v_before)
    )
    return around_x, around_y, around_z


def split(value):
    top = value.astype(jnp.bfloat16)
    return top, (value - top.astype(jnp.float32)).astype(jnp.bfloat16)


def rows_of(chips, step, part, snaps):
    chip, core = whereabouts()
    owner = lax.rem(chip + chips - step, chips) * CORES + (1 - core if part else core)
    return pl.multiple_of(owner * snaps, snaps)


def curls(chips, gets, steps, coef, amplitude, plane, cols, snaps, store):
    depth = amplitude.shape[2]
    for col in range(cols):
        row = [
            jnp.broadcast_to(coef[plane, index, pl.ds(col, 1), :], (snaps, depth))
            for index in range(11)
        ]
        for step in steps:
            for part in range(CORES):
                start = rows_of(chips, step, part, snaps)
                mods = [amplitude[col + k, pl.ds(start, snaps), :] for k in range(3)]
                get = functools.partial(gets, step, part)
                for comp, value in enumerate(curl(get, row, mods, plane, col)):
                    store(comp, col, step, part, start, split(value))


def near_kernel(chips, planes, modulation, metric, large, *refs):
    sources, refs = refs[: planes + 6], refs[planes + 6 :]
    early, coef, amplitude = refs[:3]
    slots, sem = refs[3:-1], refs[-1]
    snaps = early.shape[5]
    cols = early.shape[2]
    chip, core = whereabouts()
    first = pl.multiple_of((chip * CORES + core) * cols, 8)
    views = [modulation, metric.at[:, :, pl.ds(first, cols)], large]
    views += [item.at[:, core] for item in sources[:planes]]
    edge, other, low, high, low_other, high_other = sources[planes:]
    views += [edge, other, low.at[:, core], high.at[:, core], low_other, high_other]
    fetch_all(views, slots, sem.at[0])
    mod, metric, large = slots[:3]
    own = slots[3 : planes + 3]
    edge, other, low, high, low_other, high_other = slots[planes + 3 :]

    wide = jnp.concatenate([mod[...], mod[...]], axis=1)
    wide = pltpu.roll(wide, lax.rem(wide.shape[1] + 1 - first, wide.shape[1]), 1)
    for col in range(cols + 2):
        amplitude[col] = jnp.broadcast_to(wide[:, col : col + 1], amplitude.shape[1:])
    coefficients(own, low, high, metric, large, coef, first)

    def gets(step, part, comp, plane, col):
        if plane < 0:
            return (low_other if part else low)[comp, col]
        if plane == planes:
            return (high_other if part else high)[comp, col]
        if part:
            return other[comp, plane, col + 1]
        if col in (-1, cols):
            return edge[comp, 2 * plane + (col > 0)]
        return own[plane][comp, col]

    for plane in range(planes):

        def store(comp, col, step, part, start, halves):
            for level in range(2):
                early[comp, plane, col, level, part] = halves[level]

        curls(chips, gets, [0], coef, amplitude, plane, cols, snaps, store)


def near_stage(modulation, metric, large, sources, chips, cols):
    everyone, width = modulation.shape
    comps, planes, _, depth = large.shape
    snaps = everyone // (chips * CORES)
    whole = pl.BlockSpec(memory_space=pltpu.VMEM)
    shapes = [item.shape for item in sources]
    halved = [shape[:1] + shape[2:] for shape in shapes]
    shapes = halved[:planes] + shapes[planes : planes + 2] + halved[planes + 2 : planes + 4] + shapes[planes + 4 :]
    slots = [
        pltpu.VMEM(modulation.shape, modulation.dtype),
        pltpu.VMEM((4, planes, cols, depth), metric.dtype),
        pltpu.VMEM(large.shape, large.dtype),
    ]
    slots += [pltpu.VMEM(shape, large.dtype) for shape in shapes]
    return pl.pallas_call(
        functools.partial(near_kernel, chips, planes),
        in_specs=[pl.BlockSpec(memory_space=pl.ANY)] * (3 + len(sources)),
        out_specs=[whole] * 3,
        out_shape=[
            jax.ShapeDtypeStruct((comps, planes, cols, 2, CORES, snaps, depth), jnp.bfloat16),
            jax.ShapeDtypeStruct((planes, 11, cols, depth), jnp.float32),
            jax.ShapeDtypeStruct((cols + 2, everyone, depth), jnp.float32),
        ],
        scratch_shapes=slots + [pltpu.SemaphoreType.DMA((1,))],
        compiler_params=pltpu.CompilerParams(vmem_limit_bytes=VMEM_BYTES),
        cost_estimate=pl.CostEstimate(flops=0, bytes_accessed=8 << 20, transcendentals=0),
        name="near_stage",
    )(modulation, metric, large, *sources)


def far_kernel(chips, keys, first, planes, coef, amplitude, early, before, *refs):
    sources, refs = refs[: len(keys)], refs[len(keys) :]
    parts, gram, total = refs[:3]
    slots, sem = refs[3:-1], refs[-1]
    arrays = dict(zip(keys, slots))
    cols = early.shape[2]
    snaps = early.shape[5]
    everyone = amplitude.shape[1]
    fetch_all(sources, slots, sem.at[0])

    def gets(step, part, comp, plane, col):
        span = slice(part * snaps, (part + 1) * snaps)
        if 0 <= plane < planes and col in (-1, cols):
            return arrays[step, "edge"][comp, 2 * plane + (col > 0), span]
        name = "low" if plane < 0 else "high" if plane == planes else plane
        return arrays[step, name][comp, col, span]

    total[...] = jnp.zeros_like(total)
    for index in range(parts.shape[1]):
        plane = first + index

        def store(comp, col, step, part, start, halves):
            for level in range(2):
                parts[comp, index, col, pl.ds(start + level * everyone, snaps), :] = halves[level]

        for part in range(CORES):
            start = rows_of(chips, 0, part, snaps)
            for comp in range(3):
                for col in range(cols):
                    halves = [early[comp, plane, col, level, part] for level in range(2)]
                    store(comp, col, 0, part, start, halves)
        steps = range(1, chips)
        curls(chips, gets, steps, coef, amplitude, plane, cols, snaps, store)
        for comp in range(3):
            for col in range(0, cols, 2):
                both = jnp.concatenate([parts[comp, index, col], parts[comp, index, col + 1]], 1)
                total[...] += lax.dot_general(
                    both, both, (((1,), (1,)), ((), ())), preferred_element_type=jnp.float32
                )
    gram[...] = before[...] + (
        total[:everyone, :everyone]
        + total[everyone:, everyone:]
        + (total[:everyone, everyone:] + total[everyone:, :everyone])
    )


def far_stage(coef, amplitude, early, before, arrays, chips, first, last):
    comps, planes, cols, _, _, snaps, depth = early.shape
    everyone = snaps * chips * CORES
    wanted = {"edge"} | set(range(max(first - 1, 0), min(last + 1, planes)))
    if first == 0:
        wanted.add("low")
    if last == planes:
        wanted.add("high")
    chosen = {key: item for key, item in arrays.items() if key[1] in wanted}
    whole = pl.BlockSpec(memory_space=pltpu.VMEM)
    return pl.pallas_call(
        functools.partial(far_kernel, chips, tuple(chosen), first, planes),
        in_specs=[whole] * 4 + [pl.BlockSpec(memory_space=pl.ANY)] * len(chosen),
        out_specs=[whole, whole],
        out_shape=[
            jax.ShapeDtypeStruct((comps, last - first, cols, 2 * everyone, depth), jnp.bfloat16),
            jax.ShapeDtypeStruct((everyone, everyone), jnp.float32),
        ],
        scratch_shapes=[pltpu.VMEM((2 * everyone, 2 * everyone), jnp.float32)]
        + [pltpu.VMEM(item.shape, item.dtype) for item in chosen.values()]
        + [pltpu.SemaphoreType.DMA((1,))],
        compiler_params=pltpu.CompilerParams(vmem_limit_bytes=VMEM_BYTES),
        cost_estimate=pl.CostEstimate(flops=0, bytes_accessed=8 << 20, transcendentals=0),
        name="far_stage",
    )(coef, amplitude, early, before, *chosen.values())


def whiten_kernel(count, gram, *refs):
    pieces, (out, slots, sems) = refs[:-3], refs[-3:]
    everyone = gram.shape[0]
    comps, cols, depth = pieces[0].shape[0], pieces[0].shape[2], pieces[0].shape[4]
    pitch = slots.shape[1] // everyone

    def dot(a, b):
        return jnp.dot(a, b, precision=lax.Precision.HIGHEST, preferred_element_type=jnp.float32)

    correlation = gram[...] / count
    frob_scale = jnp.sqrt(jnp.sum(correlation * correlation, keepdims=True) + 1e-06)
    approx = correlation / frob_scale
    row = lax.broadcasted_iota(jnp.int32, (everyone, everyone), 0)
    col = lax.broadcasted_iota(jnp.int32, (everyone, everyone), 1)
    diagonal = jnp.where(row == col, 3.0, 0.0)
    factor = 0.5 * (diagonal - approx)
    inverse = factor
    for _ in range(1, NSITER):
        approx = dot(approx, factor)
        factor = 0.5 * (diagonal - dot(inverse, approx))
        inverse = dot(factor, inverse)
    top, rest = split(inverse / jnp.sqrt(frob_scale))
    left = jnp.concatenate([top, top, rest, rest], axis=1)
    slot, plane, copies = 0, 0, []
    for piece in pieces:
        for index in range(piece.shape[1]):
            for comp in range(comps):
                for first in range(0, cols, 2):
                    both = [piece[comp, index, first], piece[comp, index, first + 1]]
                    both = jnp.concatenate(both, axis=1)
                    mixed = jnp.dot(
                        left,
                        jnp.concatenate([both, both], axis=0),
                        preferred_element_type=jnp.float32,
                    )
                    for sub in range(2):
                        slots[slot, pl.ds(first + sub, everyone, stride=pitch), :] = mixed[
                            :, sub * depth : (sub + 1) * depth
                        ]
                source = slots.reshape(slots.shape[0], everyone, pitch, depth)
                copies.append(
                    pltpu.make_async_copy(
                        source.at[slot, :, pl.ds(0, cols)],
                        out.at[:, comp, plane],
                        sems.at[slot],
                    )
                )
                copies[-1].start()
                slot += 1
            plane += 1
    for item in copies:
        item.wait()


def whiten(gram, pieces, count):
    everyone = gram.shape[0]
    comps, _, cols, _, depth = pieces[0].shape
    planes = sum(piece.shape[1] for piece in pieces)
    pitch = cols + 8 if (cols // 8) % 2 == 0 else cols
    whole = pl.BlockSpec(memory_space=pltpu.VMEM)
    return pl.pallas_call(
        functools.partial(whiten_kernel, count),
        in_specs=[whole] * (1 + len(pieces)),
        out_specs=pl.BlockSpec(memory_space=pl.ANY),
        out_shape=jax.ShapeDtypeStruct((everyone, comps, planes, cols, depth), jnp.float32),
        scratch_shapes=[
            pltpu.VMEM((comps * planes, everyone * pitch, depth), jnp.float32),
            pltpu.SemaphoreType.DMA((comps * planes,)),
        ],
        compiler_params=pltpu.CompilerParams(vmem_limit_bytes=VMEM_BYTES),
        name="whiten",
    )(gram, *pieces)


def to_chip(array, step):
    count = lax.axis_size("snap")
    pairs = [(i, (i + step * CORES) % count) for i in range(count)]
    return lax.ppermute(array, "snap", pairs)


def to_core(array):
    return lax.ppermute(array, "snap", [(i, i ^ 1) for i in range(lax.axis_size("snap"))])


def to_slab(array, step):
    count = lax.axis_size("slab")
    pairs = [(i, i + step) for i in range(count) if 0 <= i + step < count]
    return lax.ppermute(array, "slab", pairs)


def all_sum(value):
    for axis in ("snap", "slab"):
        count = lax.axis_size(axis)
        if count & (count - 1):
            value = lax.psum(value, axis)
            continue
        stride = 1
        while stride < count:
            pairs = [(i, i ^ stride) for i in range(count)]
            value = value + lax.ppermute(value, axis, pairs)
            stride *= 2
    return value


def per_device(flow, large_scale, modulation, metric):
    snap_count = lax.axis_size("snap")
    slab_count = lax.axis_size("slab")
    _, comps, planes, width, depth = flow.shape
    chips = snap_count // CORES
    cols = width // snap_count
    core = lax.rem(lax.axis_index("snap"), CORES)

    def half(array):
        return lax.dynamic_index_in_dim(array, 1 - core, 1, keepdims=False)

    own, own_edge, own_other, mine, other = pack(flow, large_scale, chips, cols)
    low, high = to_slab(own[-1], 1), to_slab(own[0], -1)
    arrays = {}
    for step in range(1, chips):
        both = jnp.concatenate([mine[step - 1], to_core(other[step - 1])], axis=3)
        order = [planes - 1] + list(range(planes - 1))
        for plane in order:
            arrays[step, plane] = to_chip(both[:, plane, 1:-1], step)
        edge = jnp.stack([both[:, :, 0], both[:, :, -1]], axis=2)
        edge = edge.reshape(comps, 2 * planes, *edge.shape[3:])
        edge, _ = lax.optimization_barrier((edge, arrays[step, 0]))
        arrays[step, "edge"] = to_chip(edge, step)
        arrays[step, "low"] = to_slab(arrays[step, planes - 1], 1)
        arrays[step, "high"] = to_slab(arrays[step, 0], -1)
    sources = own + [own_edge, to_core(own_other), low, high]
    sources += [to_core(half(low)), to_core(half(high))]
    early, coef, amplitude = near_stage(modulation, metric, large_scale, sources, chips, cols)
    gram = jnp.zeros(modulation.shape[:1] * 2, jnp.float32)
    pieces = []
    for begin, end in ((0, planes - 1), (planes - 1, planes)):
        if begin < end:
            piece, gram = far_stage(coef, amplitude, early, gram, arrays, chips, begin, end)
            pieces.append(piece)
    return whiten(all_sum(gram), pieces, float(comps * planes * slab_count * width * depth))


def solution(mesh):
    return jax.shard_map(
        per_device,
        mesh=mesh,
        in_specs=(
            P("snap", None, "slab", None, None),
            P(None, "slab", None, None),
            P(),
            P(None, "slab", None, None),
        ),
        out_specs=P(None, None, "slab", "snap", None),
        check_vma=False,
    )
```

time: 153 us -> 79.1 us (0.52)
  blocking collectives: 81.8 us -> 0 us
  starting transfers between devices: 6.21 us -> 25.3 us
  Pallas kernels: 0 us -> 13.5 us
  matrix products: 9.95 us -> 0 us
  other arithmetic: 9.88 us -> 0.04 us
  local copies, waits for them, and re-layouts: 9.73 us -> 4.28 us
  waiting for transfers between devices: 33.6 us -> 35.5 us
    psum x1 -> x0, blocking collectives: 41.6 us -> none  [per_device(): gram_total = lax.psum(gram_local, ('slab', 'snap'))]
    all_to_all x1 -> x0, blocking collectives: 40.3 us -> none  [per_device(): lax.all_to_all(pieces, 'snap', split_axis=3, concat_axis=0, tiled=True)]
    ppermute x2 -> x16, starting transfers between devices: 6.21 us -> 25.3 us  [the longest x4 12.2 us: to_slab(): return lax.ppermute(array, 'slab', pairs)]
    pallas_call x0 -> x6, Pallas kernels: none -> 13.5 us  [the longest x1 4.32 us: whiten(): pl.pallas_call(functools.partial(whiten_kernel, count), in_specs=[whole]...]
    dot_general x19 -> x0, matrix products: 9.95 us -> none  [the longest x1 4.62 us: per_device(): result = jnp.dot(weights, snapshot_rows, precision=lax.Precision.HIGHEST)]
    dot_general x1 -> x0, local copies, waits for them, and re-layouts: 3.49 us -> none  [per_device(): result = jnp.dot(weights, snapshot_rows, precision=lax.Precision.HIGHEST)]
    concatenate x4 -> x0, other arithmetic: 3.44 us -> none  [the longest x1 2.84 us: planes_padded(): joined = jnp.concatenate([flow, large_scale[None]], axis=0)]
    another operation x2 -> x1, local copies, waits for them, and re-layouts: 3.3 us -> 0.01 us  [per_device(): edge = jnp.stack([both[:, :, 0], both[:, :, -1]], axis=2)]
  transfers between devices with their start and end apart: 2 -> 16, of which waited for: 1 -> 9; matrix products, arithmetic and copies ran while one was open for 1% -> 2% of each run, Pallas kernels for 0% -> 6%
where the time goes in v2:
time: 79.1 us; the launch traced here: 78.8 us
  waiting for transfers between devices  35.5 us (45%)
  starting transfers between devices  25.3 us (32%)
  Pallas kernels  13.5 us (17%)
  local copies, waits for them, and re-layouts  4.28 us (5%)
    ppermute x4, waiting for transfers between devices, to_slab(): return lax.ppermute(array, 'slab', pairs)  23.6 us
    ppermute x4, starting transfers between devices, to_slab(): return lax.ppermute(array, 'slab', pairs)  12.2 us
    ppermute x5, waiting for transfers between devices, all_sum(): value = value + lax.ppermute(value, axis, pairs)  9.95 us
    ppermute x5, starting transfers between devices, all_sum(): value = value + lax.ppermute(value, axis, pairs)  8.34 us
    pallas_call x1, Pallas kernels, whiten(): pl.pallas_call(functools.partial(whiten_kernel, count), in_specs=[whole]...  4.32 us
    pallas_call x2, Pallas kernels, far_stage(): pl.pallas_call(functools.partial(far_kernel, chips, tuple(chosen), first,...  3.95 us
    ppermute x3, starting transfers between devices, to_chip(): return lax.ppermute(array, 'snap', pairs)  3.6 us
    pallas_call x1, Pallas kernels, near_stage(): pl.pallas_call(functools.partial(near_kernel, chips, planes), in_specs=[p...  2.77 us
  transfers between devices with their start and end apart: 16, of which 9 were waited for; matrix products, arithmetic and copies ran while one was open for 2% of the time, Pallas kernels for 6%

profile of v2, /device:TPU:0, one launch (start us, length us, event | category | flops | bytes accessed | tf_op | source)
XLA Modules:
  0.0 78.8 jit_solution(13886767543615955786)
XLA Ops:
  0.0 1.4 %copy-done = bf16[16,3,2,64,128]{4,3,2,1,0:T(8,128)(2,1)S(1)} copy-done((bf16[16,3,2,64,128]{4,3,2,1,0:T(8,128)(2,1)S(1)}, bf16[16,3,2,64,128]{4,3,2,1,0:T(8,128)(2,1)}, u32[]{:S(2)}) %copy-start) | copy-done | bytes 1572888
  1.4 0.9 %copy-done.1 = bf16[3,2,64,128]{3,2,1,0:T(8,128)(2,1)S(1)} copy-done((bf16[3,2,64,128]{3,2,1,0:T(8,128)(2,1)S(1)}, bf16[3,2,64,128]{3,2,1,0:T(8,128)(2,1)}, u32[]{:S(2)}) %copy-start.1) | copy-done | bytes 98328
  2.3 0.7 pack_own.1
  3.0 1.8 %pack_away.1 = (bf16[3,4,16,128]{3,2,1,0:T(8,128)(2,1)S(1)}, bf16[3,2,18,16,128]{4,3,2,1,0:T(8,128)(2,1)}, bf16[3,2,18,16,128]{4,3,2,1,0:T(8,128)(2,1)S(1)}, bf16[3,2,18,16,128]{4,3,2,1,0:T(8,128)(2,1)S(1)}) custom-call(bf16[16,3,2,64,128]{4,3,2,1,0:T(8,128)(2,1)S(1)} %copy-done, bf16[3,2,17,16,128]{4,3,2,1,0:T(8,128)(2,1)S(1)} %get-tuple-element.19.first.refs_0_), custom_call_target="tpu_custom_call" | custom-call | tf_op jit(solution)/shard_map/pack_away/pallas_call | solution.py:95
  4.8 0.5 collective-permute-start.5
  5.3 1.3 %collective-permute-start.2 = (bf16[3,2,17,16,128]{4,3,2,1,0:T(8,128)(2,1)S(1)}, bf16[3,2,17,16,128]{4,3,2,1,0:T(8,128)(2,1)S(1)}, u32[]{:S(2)}, u32[]{:S(2)}) collective-permute-start(bf16[3,2,17,16,128]{4,3,2,1,0:T(8,128)(2,1)S(1)} %get-tuple-element.19.first.refs_0_), channel_id=1, source_target_pairs={{4,0},{8,4},{12,8},{16,12},{20,16},{24,20},{28,24},{5,1},{9,5},{13... | collective-permute-start | bytes 1253384 | tf_op jit(solution)/shard_map/ppermute | solution.py:465
  6.6 5.1 %collective-permute-start.1 = (bf16[3,2,17,16,128]{4,3,2,1,0:T(8,128)(2,1)S(1)}, bf16[3,2,17,16,128]{4,3,2,1,0:T(8,128)(2,1)S(1)}, u32[]{:S(2)}, u32[]{:S(2)}) collective-permute-start(bf16[3,2,17,16,128]{4,3,2,1,0:T(8,128)(2,1)S(1)} %get-tuple-element.20.refs_1_), channel_id=1, source_target_pairs={{0,4},{4,8},{8,12},{12,16},{16,20},{20,24},{24,28},{1,5},{5,9},{9,... | collective-permute-start | bytes 1253384 | tf_op jit(solution)/shard_map/ppermute | solution.py:465
  11.8 0.0 collective-permute-done.5
  11.8 0.1 constant_dynamic-update-slice_fusion
  11.8 0.0 copy-start.5
  11.8 0.0 copy-start.2
  11.9 0.0 copy-start.3
  11.9 0.0 copy-start.4
  11.9 1.0 %slice_bitcast_fusion = (bf16[3,16,32,128]{3,2,1,0:T(8,128)(2,1)}, bf16[3,16,32,128]{3,2,1,0:T(8,128)(2,1)}) fusion(bf16[3,2,18,32,128]{4,3,2,0,1:T(8,128)(2,1)S(1)} %constant_dynamic-update-slice_fusion), kind=kLoop, calls=%fused_computation.1 | loop fusion | bytes 1572864 | tf_op jit(solution)/shard_map/squeeze | solution.py:500
  12.8 2.0 %collective-permute-start.7 = (bf16[3,16,32,128]{3,2,1,0:T(8,128)(2,1)}, bf16[3,16,32,128]{3,2,1,0:T(8,128)(2,1)S(1)}, u32[]{:S(2)}, u32[]{:S(2)}) collective-permute-start(bf16[3,16,32,128]{3,2,1,0:T(8,128)(2,1)} %get-tuple-element.35), channel_id=1, source_target_pairs={{0,2},{1,3},{2,0},{3,1},{4,6},{5,7},{6,4},{7,5},{8,10},{9,11},{10,... | collective-permute-start | bytes 1179656 | tf_op jit(solution)/shard_map/ppermute | solution.py:455
  14.8 0.1 collective-permute-start.6
  14.9 0.0 copy-done.5
  14.9 0.0 collective-permute-start
  14.9 14.3 %collective-permute-done.1.refs_4_ = bf16[3,2,17,16,128]{4,3,2,1,0:T(8,128)(2,1)S(1)} collective-permute-done((bf16[3,2,17,16,128]{4,3,2,1,0:T(8,128)(2,1)S(1)}, bf16[3,2,17,16,128]{4,3,2,1,0:T(8,128)(2,1)S(1)}, u32[]{:S(2)}, u32[]{:S(2)}) %collective-permute-start.1) | collective-permute-done | bytes 417824 | tf_op jit(solution)/shard_map/ppermute | solution.py:465
  29.2 0.1 collective-permute-start.3
  29.3 0.0 collective-permute-done.2.refs_5_
  29.3 0.5 collective-permute-start.4
  29.9 0.0 collective-permute-done.7.refs_1_
  29.9 1.3 %collective-permute-start.10 = (bf16[3,16,32,128]{3,2,1,0:T(8,128)(2,1)S(1)}, bf16[3,16,32,128]{3,2,1,0:T(8,128)(2,1)S(1)}, u32[]{:S(2)}, u32[]{:S(2)}) collective-permute-start(bf16[3,16,32,128]{3,2,1,0:T(8,128)(2,1)S(1)} %collective-permute-done.7.refs_1_), channel_id=1, source_target_pairs={{4,0},{8,4},{12,8},{16,12},{20,16},{24,20},{28,24},{5,1},{9,5},{13... | collective-permute-start | bytes 1179656 | tf_op jit(solution)/shard_map/ppermute | solution.py:465
  31.1 1.6 %collective-permute-done.6.refs_0_ = bf16[3,16,32,128]{3,2,1,0:T(8,128)(2,1)S(1)} collective-permute-done((bf16[3,16,32,128]{3,2,1,0:T(8,128)(2,1)}, bf16[3,16,32,128]{3,2,1,0:T(8,128)(2,1)S(1)}, u32[]{:S(2)}, u32[]{:S(2)}) %collective-permute-start.6) | collective-permute-done | bytes 393248 | tf_op jit(solution)/shard_map/ppermute | solution.py:455
  32.7 4.5 %collective-permute-start.9 = (bf16[3,16,32,128]{3,2,1,0:T(8,128)(2,1)S(1)}, bf16[3,16,32,128]{3,2,1,0:T(8,128)(2,1)S(1)}, u32[]{:S(2)}, u32[]{:S(2)}) collective-permute-start(bf16[3,16,32,128]{3,2,1,0:T(8,128)(2,1)S(1)} %collective-permute-done.6.refs_0_), channel_id=1, source_target_pairs={{0,4},{4,8},{8,12},{12,16},{16,20},{20,24},{24,28},{1,5},{5,9},{9,... | collective-permute-start | bytes 1179656 | tf_op jit(solution)/shard_map/ppermute | solution.py:465
  37.2 0.8 %fusion = (bf16[3,2,1,32,128]{4,3,2,0,1:T(8,128)(2,1)S(1)}, bf16[3,2,1,32,128]{4,3,2,0,1:T(8,128)(2,1)S(1)}) fusion(bf16[3,2,18,32,128]{4,3,2,0,1:T(8,128)(2,1)} %copy-done.5), kind=kLoop, calls=%fused_computation.7 | loop fusion | bytes 196608 | tf_op jit(solution)/shard_map/slice | solution.py:501
  38.1 0.0 collective-permute-done.refs_3_
  38.1 1.6 %collective-permute-start.8 = (bf16[3,4,32,128]{3,2,1,0:T(8,128)(2,1)S(1)}, bf16[3,4,32,128]{3,2,1,0:T(8,128)(2,1)S(1)}, u32[]{:S(2)}, u32[]{:S(2)}) collective-permute-start(bf16[3,4,32,128]{3,2,1,0:T(8,128)(2,1)S(1)} %bitcast.9), channel_id=1, source_target_pairs={{0,2},{1,3},{2,0},{3,1},{4,6},{5,7},{6,4},{7,5},{8,10},{9,11},{10,... | collective-permute-start | bytes 294920 | tf_op jit(solution)/shard_map/ppermute | solution.py:455
  39.7 0.0 collective-permute-done.3.refs_6_
  39.7 0.0 collective-permute-done.4.refs_7_
  39.7 2.8 %near_stage.1 = (bf16[3,2,16,2,2,16,128]{6,5,4,3,2,1,0:T(8,128)(2,1)S(1)}, f32[2,11,16,128]{3,2,1,0:T(8,128)S(1)}, f32[18,64,128]{2,1,0:T(8,128)S(1)}) custom-call(f32[64,64]{1,0:T(8,128)S(1)} %copy-done.4, f32[4,2,64,128]{3,2,1,0:T(8,128)S(1)} %copy-done.3, bf16[3,2,64,128]{3,2,1,0:T(8,128)(2,1)S(1)} %copy-done.2, ...), custom_call_target="tpu_custom_call" | custom-call | bytes 8388608 | tf_op jit(solution)/shard_map/near_stage/pallas_call | solution.py:289
  42.5 0.3 collective-permute-done.8.refs_2_
  42.8 9.3 %collective-permute-done.9.refs_3_ = bf16[3,16,32,128]{3,2,1,0:T(8,128)(2,1)S(1)} collective-permute-done((bf16[3,16,32,128]{3,2,1,0:T(8,128)(2,1)S(1)}, bf16[3,16,32,128]{3,2,1,0:T(8,128)(2,1)S(1)}, u32[]{:S(2)}, u32[]{:S(2)}) %collective-permute-start.9) | collective-permute-done | bytes 393248 | tf_op jit(solution)/shard_map/ppermute | solution.py:465
  52.1 2.0 %far_stage.2 = (bf16[3,1,16,128,128]{4,3,2,1,0:T(8,128)(2,1)S(1)}, f32[64,64]{1,0:T(8,128)S(1)}) custom-call(f32[2,11,16,128]{3,2,1,0:T(8,128)S(1)} %get-tuple-element.23.coef, f32[18,64,128]{2,1,0:T(8,128)S(1)} %get-tuple-element.24.amplitude, bf16[3,2,16,2,2,16,128]{6,5,4,3,2,1,0:T(8,128)(2,1)S(1)} %get-tuple-element.25.early, ...), custom_call_target="tpu_custom_call" | custom-call | bytes 8388608 | tf_op jit(solution)/shard_map/far_stage/pallas_call | solution.py:361
  54.1 0.0 collective-permute-done.10.refs_3_
  54.1 2.0 %far_stage.3 = (bf16[3,1,16,128,128]{4,3,2,1,0:T(8,128)(2,1)S(1)}, f32[64,64]{1,0:T(8,128)S(1)}) custom-call(f32[2,11,16,128]{3,2,1,0:T(8,128)S(1)} %get-tuple-element.23.coef, f32[18,64,128]{2,1,0:T(8,128)S(1)} %get-tuple-element.24.amplitude, bf16[3,2,16,2,2,16,128]{6,5,4,3,2,1,0:T(8,128)(2,1)S(1)} %get-tuple-element.25.early, ...), custom_call_target="tpu_custom_call" | custom-call | bytes 8388608 | tf_op jit(solution)/shard_map/far_stage/pallas_call | solution.py:361
  56.1 0.1 collective-permute-start.11
  56.2 1.2 %collective-permute-done.11 = f32[64,64]{1,0:T(8,128)S(1)} collective-permute-done((f32[64,64]{1,0:T(8,128)S(1)}, f32[64,64]{1,0:T(8,128)S(1)}, u32[]{:S(2)}, u32[]{:S(2)}) %collective-permute-start.11) | collective-permute-done | bytes 16416 | tf_op jit(solution)/shard_map/ppermute | solution.py:477
  57.4 1.5 %collective-permute-start.12 = (f32[64,64]{1,0:T(8,128)S(1)}, f32[64,64]{1,0:T(8,128)S(1)}, u32[]{:S(2)}, u32[]{:S(2)}) collective-permute-start(f32[64,64]{1,0:T(8,128)S(1)} %add.22), channel_id=1, source_target_pairs={{0,2},{1,3},{2,0},{3,1},{4,6},{5,7},{6,4},{7,5},{8,10},{9,11},{10,... | collective-permute-start | bytes 49160 | tf_op jit(solution)/shard_map/ppermute | solution.py:477
  58.9 2.4 %collective-permute-done.12 = f32[64,64]{1,0:T(8,128)S(1)} collective-permute-done((f32[64,64]{1,0:T(8,128)S(1)}, f32[64,64]{1,0:T(8,128)S(1)}, u32[]{:S(2)}, u32[]{:S(2)}) %collective-permute-start.12) | collective-permute-done | bytes 16416 | tf_op jit(solution)/shard_map/ppermute | solution.py:477
  61.3 2.5 %collective-permute-start.13 = (f32[64,64]{1,0:T(8,128)S(1)}, f32[64,64]{1,0:T(8,128)S(1)}, u32[]{:S(2)}, u32[]{:S(2)}) collective-permute-start(f32[64,64]{1,0:T(8,128)S(1)} %add.23), channel_id=1, source_target_pairs={{0,4},{4,0},{8,12},{12,8},{16,20},{20,16},{24,28},{28,24},{1,5},{5... | collective-permute-start | bytes 49160 | tf_op jit(solution)/shard_map/ppermute | solution.py:477
  63.8 1.9 %collective-permute-done.13 = f32[64,64]{1,0:T(8,128)S(1)} collective-permute-done((f32[64,64]{1,0:T(8,128)S(1)}, f32[64,64]{1,0:T(8,128)S(1)}, u32[]{:S(2)}, u32[]{:S(2)}) %collective-permute-start.13) | collective-permute-done | bytes 16416 | tf_op jit(solution)/shard_map/ppermute | solution.py:477
  65.7 1.5 %collective-permute-start.14 = (f32[64,64]{1,0:T(8,128)S(1)}, f32[64,64]{1,0:T(8,128)S(1)}, u32[]{:S(2)}, u32[]{:S(2)}) collective-permute-start(f32[64,64]{1,0:T(8,128)S(1)} %add.24), channel_id=1, source_target_pairs={{0,8},{4,12},{8,0},{12,4},{16,24},{20,28},{24,16},{28,20},{1,9},{5... | collective-permute-start | bytes 49160 | tf_op jit(solution)/shard_map/ppermute | solution.py:477
  67.2 2.4 %collective-permute-done.14 = f32[64,64]{1,0:T(8,128)S(1)} collective-permute-done((f32[64,64]{1,0:T(8,128)S(1)}, f32[64,64]{1,0:T(8,128)S(1)}, u32[]{:S(2)}, u32[]{:S(2)}) %collective-permute-start.14) | collective-permute-done | bytes 16416 | tf_op jit(solution)/shard_map/ppermute | solution.py:477
  69.6 2.7 %collective-permute-start.15 = (f32[64,64]{1,0:T(8,128)S(1)}, f32[64,64]{1,0:T(8,128)S(1)}, u32[]{:S(2)}, u32[]{:S(2)}) collective-permute-start(f32[64,64]{1,0:T(8,128)S(1)} %add.25), channel_id=1, source_target_pairs={{0,16},{4,20},{8,24},{12,28},{16,0},{20,4},{24,8},{28,12},{1,17},{... | collective-permute-start | bytes 49160 | tf_op jit(solution)/shard_map/ppermute | solution.py:477
  72.4 2.1 %collective-permute-done.15 = f32[64,64]{1,0:T(8,128)S(1)} collective-permute-done((f32[64,64]{1,0:T(8,128)S(1)}, f32[64,64]{1,0:T(8,128)S(1)}, u32[]{:S(2)}, u32[]{:S(2)}) %collective-permute-start.15) | collective-permute-done | bytes 16416 | tf_op jit(solution)/shard_map/ppermute | solution.py:477
  74.4 4.3 %whiten.1 = f32[64,3,2,16,128]{4,3,2,1,0:T(8,128)} custom-call(f32[64,64]{1,0:T(8,128)S(1)} %add.26.gram, bf16[3,1,16,128,128]{4,3,2,1,0:T(8,128)(2,1)S(1)} %get-tuple-element.31.refs_0_, bf16[3,1,16,128,128]{4,3,2,1,0:T(8,128)(2,1)S(1)} %get-tuple-element.32.refs_1_), custom_call_target="tpu_custom_call" | custom-call | tf_op jit(solution)/shard_map/whiten/pallas_call | solution.py:438
  (17 shorter events, 0.1 us)
Async XLA Ops:
  0.0 1.4 %copy-start = (bf16[16,3,2,64,128]{4,3,2,1,0:T(8,128)(2,1)S(1)}, bf16[16,3,2,64,128]{4,3,2,1,0:T(8,128)(2,1)}, u32[]{:S(2)}) copy-start(bf16[16,3,2,64,128]{4,3,2,1,0:T(8,128)(2,1)} %flow.3) | copy-start | bytes 4718596
  1.4 0.9 %copy-start.1 = (bf16[3,2,64,128]{3,2,1,0:T(8,128)(2,1)S(1)}, bf16[3,2,64,128]{3,2,1,0:T(8,128)(2,1)}, u32[]{:S(2)}) copy-start(bf16[3,2,64,128]{3,2,1,0:T(8,128)(2,1)} %large.3) | copy-start | bytes 294916
  4.8 7.0 %collective-permute-start.5 = (bf16[3,2,18,16,128]{4,3,2,0,1:T(8,128)(2,1)S(1)}, bf16[3,2,18,16,128]{4,3,2,0,1:T(8,128)(2,1)S(1)}, u32[]{:S(2)}, u32[]{:S(2)}) collective-permute-start(bf16[3,2,18,16,128]{4,3,2,0,1:T(8,128)(2,1)S(1)} %copy.7), channel_id=1, source_target_pairs={{0,1},{1,0},{2,3},{3,2},{4,5},{5,4},{6,7},{7,6},{8,9},{9,8},{10,11... | collective-permute-start | bytes 1327112 | tf_op jit(solution)/shard_map/ppermute | solution.py:459
  5.3 24.0 %collective-permute-start.2 = (bf16[3,2,17,16,128]{4,3,2,1,0:T(8,128)(2,1)S(1)}, bf16[3,2,17,16,128]{4,3,2,1,0:T(8,128)(2,1)S(1)}, u32[]{:S(2)}, u32[]{:S(2)}) collective-permute-start(bf16[3,2,17,16,128]{4,3,2,1,0:T(8,128)(2,1)S(1)} %get-tuple-element.19.first.refs_0_), channel_id=1, source_target_pairs={{4,0},{8,4},{12,8},{16,12},{20,16},{24,20},{28,24},{5,1},{9,5},{13... | collective-permute-start | bytes 1253384 | tf_op jit(solution)/shard_map/ppermute | solution.py:465
  6.6 22.6 %collective-permute-start.1 = (bf16[3,2,17,16,128]{4,3,2,1,0:T(8,128)(2,1)S(1)}, bf16[3,2,17,16,128]{4,3,2,1,0:T(8,128)(2,1)S(1)}, u32[]{:S(2)}, u32[]{:S(2)}) collective-permute-start(bf16[3,2,17,16,128]{4,3,2,1,0:T(8,128)(2,1)S(1)} %get-tuple-element.20.refs_1_), channel_id=1, source_target_pairs={{0,4},{4,8},{8,12},{12,16},{16,20},{20,24},{24,28},{1,5},{5,9},{9,... | collective-permute-start | bytes 1253384 | tf_op jit(solution)/shard_map/ppermute | solution.py:465
  11.8 3.0 %copy-start.5 = (bf16[3,2,18,32,128]{4,3,2,0,1:T(8,128)(2,1)}, bf16[3,2,18,32,128]{4,3,2,0,1:T(8,128)(2,1)S(1)}, u32[]{:S(2)}) copy-start(bf16[3,2,18,32,128]{4,3,2,0,1:T(8,128)(2,1)S(1)} %constant_dynamic-update-slice_fusion) | copy-start | bytes 2654212
  11.8 27.8 %copy-start.2 = (bf16[3,2,64,128]{3,2,1,0:T(8,128)(2,1)S(1)}, bf16[3,2,64,128]{3,2,1,0:T(8,128)(2,1)}, u32[]{:S(2)}) copy-start(bf16[3,2,64,128]{3,2,1,0:T(8,128)(2,1)} %large.3) | copy-start | bytes 294916
  11.9 27.8 %copy-start.3 = (f32[4,2,64,128]{3,2,1,0:T(8,128)S(1)}, f32[4,2,64,128]{3,2,1,0:T(8,128)}, u32[]{:S(2)}) copy-start(f32[4,2,64,128]{3,2,1,0:T(8,128)} %metric.1) | copy-start | bytes 786436
  11.9 27.8 %copy-start.4 = (f32[64,64]{1,0:T(8,128)S(1)}, f32[64,64]{1,0:T(8,128)}, u32[]{:S(2)}) copy-start(f32[64,64]{1,0:T(8,128)} %modulation.1) | copy-start | bytes 49156
  12.8 17.0 %collective-permute-start.7 = (bf16[3,16,32,128]{3,2,1,0:T(8,128)(2,1)}, bf16[3,16,32,128]{3,2,1,0:T(8,128)(2,1)S(1)}, u32[]{:S(2)}, u32[]{:S(2)}) collective-permute-start(bf16[3,16,32,128]{3,2,1,0:T(8,128)(2,1)} %get-tuple-element.35), channel_id=1, source_target_pairs={{0,2},{1,3},{2,0},{3,1},{4,6},{5,7},{6,4},{7,5},{8,10},{9,11},{10,... | collective-permute-start | bytes 1179656 | tf_op jit(solution)/shard_map/ppermute | solution.py:455
  14.8 17.9 %collective-permute-start.6 = (bf16[3,16,32,128]{3,2,1,0:T(8,128)(2,1)}, bf16[3,16,32,128]{3,2,1,0:T(8,128)(2,1)S(1)}, u32[]{:S(2)}, u32[]{:S(2)}) collective-permute-start(bf16[3,16,32,128]{3,2,1,0:T(8,128)(2,1)} %get-tuple-element.36), channel_id=1, source_target_pairs={{0,2},{1,3},{2,0},{3,1},{4,6},{5,7},{6,4},{7,5},{8,10},{9,11},{10,... | collective-permute-start | bytes 1179656 | tf_op jit(solution)/shard_map/ppermute | solution.py:455
  14.9 23.2 %collective-permute-start = (bf16[3,2,18,16,128]{4,3,2,1,0:T(8,128)(2,1)}, bf16[3,2,18,16,128]{4,3,2,1,0:T(8,128)(2,1)S(1)}, u32[]{:S(2)}, u32[]{:S(2)}) collective-permute-start(bf16[3,2,18,16,128]{4,3,2,1,0:T(8,128)(2,1)} %get-tuple-element.22), channel_id=1, source_target_pairs={{0,1},{1,0},{2,3},{3,2},{4,5},{5,4},{6,7},{7,6},{8,9},{9,8},{10,11... | collective-permute-start | bytes 1327112 | tf_op jit(solution)/shard_map/ppermute | solution.py:459
  29.2 10.5 %collective-permute-start.3 = (bf16[3,17,16,128]{3,2,1,0:T(8,128)(2,1)S(1)}, bf16[3,17,16,128]{3,2,1,0:T(8,128)(2,1)S(1)}, u32[]{:S(2)}, u32[]{:S(2)}) collective-permute-start(bf16[3,17,16,128]{3,2,1,0:T(8,128)(2,1)S(1)} %dynamic-slice_bitcast_fusion.1), channel_id=1, source_target_pairs={{0,1},{1,0},{2,3},{3,2},{4,5},{5,4},{6,7},{7,6},{8,9},{9,8},{10,11... | collective-permute-start | bytes 626696 | tf_op jit(solution)/shard_map/ppermute | solution.py:459
  29.3 10.4 %collective-permute-start.4 = (bf16[3,17,16,128]{3,2,1,0:T(8,128)(2,1)S(1)}, bf16[3,17,16,128]{3,2,1,0:T(8,128)(2,1)S(1)}, u32[]{:S(2)}, u32[]{:S(2)}) collective-permute-start(bf16[3,17,16,128]{3,2,1,0:T(8,128)(2,1)S(1)} %dynamic-slice_bitcast_fusion), channel_id=1, source_target_pairs={{0,1},{1,0},{2,3},{3,2},{4,5},{5,4},{6,7},{7,6},{8,9},{9,8},{10,11... | collective-permute-start | bytes 626696 | tf_op jit(solution)/shard_map/ppermute | solution.py:459
  29.9 24.3 %collective-permute-start.10 = (bf16[3,16,32,128]{3,2,1,0:T(8,128)(2,1)S(1)}, bf16[3,16,32,128]{3,2,1,0:T(8,128)(2,1)S(1)}, u32[]{:S(2)}, u32[]{:S(2)}) collective-permute-start(bf16[3,16,32,128]{3,2,1,0:T(8,128)(2,1)S(1)} %collective-permute-done.7.refs_1_), channel_id=1, source_target_pairs={{4,0},{8,4},{12,8},{16,12},{20,16},{24,20},{28,24},{5,1},{9,5},{13... | collective-permute-start | bytes 1179656 | tf_op jit(solution)/shard_map/ppermute | solution.py:465
  32.7 19.4 %collective-permute-start.9 = (bf16[3,16,32,128]{3,2,1,0:T(8,128)(2,1)S(1)}, bf16[3,16,32,128]{3,2,1,0:T(8,128)(2,1)S(1)}, u32[]{:S(2)}, u32[]{:S(2)}) collective-permute-start(bf16[3,16,32,128]{3,2,1,0:T(8,128)(2,1)S(1)} %collective-permute-done.6.refs_0_), channel_id=1, source_target_pairs={{0,4},{4,8},{8,12},{12,16},{16,20},{20,24},{24,28},{1,5},{5,9},{9,... | collective-permute-start | bytes 1179656 | tf_op jit(solution)/shard_map/ppermute | solution.py:465
  38.1 4.7 %collective-permute-start.8 = (bf16[3,4,32,128]{3,2,1,0:T(8,128)(2,1)S(1)}, bf16[3,4,32,128]{3,2,1,0:T(8,128)(2,1)S(1)}, u32[]{:S(2)}, u32[]{:S(2)}) collective-permute-start(bf16[3,4,32,128]{3,2,1,0:T(8,128)(2,1)S(1)} %bitcast.9), channel_id=1, source_target_pairs={{0,2},{1,3},{2,0},{3,1},{4,6},{5,7},{6,4},{7,5},{8,10},{9,11},{10,... | collective-permute-start | bytes 294920 | tf_op jit(solution)/shard_map/ppermute | solution.py:455
  56.1 1.3 %collective-permute-start.11 = (f32[64,64]{1,0:T(8,128)S(1)}, f32[64,64]{1,0:T(8,128)S(1)}, u32[]{:S(2)}, u32[]{:S(2)}) collective-permute-start(f32[64,64]{1,0:T(8,128)S(1)} %get-tuple-element.30), channel_id=1, source_target_pairs={{0,1},{1,0},{2,3},{3,2},{4,5},{5,4},{6,7},{7,6},{8,9},{9,8},{10,11... | collective-permute-start | bytes 49160 | tf_op jit(solution)/shard_map/ppermute | solution.py:477
  57.4 3.9 %collective-permute-start.12 = (f32[64,64]{1,0:T(8,128)S(1)}, f32[64,64]{1,0:T(8,128)S(1)}, u32[]{:S(2)}, u32[]{:S(2)}) collective-permute-start(f32[64,64]{1,0:T(8,128)S(1)} %add.22), channel_id=1, source_target_pairs={{0,2},{1,3},{2,0},{3,1},{4,6},{5,7},{6,4},{7,5},{8,10},{9,11},{10,... | collective-permute-start | bytes 49160 | tf_op jit(solution)/shard_map/ppermute | solution.py:477
  61.3 4.4 %collective-permute-start.13 = (f32[64,64]{1,0:T(8,128)S(1)}, f32[64,64]{1,0:T(8,128)S(1)}, u32[]{:S(2)}, u32[]{:S(2)}) collective-permute-start(f32[64,64]{1,0:T(8,128)S(1)} %add.23), channel_id=1, source_target_pairs={{0,4},{4,0},{8,12},{12,8},{16,20},{20,16},{24,28},{28,24},{1,5},{5... | collective-permute-start | bytes 49160 | tf_op jit(solution)/shard_map/ppermute | solution.py:477
  65.7 3.9 %collective-permute-start.14 = (f32[64,64]{1,0:T(8,128)S(1)}, f32[64,64]{1,0:T(8,128)S(1)}, u32[]{:S(2)}, u32[]{:S(2)}) collective-permute-start(f32[64,64]{1,0:T(8,128)S(1)} %add.24), channel_id=1, source_target_pairs={{0,8},{4,12},{8,0},{12,4},{16,24},{20,28},{24,16},{28,20},{1,9},{5... | collective-permute-start | bytes 49160 | tf_op jit(solution)/shard_map/ppermute | solution.py:477
  69.6 4.8 %collective-permute-start.15 = (f32[64,64]{1,0:T(8,128)S(1)}, f32[64,64]{1,0:T(8,128)S(1)}, u32[]{:S(2)}, u32[]{:S(2)}) collective-permute-start(f32[64,64]{1,0:T(8,128)S(1)} %add.25), channel_id=1, source_target_pairs={{0,16},{4,20},{8,24},{12,28},{16,0},{20,4},{24,8},{28,12},{1,17},{... | collective-permute-start | bytes 49160 | tf_op jit(solution)/shard_map/ppermute | solution.py:477

commit v3 on v2

--- a/solution.py
+++ b/solution.py
@@ -15,6 +15,20 @@
 def whereabouts():
     place = lax.axis_index("snap")
     return lax.div(place, CORES), lax.rem(place, CORES)
+
+
+def plane_at(slot, planes):
+    upper = lax.rem(lax.axis_index("slab"), 2)
+    if slot == 0:
+        return (1 - upper) * (planes - 1)
+    if slot == 1:
+        return upper * (planes - 1)
+    return slot - 1
+
+
+def halo_at(slot, planes):
+    upper = lax.rem(lax.axis_index("slab"), 2)
+    return (1 - upper if slot == 0 else upper) * (planes + 1)
 
 
 def pack_columns(flow, flat, plane):
@@ -37,49 +51,44 @@
     comp = pl.program_id(0)
     fetch = pltpu.make_async_copy(large.at[comp], near, sem.at[0])
     fetch.start()
-    for plane in range(planes):
-        column = pack_columns(flow, flat, plane)
+    for slot in range(planes):
+        column = pack_columns(flow, flat, plane_at(slot, planes))
         for part in range(CORES):
             start = chip * (CORES * cols) + part * cols
             for col in range(cols):
-                own[plane][0, part, col] = column(start + col)
+                own[slot][0, part, col] = column(start + col)
     fetch.wait()
     large_rows[...] = near[...].astype(jnp.float32)
-    for plane in range(planes):
+    for slot in range(planes):
         for part in range(CORES):
             start = chip * (CORES * cols) + part * cols
-            rows = large_rows[plane, pl.ds(pl.multiple_of(start, 8), cols), :]
+            rows = large_rows[plane_at(slot, planes), pl.ds(pl.multiple_of(start, 8), cols), :]
             if cols < extra * snaps:
                 rows = jnp.concatenate([rows] * (extra * snaps // cols), axis=0)
             for piece in range(extra):
                 tile = rows[piece * snaps : (piece + 1) * snaps]
-                own[plane][0, part, cols + piece] = tile.astype(jnp.bfloat16)
-
-
-def pack_away_kernel(chips, planes, cols, flow, first, *refs):
-    outs, flat = list(refs[:-1]), refs[-1]
+                own[slot][0, part, cols + piece] = tile.astype(jnp.bfloat16)
+
+
+def pack_windows_kernel(chips, planes, cols, mine, flow, first, *refs):
+    outs, flat = refs[:-1], refs[-1]
     width = flow.shape[3]
-    own_edge, own_other = outs.pop(0), outs.pop(0)
-    mine, other = outs[: chips - 1], outs[chips - 1 :]
     chip, core = whereabouts()
-    for plane in range(planes):
-        column = pack_columns(flow, flat, plane)
-
-        def window(target, start):
-            target[0, plane, 0] = column(lax.rem(start - 1 + width, width))
+    part = core if mine else 1 - core
+    for slot in range(planes):
+        column = pack_columns(flow, flat, plane_at(slot, planes))
+        for target, step in zip(outs, [*range(1, chips), 0]):
+            start = lax.rem(chip + step, chips) * (CORES * cols) + part * cols
+            left = column(lax.rem(start - 1 + width, width))
+            right = column(lax.rem(start + cols, width))
+            if mine and step == 0:
+                target[0, 2 * slot] = left
+                target[0, 2 * slot + 1] = right
+                continue
+            target[0, slot, 0] = left
             for col in range(cols):
-                target[0, plane, col + 1] = column(start + col)
-            target[0, plane, cols + 1] = column(lax.rem(start + cols, width))
-
-        for step in range(1, chips):
-            base = lax.rem(chip + step, chips) * (CORES * cols)
-            window(other[step - 1], base + (1 - core) * cols)
-            window(mine[step - 1], base + core * cols)
-        base = chip * (CORES * cols)
-        window(own_other, base + (1 - core) * cols)
-        start = base + core * cols
-        own_edge[0, 2 * plane] = column(lax.rem(start - 1 + width, width))
-        own_edge[0, 2 * plane + 1] = column(lax.rem(start + cols, width))
+                target[0, slot, col + 1] = column(start + col)
+            target[0, slot, cols + 1] = right
 
 
 def pack(flow, large, chips, cols):
@@ -119,39 +128,38 @@
         "pack_own",
     )
     window = (comps, planes, cols + 2, snaps, depth)
-    outs = call(
-        functools.partial(pack_away_kernel, chips, planes, cols),
-        [(comps, 2 * planes, snaps, depth)] + [window] * (2 * chips - 1),
+    edge = (comps, 2 * planes, snaps, depth)
+    other = call(
+        functools.partial(pack_windows_kernel, chips, planes, cols, False),
+        [window] * chips,
         own[0],
         [],
-        "pack_away",
-    )
-    return own, outs[0], outs[1], outs[2 : chips + 1], outs[chips + 1 :]
-
-
-def fetch_all(views, slots, sem):
-    copies = [pltpu.make_async_copy(view, slot, sem) for view, slot in zip(views, slots)]
-    for item in copies:
-        item.start()
-    for item in copies:
-        item.wait()
-
-
-def coefficients(own, low, high, metric, large, coef, first):
+        "pack_other",
+    )
+    mine = call(
+        functools.partial(pack_windows_kernel, chips, planes, cols, True),
+        [window] * (chips - 1) + [edge],
+        other[0],
+        [],
+        "pack_mine",
+    )
+    return own, mine, other
+
+
+def coefficients(wide, metric, large, coef, first):
     comps, (_, planes, cols, depth) = 3, metric.shape
     width = large.shape[2]
 
     def rolled(comp, plane):
-        if plane < 0 or plane == planes:
-            near = low if plane < 0 else high
-            rows = [near[comp, piece] for piece in range(cols, near.shape[1])]
-            return jnp.concatenate(rows, axis=0).astype(jnp.float32)[:cols]
         values = large[comp, plane].astype(jnp.float32)
         return pltpu.roll(values, lax.rem(width + 1 - first, width), 0)
 
     def at(comp, plane):
-        values = rolled(comp, plane)
-        return values if plane in (-1, planes) else values[1 : cols + 1]
+        if 0 <= plane < planes:
+            return rolled(comp, plane)[1 : cols + 1]
+        side = 0 if plane < 0 else 1
+        rows = [wide[side, comp, piece] for piece in range(wide.shape[2])]
+        return jnp.concatenate(rows, axis=0).astype(jnp.float32)[:cols]
 
     for plane in range(planes):
         half_x, half_shear, half_y, half_z = [0.5 * metric[k, plane] for k in range(4)]
@@ -213,7 +221,7 @@
     return pl.multiple_of(owner * snaps, snaps)
 
 
-def curls(chips, gets, steps, coef, amplitude, plane, cols, snaps, store):
+def curls(chips, field, steps, coef, amplitude, plane, cols, snaps, store):
     depth = amplitude.shape[2]
     for col in range(cols):
         row = [
@@ -224,68 +232,73 @@
             for part in range(CORES):
                 start = rows_of(chips, step, part, snaps)
                 mods = [amplitude[col + k, pl.ds(start, snaps), :] for k in range(3)]
-                get = functools.partial(gets, step, part)
-                for comp, value in enumerate(curl(get, row, mods, plane, col)):
+                get = functools.partial(field, step, part)
+                for comp, value in enumerate(curl(get, row, mods, plane + 1, col + 1)):
                     store(comp, col, step, part, start, split(value))
 
 
 def near_kernel(chips, planes, modulation, metric, large, *refs):
-    sources, refs = refs[: planes + 6], refs[planes + 6 :]
-    early, coef, amplitude = refs[:3]
-    slots, sem = refs[3:-1], refs[-1]
-    snaps = early.shape[5]
-    cols = early.shape[2]
+    own, (edge, other, pair, away, pair_other, away_other) = refs[:planes], refs[planes : planes + 6]
+    early, coef, amplitude, mod, metric_mine, large_mine, wide, field, sem = refs[planes + 6 :]
+    snaps, cols = early.shape[5], early.shape[2]
+    extra = wide.shape[2]
     chip, core = whereabouts()
     first = pl.multiple_of((chip * CORES + core) * cols, 8)
-    views = [modulation, metric.at[:, :, pl.ds(first, cols)], large]
-    views += [item.at[:, core] for item in sources[:planes]]
-    edge, other, low, high, low_other, high_other = sources[planes:]
-    views += [edge, other, low.at[:, core], high.at[:, core], low_other, high_other]
-    fetch_all(views, slots, sem.at[0])
-    mod, metric, large = slots[:3]
-    own = slots[3 : planes + 3]
-    edge, other, low, high, low_other, high_other = slots[planes + 3 :]
-
-    wide = jnp.concatenate([mod[...], mod[...]], axis=1)
-    wide = pltpu.roll(wide, lax.rem(wide.shape[1] + 1 - first, wide.shape[1]), 1)
+    middle, left, right = pl.ds(1, cols), pl.ds(0, 1), pl.ds(cols + 1, 1)
+    moves = [
+        (modulation, mod),
+        (metric.at[:, :, pl.ds(first, cols)], metric_mine),
+        (large, large_mine),
+    ]
+    for slot in range(planes):
+        plane = plane_at(slot, planes) + 1
+        moves += [
+            (own[slot].at[:, core, pl.ds(0, cols)], field.at[0, plane, :, middle]),
+            (edge.at[:, pl.ds(2 * slot, 1)], field.at[0, plane, :, left]),
+            (edge.at[:, pl.ds(2 * slot + 1, 1)], field.at[0, plane, :, right]),
+            (other.at[:, slot], field.at[1, plane]),
+        ]
+    for slot, (close, far) in enumerate(((pair, pair_other), (away, away_other))):
+        halo = halo_at(slot, planes)
+        moves += [
+            (close.at[:, core, pl.ds(0, cols)], field.at[0, halo, :, middle]),
+            (far.at[:, pl.ds(0, cols)], field.at[1, halo, :, middle]),
+            (close.at[:, core, pl.ds(cols, extra)], wide.at[jnp.minimum(halo, 1)]),
+        ]
+    fetch_all(moves, sem.at[0])
+
+    doubled = jnp.concatenate([mod[...], mod[...]], axis=1)
+    doubled = pltpu.roll(doubled, lax.rem(doubled.shape[1] + 1 - first, doubled.shape[1]), 1)
     for col in range(cols + 2):
-        amplitude[col] = jnp.broadcast_to(wide[:, col : col + 1], amplitude.shape[1:])
-    coefficients(own, low, high, metric, large, coef, first)
-
-    def gets(step, part, comp, plane, col):
-        if plane < 0:
-            return (low_other if part else low)[comp, col]
-        if plane == planes:
-            return (high_other if part else high)[comp, col]
-        if part:
-            return other[comp, plane, col + 1]
-        if col in (-1, cols):
-            return edge[comp, 2 * plane + (col > 0)]
-        return own[plane][comp, col]
-
-    for plane in range(planes):
+        amplitude[col] = jnp.broadcast_to(doubled[:, col : col + 1], amplitude.shape[1:])
+    coefficients(wide, metric_mine, large_mine, coef, first)
+
+    def tile(step, part, comp, plane, col):
+        return field[part, plane, comp, col]
+
+    for slot in range(planes):
 
         def store(comp, col, step, part, start, halves):
             for level in range(2):
-                early[comp, plane, col, level, part] = halves[level]
-
-        curls(chips, gets, [0], coef, amplitude, plane, cols, snaps, store)
+                early[comp, slot, col, level, part] = halves[level]
+
+        curls(chips, tile, [0], coef, amplitude, plane_at(slot, planes), cols, snaps, store)
+
+
+def fetch_all(moves, sem):
+    copies = [pltpu.make_async_copy(source, target, sem) for source, target in moves]
+    for item in copies:
+        item.start()
+    for item in copies:
+        item.wait()
 
 
 def near_stage(modulation, metric, large, sources, chips, cols):
-    everyone, width = modulation.shape
+    everyone, _ = modulation.shape
     comps, planes, _, depth = large.shape
     snaps = everyone // (chips * CORES)
+    extra = sources[0].shape[2] - cols
     whole = pl.BlockSpec(memory_space=pltpu.VMEM)
-    shapes = [item.shape for item in sources]
-    halved = [shape[:1] + shape[2:] for shape in shapes]
-    shapes = halved[:planes] + shapes[planes : planes + 2] + halved[planes + 2 : planes + 4] + shapes[planes + 4 :]
-    slots = [
-        pltpu.VMEM(modulation.shape, modulation.dtype),
-        pltpu.VMEM((4, planes, cols, depth), metric.dtype),
-        pltpu.VMEM(large.shape, large.dtype),
-    ]
-    slots += [pltpu.VMEM(shape, large.dtype) for shape in shapes]
     return pl.pallas_call(
         functools.partial(near_kernel, chips, planes),
         in_specs=[pl.BlockSpec(memory_space=pl.ANY)] * (3 + len(sources)),
@@ -295,33 +308,44 @@
             jax.ShapeDtypeStruct((planes, 11, cols, depth), jnp.float32),
             jax.ShapeDtypeStruct((cols + 2, everyone, depth), jnp.float32),
         ],
-        scratch_shapes=slots + [pltpu.SemaphoreType.DMA((1,))],
+        scratch_shapes=[
+            pltpu.VMEM(modulation.shape, modulation.dtype),
+            pltpu.VMEM((4, planes, cols, depth), metric.dtype),
+            pltpu.VMEM(large.shape, large.dtype),
+            pltpu.VMEM((2, comps, extra, snaps, depth), large.dtype),
+            pltpu.VMEM((CORES, planes + 2, comps, cols + 2, snaps, depth), large.dtype),
+            pltpu.SemaphoreType.DMA((1,)),
+        ],
         compiler_params=pltpu.CompilerParams(vmem_limit_bytes=VMEM_BYTES),
         cost_estimate=pl.CostEstimate(flops=0, bytes_accessed=8 << 20, transcendentals=0),
         name="near_stage",
     )(modulation, metric, large, *sources)
 
 
-def far_kernel(chips, keys, first, planes, coef, amplitude, early, before, *refs):
-    sources, refs = refs[: len(keys)], refs[len(keys) :]
-    parts, gram, total = refs[:3]
-    slots, sem = refs[3:-1], refs[-1]
-    arrays = dict(zip(keys, slots))
-    cols = early.shape[2]
-    snaps = early.shape[5]
+def far_kernel(chips, planes, slots, halo, coef, amplitude, early, before, *refs):
+    sources, (parts, gram, field, total, sem) = list(refs[:-5]), refs[-5:]
+    cols, snaps = early.shape[2], early.shape[5]
     everyone = amplitude.shape[1]
-    fetch_all(sources, slots, sem.at[0])
-
-    def gets(step, part, comp, plane, col):
-        span = slice(part * snaps, (part + 1) * snaps)
-        if 0 <= plane < planes and col in (-1, cols):
-            return arrays[step, "edge"][comp, 2 * plane + (col > 0), span]
-        name = "low" if plane < 0 else "high" if plane == planes else plane
-        return arrays[step, name][comp, col, span]
+    middle, left, right = pl.ds(1, cols), pl.ds(0, 1), pl.ds(cols + 1, 1)
+    moves = []
+    for step in range(1, chips):
+        own = [sources.pop(0) for _ in range(planes)]
+        edge, beyond = sources.pop(0), sources.pop(0)
+        for slot in range(planes):
+            target = field.at[step - 1, plane_at(slot, planes) + 1]
+            moves += [
+                (own[slot], target.at[:, middle]),
+                (edge.at[:, pl.ds(2 * slot, 1)], target.at[:, left]),
+                (edge.at[:, pl.ds(2 * slot + 1, 1)], target.at[:, right]),
+            ]
+        moves.append((beyond, field.at[step - 1, halo_at(halo, planes), :, middle]))
+    fetch_all(moves, sem.at[0])
+
+    def tile(step, part, comp, plane, col):
+        return field[step - 1, plane, comp, col, part * snaps : (part + 1) * snaps]
 
     total[...] = jnp.zeros_like(total)
-    for index in range(parts.shape[1]):
-        plane = first + index
+    for index, slot in enumerate(slots):
 
         def store(comp, col, step, part, start, halves):
             for level in range(2):
@@ -331,10 +355,11 @@
             start = rows_of(chips, 0, part, snaps)
             for comp in range(3):
                 for col in range(cols):
-                    halves = [early[comp, plane, col, level, part] for level in range(2)]
+                    halves = [early[comp, slot, col, level, part] for level in range(2)]
                     store(comp, col, 0, part, start, halves)
         steps = range(1, chips)
-        curls(chips, gets, steps, coef, amplitude, plane, cols, snaps, store)
+        plane = plane_at(slot, planes)
+        curls(chips, tile, steps, coef, amplitude, plane, cols, snaps, store)
         for comp in range(3):
             for col in range(0, cols, 2):
                 both = jnp.concatenate([parts[comp, index, col], parts[comp, index, col + 1]], 1)
@@ -348,31 +373,29 @@
     )
 
 
-def far_stage(coef, amplitude, early, before, arrays, chips, first, last):
+def far_stage(coef, amplitude, early, before, sources, chips, slots, halo):
     comps, planes, cols, _, _, snaps, depth = early.shape
     everyone = snaps * chips * CORES
-    wanted = {"edge"} | set(range(max(first - 1, 0), min(last + 1, planes)))
-    if first == 0:
-        wanted.add("low")
-    if last == planes:
-        wanted.add("high")
-    chosen = {key: item for key, item in arrays.items() if key[1] in wanted}
     whole = pl.BlockSpec(memory_space=pltpu.VMEM)
     return pl.pallas_call(
-        functools.partial(far_kernel, chips, tuple(chosen), first, planes),
-        in_specs=[whole] * 4 + [pl.BlockSpec(memory_space=pl.ANY)] * len(chosen),
+        functools.partial(far_kernel, chips, planes, slots, halo),
+        in_specs=[whole] * 4 + [pl.BlockSpec(memory_space=pl.ANY)] * len(sources),
         out_specs=[whole, whole],
         out_shape=[
-            jax.ShapeDtypeStruct((comps, last - first, cols, 2 * everyone, depth), jnp.bfloat16),
+            jax.ShapeDtypeStruct((comps, len(slots), cols, 2 * everyone, depth), jnp.bfloat16),
             jax.ShapeDtypeStruct((everyone, everyone), jnp.float32),
         ],
-        scratch_shapes=[pltpu.VMEM((2 * everyone, 2 * everyone), jnp.float32)]
-        + [pltpu.VMEM(item.shape, item.dtype) for item in chosen.values()]
-        + [pltpu.SemaphoreType.DMA((1,))],
+        scratch_shapes=[
+            pltpu.VMEM(
+                (chips - 1, planes + 2, comps, cols + 2, CORES * snaps, depth), jnp.bfloat16
+            ),
+            pltpu.VMEM((2 * everyone, 2 * everyone), jnp.float32),
+            pltpu.SemaphoreType.DMA((1,)),
+        ],
         compiler_params=pltpu.CompilerParams(vmem_limit_bytes=VMEM_BYTES),
         cost_estimate=pl.CostEstimate(flops=0, bytes_accessed=8 << 20, transcendentals=0),
         name="far_stage",
-    )(coef, amplitude, early, before, *chosen.values())
+    )(coef, amplitude, early, before, *sources)
 
 
 def whiten_kernel(count, gram, *refs):
@@ -398,9 +421,12 @@
         inverse = dot(factor, inverse)
     top, rest = split(inverse / jnp.sqrt(frob_scale))
     left = jnp.concatenate([top, top, rest, rest], axis=1)
-    slot, plane, copies = 0, 0, []
+    slot, copies = 0, []
+    planes = sum(piece.shape[1] for piece in pieces)
+    order = [1] + list(range(2, planes)) + [0]
     for piece in pieces:
         for index in range(piece.shape[1]):
+            plane = plane_at(order.pop(0), planes)
             for comp in range(comps):
                 for first in range(0, cols, 2):
                     both = [piece[comp, index, first], piece[comp, index, first + 1]]
@@ -424,7 +450,6 @@
                 )
                 copies[-1].start()
                 slot += 1
-            plane += 1
     for item in copies:
         item.wait()
 
@@ -459,10 +484,10 @@
     return lax.ppermute(array, "snap", [(i, i ^ 1) for i in range(lax.axis_size("snap"))])
 
 
-def to_slab(array, step):
+def to_pair(array, first):
     count = lax.axis_size("slab")
-    pairs = [(i, i + step) for i in range(count) if 0 <= i + step < count]
-    return lax.ppermute(array, "slab", pairs)
+    pairs = [(i, i + 1) for i in range(first, count - 1, 2)]
+    return lax.ppermute(array, "slab", pairs + [(j, i) for i, j in pairs])
 
 
 def all_sum(value):
@@ -490,29 +515,31 @@
     def half(array):
         return lax.dynamic_index_in_dim(array, 1 - core, 1, keepdims=False)
 
-    own, own_edge, own_other, mine, other = pack(flow, large_scale, chips, cols)
-    low, high = to_slab(own[-1], 1), to_slab(own[0], -1)
-    arrays = {}
+    assert planes >= 2
+    own, mine, other = pack(flow, large_scale, chips, cols)
+    pair = to_pair(own[0], 0)
+    outer, arrays = own[1], []
     for step in range(1, chips):
         both = jnp.concatenate([mine[step - 1], to_core(other[step - 1])], axis=3)
-        order = [planes - 1] + list(range(planes - 1))
-        for plane in order:
-            arrays[step, plane] = to_chip(both[:, plane, 1:-1], step)
+        outer, both = lax.optimization_barrier((outer, both))
+        here = [to_chip(both[:, slot, 1:-1], step) for slot in range(planes)]
         edge = jnp.stack([both[:, :, 0], both[:, :, -1]], axis=2)
         edge = edge.reshape(comps, 2 * planes, *edge.shape[3:])
-        edge, _ = lax.optimization_barrier((edge, arrays[step, 0]))
-        arrays[step, "edge"] = to_chip(edge, step)
-        arrays[step, "low"] = to_slab(arrays[step, planes - 1], 1)
-        arrays[step, "high"] = to_slab(arrays[step, 0], -1)
-    sources = own + [own_edge, to_core(own_other), low, high]
-    sources += [to_core(half(low)), to_core(half(high))]
+        edge, _ = lax.optimization_barrier((edge, here[0]))
+        arrays.append((here + [to_chip(edge, step)], to_pair(here[0], 0), to_pair(here[1], 1)))
+    away = to_pair(outer, 1)
+    pair, away, _ = lax.optimization_barrier((pair, away, [here[:planes] for here, *_ in arrays]))
+    sources = own + [mine[-1], to_core(other[-1]), pair, away]
+    sources += [to_core(half(pair)), to_core(half(away))]
     early, coef, amplitude = near_stage(modulation, metric, large_scale, sources, chips, cols)
     gram = jnp.zeros(modulation.shape[:1] * 2, jnp.float32)
     pieces = []
-    for begin, end in ((0, planes - 1), (planes - 1, planes)):
-        if begin < end:
-            piece, gram = far_stage(coef, amplitude, early, gram, arrays, chips, begin, end)
-            pieces.append(piece)
+    for slots, halo in (((1,) + tuple(range(2, planes)), 1), ((0,), 0)):
+        sources = []
+        for here, *halos in arrays:
+            sources += here + [halos[halo]]
+        piece, gram = far_stage(coef, amplitude, early, gram, sources, chips, slots, halo)
+        pieces.append(piece)
     return whiten(all_sum(gram), pieces, float(comps * planes * slab_count * width * depth))
 
 

time: 79.1 us -> 68.9 us (0.87)
  waiting for transfers between devices: 35.5 us -> 30.4 us
  starting transfers between devices: 25.3 us -> 21.2 us
  Pallas kernels: 13.5 us -> 12.6 us
    ppermute x4, waiting for transfers between devices: 23.6 us -> 3.26 us  [to_pair(): return lax.ppermute(array, 'slab', pairs + [(j, i) for i, j in pairs])]
    ppermute x3, waiting for transfers between devices: 1.87 us -> 17.2 us  [to_chip(): return lax.ppermute(array, 'snap', pairs)]
    ppermute x4, starting transfers between devices: 12.2 us -> 8.06 us  [to_pair(): return lax.ppermute(array, 'slab', pairs + [(j, i) for i, j in pairs])]
    pallas_call x2, Pallas kernels: 3.95 us -> 3.07 us  [far_stage(): pl.pallas_call(functools.partial(far_kernel, chips, planes, slots, halo),...]
    pallas_call x2 -> x3, Pallas kernels: 2.46 us -> 2.94 us  [call(): pl.pallas_call(kernel, grid=(comps,), in_specs=[pl.BlockSpec((snaps, 1, p...]
    unnamed x13 -> x12, local copies, waits for them, and re-layouts: 2.36 us -> 2.32 us
  transfers between devices with their start and end apart: 16 -> 16, of which waited for: 9 -> 9; matrix products, arithmetic and copies ran while one was open for 2% -> 3% of each run, Pallas kernels for 6% -> 6%
where the time goes in v3:
time: 68.9 us; the launch traced here: 68.6 us
  waiting for transfers between devices  30.4 us (44%)
  starting transfers between devices  21.2 us (31%)
  Pallas kernels  12.6 us (18%)
  local copies, waits for them, and re-layouts  4.21 us (6%)
    ppermute x3, waiting for transfers between devices, to_chip(): return lax.ppermute(array, 'snap', pairs)  17.2 us
    ppermute x5, waiting for transfers between devices, all_sum(): value = value + lax.ppermute(value, axis, pairs)  9.9 us
    ppermute x5, starting transfers between devices, all_sum(): value = value + lax.ppermute(value, axis, pairs)  8.38 us
    ppermute x4, starting transfers between devices, to_pair(): return lax.ppermute(array, 'slab', pairs + [(j, i) for i, j in pairs])  8.06 us
    pallas_call x1, Pallas kernels, whiten(): pl.pallas_call(functools.partial(whiten_kernel, count), in_specs=[whole]...  4.32 us
    ppermute x3, starting transfers between devices, to_chip(): return lax.ppermute(array, 'snap', pairs)  3.58 us
    ppermute x4, waiting for transfers between devices, to_pair(): return lax.ppermute(array, 'slab', pairs + [(j, i) for i, j in pairs])  3.26 us
    pallas_call x2, Pallas kernels, far_stage(): pl.pallas_call(functools.partial(far_kernel, chips, planes, slots, halo),...  3.07 us
  transfers between devices with their start and end apart: 16, of which 9 were waited for; matrix products, arithmetic and copies ran while one was open for 3% of the time, Pallas kernels for 6%

profile of v3, /device:TPU:0, one launch (start us, length us, event | category | flops | bytes accessed | tf_op | source)
XLA Modules:
  0.0 68.6 jit_solution(7197552517381686850)
XLA Ops:
  0.0 1.4 %copy-done = bf16[16,3,2,64,128]{4,3,2,1,0:T(8,128)(2,1)S(1)} copy-done((bf16[16,3,2,64,128]{4,3,2,1,0:T(8,128)(2,1)S(1)}, bf16[16,3,2,64,128]{4,3,2,1,0:T(8,128)(2,1)}, u32[]{:S(2)}) %copy-start) | copy-done | bytes 1572888
  1.4 0.9 %copy-done.1 = bf16[3,2,64,128]{3,2,1,0:T(8,128)(2,1)S(1)} copy-done((bf16[3,2,64,128]{3,2,1,0:T(8,128)(2,1)S(1)}, bf16[3,2,64,128]{3,2,1,0:T(8,128)(2,1)}, u32[]{:S(2)}) %copy-start.1) | copy-done | bytes 98328
  2.3 0.7 %pack_own.1 = (bf16[3,2,17,16,128]{4,3,2,1,0:T(8,128)(2,1)S(1)}, bf16[3,2,17,16,128]{4,3,2,1,0:T(8,128)(2,1)S(1)}) custom-call(bf16[16,3,2,64,128]{4,3,2,1,0:T(8,128)(2,1)S(1)} %copy-done, bf16[3,2,64,128]{3,2,1,0:T(8,128)(2,1)S(1)} %copy-done.1), custom_call_target="tpu_custom_call" | custom-call | tf_op jit(solution)/shard_map/pack_own/pallas_call | solution.py:104
  3.0 1.7 %pack_other.1 = (bf16[3,2,18,16,128]{4,3,2,1,0:T(8,128)(2,1)S(1)}, bf16[3,2,18,16,128]{4,3,2,1,0:T(8,128)(2,1)}) custom-call(bf16[16,3,2,64,128]{4,3,2,1,0:T(8,128)(2,1)S(1)} %copy-done, bf16[3,2,17,16,128]{4,3,2,1,0:T(8,128)(2,1)S(1)} %get-tuple-element.23.first.refs_0_), custom_call_target="tpu_custom_call" | custom-call | tf_op jit(solution)/shard_map/pack_other/pallas_call | solution.py:104
  4.8 0.5 collective-permute-start.2
  5.3 2.6 %collective-permute-start.1 = (bf16[3,2,17,16,128]{4,3,2,1,0:T(8,128)(2,1)S(1)}, bf16[3,2,17,16,128]{4,3,2,1,0:T(8,128)(2,1)S(1)}, u32[]{:S(2)}, u32[]{:S(2)}) collective-permute-start(bf16[3,2,17,16,128]{4,3,2,1,0:T(8,128)(2,1)S(1)} %get-tuple-element.23.first.refs_0_), channel_id=1, source_target_pairs={{0,4},{8,12},{16,20},{24,28},{4,0},{12,8},{20,16},{28,24},{1,5},{9... | collective-permute-start | bytes 1253384 | tf_op jit(solution)/shard_map/ppermute | solution.py:490
  7.9 0.5 pack_mine.1
  8.4 0.0 collective-permute-done.2
  8.4 0.1 pad_maximum_fusion
  8.5 0.0 copy-start.5
  8.5 0.0 copy-start.2
  8.5 0.0 copy-start.3
  8.5 0.0 copy-start.4
  8.5 0.8 %collective-permute-start.3 = (bf16[3,2,17,16,128]{4,3,2,1,0:T(8,128)(2,1)S(1)}, bf16[3,2,17,16,128]{4,3,2,1,0:T(8,128)(2,1)S(1)}, u32[]{:S(2)}, u32[]{:S(2)}) collective-permute-start(bf16[3,2,17,16,128]{4,3,2,1,0:T(8,128)(2,1)S(1)} %get-tuple-element.29.refs_1_), channel_id=1, source_target_pairs={{4,8},{12,16},{20,24},{8,4},{16,12},{24,20},{5,9},{13,17},{21,25},... | collective-permute-start | bytes 1253384 | tf_op jit(solution)/shard_map/ppermute | solution.py:490
  9.4 1.0 %slice_bitcast_fusion = (bf16[3,16,32,128]{3,2,1,0:T(8,128)(2,1)}, bf16[3,16,32,128]{3,2,1,0:T(8,128)(2,1)}) fusion(bf16[3,2,18,32,128]{4,3,2,0,1:T(8,128)(2,1)S(1)} %pad_maximum_fusion), kind=kLoop, calls=%fused_computation.1 | loop fusion | bytes 1572864 | tf_op jit(solution)/shard_map/squeeze | solution.py:525
  10.3 1.5 %collective-permute-start.5 = (bf16[3,16,32,128]{3,2,1,0:T(8,128)(2,1)}, bf16[3,16,32,128]{3,2,1,0:T(8,128)(2,1)S(1)}, u32[]{:S(2)}, u32[]{:S(2)}) collective-permute-start(bf16[3,16,32,128]{3,2,1,0:T(8,128)(2,1)} %get-tuple-element.43), channel_id=1, source_target_pairs={{0,2},{1,3},{2,0},{3,1},{4,6},{5,7},{6,4},{7,5},{8,10},{9,11},{10,... | collective-permute-start | bytes 1179656 | tf_op jit(solution)/shard_map/ppermute | solution.py:480
  11.8 0.5 collective-permute-start.4
  12.4 0.0 collective-permute-start
  12.4 0.8 %fusion = (bf16[3,2,1,32,128]{4,3,2,0,1:T(8,128)(2,1)S(1)}, bf16[3,2,1,32,128]{4,3,2,0,1:T(8,128)(2,1)S(1)}) fusion(bf16[3,2,18,32,128]{4,3,2,0,1:T(8,128)(2,1)} %copy-done.5), kind=kLoop, calls=%fused_computation.6 | loop fusion | bytes 196608 | tf_op jit(solution)/shard_map/slice | solution.py:526
  13.2 9.3 %collective-permute-done.5.refs_1_ = bf16[3,16,32,128]{3,2,1,0:T(8,128)(2,1)S(1)} collective-permute-done((bf16[3,16,32,128]{3,2,1,0:T(8,128)(2,1)}, bf16[3,16,32,128]{3,2,1,0:T(8,128)(2,1)S(1)}, u32[]{:S(2)}, u32[]{:S(2)}) %collective-permute-start.5) | collective-permute-done | bytes 393248 | tf_op jit(solution)/shard_map/ppermute | solution.py:480
  22.5 0.7 collective-permute-start.9
  23.2 7.0 %collective-permute-done.4.refs_0_ = bf16[3,16,32,128]{3,2,1,0:T(8,128)(2,1)S(1)} collective-permute-done((bf16[3,16,32,128]{3,2,1,0:T(8,128)(2,1)}, bf16[3,16,32,128]{3,2,1,0:T(8,128)(2,1)S(1)}, u32[]{:S(2)}, u32[]{:S(2)}) %collective-permute-start.4) | collective-permute-done | bytes 393248 | tf_op jit(solution)/shard_map/ppermute | solution.py:480
  30.2 4.0 %collective-permute-start.10 = (bf16[3,16,32,128]{3,2,1,0:T(8,128)(2,1)S(1)}, bf16[3,16,32,128]{3,2,1,0:T(8,128)(2,1)S(1)}, u32[]{:S(2)}, u32[]{:S(2)}) collective-permute-start(bf16[3,16,32,128]{3,2,1,0:T(8,128)(2,1)S(1)} %collective-permute-done.4.refs_0_), channel_id=1, source_target_pairs={{0,4},{8,12},{16,20},{24,28},{4,0},{12,8},{20,16},{28,24},{1,5},{9... | collective-permute-start | bytes 1179656 | tf_op jit(solution)/shard_map/ppermute | solution.py:490
  34.1 0.0 collective-permute-done.1.refs_4_
  34.1 0.0 collective-permute-done.3.refs_5_
  34.2 0.1 collective-permute-start.7
  34.3 0.5 collective-permute-start.6
  34.9 0.0 collective-permute-done.refs_3_
  34.9 1.6 %collective-permute-start.8 = (bf16[3,4,32,128]{3,2,1,0:T(8,128)(2,1)S(1)}, bf16[3,4,32,128]{3,2,1,0:T(8,128)(2,1)S(1)}, u32[]{:S(2)}, u32[]{:S(2)}) collective-permute-start(bf16[3,4,32,128]{3,2,1,0:T(8,128)(2,1)S(1)} %bitcast.9), channel_id=1, source_target_pairs={{0,2},{1,3},{2,0},{3,1},{4,6},{5,7},{6,4},{7,5},{8,10},{9,11},{10,... | collective-permute-start | bytes 294920 | tf_op jit(solution)/shard_map/ppermute | solution.py:480
  36.4 0.0 collective-permute-done.7.refs_7_
  36.4 0.0 collective-permute-done.6.refs_6_
  36.5 2.3 %near_stage.1 = (bf16[3,2,16,2,2,16,128]{6,5,4,3,2,1,0:T(8,128)(2,1)S(1)}, f32[2,11,16,128]{3,2,1,0:T(8,128)S(1)}, f32[18,64,128]{2,1,0:T(8,128)S(1)}) custom-call(f32[64,64]{1,0:T(8,128)S(1)} %copy-done.4, f32[4,2,64,128]{3,2,1,0:T(8,128)S(1)} %copy-done.3, bf16[3,2,64,128]{3,2,1,0:T(8,128)(2,1)S(1)} %copy-done.2, ...), custom_call_target="tpu_custom_call" | custom-call | bytes 8388608 | tf_op jit(solution)/shard_map/near_stage/pallas_call | solution.py:302
  38.8 0.9 %collective-permute-done.8.refs_2_ = bf16[3,4,32,128]{3,2,1,0:T(8,128)(2,1)S(1)} collective-permute-done((bf16[3,4,32,128]{3,2,1,0:T(8,128)(2,1)S(1)}, bf16[3,4,32,128]{3,2,1,0:T(8,128)(2,1)S(1)}, u32[]{:S(2)}, u32[]{:S(2)}) %collective-permute-start.8) | collective-permute-done | bytes 98336 | tf_op jit(solution)/shard_map/ppermute | solution.py:480
  39.7 0.0 collective-permute-done.9.refs_3_
  39.7 1.5 %far_stage.2 = (bf16[3,1,16,128,128]{4,3,2,1,0:T(8,128)(2,1)S(1)}, f32[64,64]{1,0:T(8,128)S(1)}) custom-call(f32[2,11,16,128]{3,2,1,0:T(8,128)S(1)} %get-tuple-element.33.coef, f32[18,64,128]{2,1,0:T(8,128)S(1)} %get-tuple-element.34.amplitude, bf16[3,2,16,2,2,16,128]{6,5,4,3,2,1,0:T(8,128)(2,1)S(1)} %get-tuple-element.35.early, ...), custom_call_target="tpu_custom_call" | custom-call | bytes 8388608 | tf_op jit(solution)/shard_map/far_stage/pallas_call | solution.py:380
  41.2 3.3 %collective-permute-done.10.refs_3_ = bf16[3,16,32,128]{3,2,1,0:T(8,128)(2,1)S(1)} collective-permute-done((bf16[3,16,32,128]{3,2,1,0:T(8,128)(2,1)S(1)}, bf16[3,16,32,128]{3,2,1,0:T(8,128)(2,1)S(1)}, u32[]{:S(2)}, u32[]{:S(2)}) %collective-permute-start.10) | collective-permute-done | bytes 393248 | tf_op jit(solution)/shard_map/ppermute | solution.py:490
  44.5 1.5 %far_stage.3 = (bf16[3,1,16,128,128]{4,3,2,1,0:T(8,128)(2,1)S(1)}, f32[64,64]{1,0:T(8,128)S(1)}) custom-call(f32[2,11,16,128]{3,2,1,0:T(8,128)S(1)} %get-tuple-element.33.coef, f32[18,64,128]{2,1,0:T(8,128)S(1)} %get-tuple-element.34.amplitude, bf16[3,2,16,2,2,16,128]{6,5,4,3,2,1,0:T(8,128)(2,1)S(1)} %get-tuple-element.35.early, ...), custom_call_target="tpu_custom_call" | custom-call | bytes 8388608 | tf_op jit(solution)/shard_map/far_stage/pallas_call | solution.py:380
  46.0 0.1 collective-permute-start.11
  46.1 1.2 %collective-permute-done.11 = f32[64,64]{1,0:T(8,128)S(1)} collective-permute-done((f32[64,64]{1,0:T(8,128)S(1)}, f32[64,64]{1,0:T(8,128)S(1)}, u32[]{:S(2)}, u32[]{:S(2)}) %collective-permute-start.11) | collective-permute-done | bytes 16416 | tf_op jit(solution)/shard_map/ppermute | solution.py:502
  47.3 1.5 %collective-permute-start.12 = (f32[64,64]{1,0:T(8,128)S(1)}, f32[64,64]{1,0:T(8,128)S(1)}, u32[]{:S(2)}, u32[]{:S(2)}) collective-permute-start(f32[64,64]{1,0:T(8,128)S(1)} %add.22), channel_id=1, source_target_pairs={{0,2},{1,3},{2,0},{3,1},{4,6},{5,7},{6,4},{7,5},{8,10},{9,11},{10,... | collective-permute-start | bytes 49160 | tf_op jit(solution)/shard_map/ppermute | solution.py:502
  48.8 2.4 %collective-permute-done.12 = f32[64,64]{1,0:T(8,128)S(1)} collective-permute-done((f32[64,64]{1,0:T(8,128)S(1)}, f32[64,64]{1,0:T(8,128)S(1)}, u32[]{:S(2)}, u32[]{:S(2)}) %collective-permute-start.12) | collective-permute-done | bytes 16416 | tf_op jit(solution)/shard_map/ppermute | solution.py:502
  51.2 2.5 %collective-permute-start.13 = (f32[64,64]{1,0:T(8,128)S(1)}, f32[64,64]{1,0:T(8,128)S(1)}, u32[]{:S(2)}, u32[]{:S(2)}) collective-permute-start(f32[64,64]{1,0:T(8,128)S(1)} %add.23), channel_id=1, source_target_pairs={{0,4},{4,0},{8,12},{12,8},{16,20},{20,16},{24,28},{28,24},{1,5},{5... | collective-permute-start | bytes 49160 | tf_op jit(solution)/shard_map/ppermute | solution.py:502
  53.7 1.9 %collective-permute-done.13 = f32[64,64]{1,0:T(8,128)S(1)} collective-permute-done((f32[64,64]{1,0:T(8,128)S(1)}, f32[64,64]{1,0:T(8,128)S(1)}, u32[]{:S(2)}, u32[]{:S(2)}) %collective-permute-start.13) | collective-permute-done | bytes 16416 | tf_op jit(solution)/shard_map/ppermute | solution.py:502
  55.6 1.6 %collective-permute-start.14 = (f32[64,64]{1,0:T(8,128)S(1)}, f32[64,64]{1,0:T(8,128)S(1)}, u32[]{:S(2)}, u32[]{:S(2)}) collective-permute-start(f32[64,64]{1,0:T(8,128)S(1)} %add.24), channel_id=1, source_target_pairs={{0,8},{4,12},{8,0},{12,4},{16,24},{20,28},{24,16},{28,20},{1,9},{5... | collective-permute-start | bytes 49160 | tf_op jit(solution)/shard_map/ppermute | solution.py:502
  57.2 2.3 %collective-permute-done.14 = f32[64,64]{1,0:T(8,128)S(1)} collective-permute-done((f32[64,64]{1,0:T(8,128)S(1)}, f32[64,64]{1,0:T(8,128)S(1)}, u32[]{:S(2)}, u32[]{:S(2)}) %collective-permute-start.14) | collective-permute-done | bytes 16416 | tf_op jit(solution)/shard_map/ppermute | solution.py:502
  59.5 2.8 %collective-permute-start.15 = (f32[64,64]{1,0:T(8,128)S(1)}, f32[64,64]{1,0:T(8,128)S(1)}, u32[]{:S(2)}, u32[]{:S(2)}) collective-permute-start(f32[64,64]{1,0:T(8,128)S(1)} %add.25), channel_id=1, source_target_pairs={{0,16},{4,20},{8,24},{12,28},{16,0},{20,4},{24,8},{28,12},{1,17},{... | collective-permute-start | bytes 49160 | tf_op jit(solution)/shard_map/ppermute | solution.py:502
  62.3 2.0 %collective-permute-done.15 = f32[64,64]{1,0:T(8,128)S(1)} collective-permute-done((f32[64,64]{1,0:T(8,128)S(1)}, f32[64,64]{1,0:T(8,128)S(1)}, u32[]{:S(2)}, u32[]{:S(2)}) %collective-permute-start.15) | collective-permute-done | bytes 16416 | tf_op jit(solution)/shard_map/ppermute | solution.py:502
  64.3 4.3 %whiten.1 = f32[64,3,2,16,128]{4,3,2,1,0:T(8,128)} custom-call(f32[64,64]{1,0:T(8,128)S(1)} %add.26.gram, bf16[3,1,16,128,128]{4,3,2,1,0:T(8,128)(2,1)S(1)} %get-tuple-element.39.refs_0_, bf16[3,1,16,128,128]{4,3,2,1,0:T(8,128)(2,1)S(1)} %get-tuple-element.40.refs_1_), custom_call_target="tpu_custom_call" | custom-call | tf_op jit(solution)/shard_map/whiten/pallas_call | solution.py:463
  (17 shorter events, 0.1 us)
Async XLA Ops:
  0.0 1.4 %copy-start = (bf16[16,3,2,64,128]{4,3,2,1,0:T(8,128)(2,1)S(1)}, bf16[16,3,2,64,128]{4,3,2,1,0:T(8,128)(2,1)}, u32[]{:S(2)}) copy-start(bf16[16,3,2,64,128]{4,3,2,1,0:T(8,128)(2,1)} %flow.5) | copy-start | bytes 4718596
  1.4 0.9 %copy-start.1 = (bf16[3,2,64,128]{3,2,1,0:T(8,128)(2,1)S(1)}, bf16[3,2,64,128]{3,2,1,0:T(8,128)(2,1)}, u32[]{:S(2)}) copy-start(bf16[3,2,64,128]{3,2,1,0:T(8,128)(2,1)} %large.3) | copy-start | bytes 294916
  4.8 3.6 %collective-permute-start.2 = (bf16[3,2,18,16,128]{4,3,2,0,1:T(8,128)(2,1)S(1)}, bf16[3,2,18,16,128]{4,3,2,0,1:T(8,128)(2,1)S(1)}, u32[]{:S(2)}, u32[]{:S(2)}) collective-permute-start(bf16[3,2,18,16,128]{4,3,2,0,1:T(8,128)(2,1)S(1)} %copy.7), channel_id=1, source_target_pairs={{0,1},{1,0},{2,3},{3,2},{4,5},{5,4},{6,7},{7,6},{8,9},{9,8},{10,11... | collective-permute-start | bytes 1327112 | tf_op jit(solution)/shard_map/ppermute | solution.py:484
  5.3 28.9 %collective-permute-start.1 = (bf16[3,2,17,16,128]{4,3,2,1,0:T(8,128)(2,1)S(1)}, bf16[3,2,17,16,128]{4,3,2,1,0:T(8,128)(2,1)S(1)}, u32[]{:S(2)}, u32[]{:S(2)}) collective-permute-start(bf16[3,2,17,16,128]{4,3,2,1,0:T(8,128)(2,1)S(1)} %get-tuple-element.23.first.refs_0_), channel_id=1, source_target_pairs={{0,4},{8,12},{16,20},{24,28},{4,0},{12,8},{20,16},{28,24},{1,5},{9... | collective-permute-start | bytes 1253384 | tf_op jit(solution)/shard_map/ppermute | solution.py:490
  8.5 3.9 %copy-start.5 = (bf16[3,2,18,32,128]{4,3,2,0,1:T(8,128)(2,1)}, bf16[3,2,18,32,128]{4,3,2,0,1:T(8,128)(2,1)S(1)}, u32[]{:S(2)}) copy-start(bf16[3,2,18,32,128]{4,3,2,0,1:T(8,128)(2,1)S(1)} %pad_maximum_fusion) | copy-start | bytes 2654212
  8.5 27.9 %copy-start.2 = (bf16[3,2,64,128]{3,2,1,0:T(8,128)(2,1)S(1)}, bf16[3,2,64,128]{3,2,1,0:T(8,128)(2,1)}, u32[]{:S(2)}) copy-start(bf16[3,2,64,128]{3,2,1,0:T(8,128)(2,1)} %large.3) | copy-start | bytes 294916
  8.5 27.9 %copy-start.3 = (f32[4,2,64,128]{3,2,1,0:T(8,128)S(1)}, f32[4,2,64,128]{3,2,1,0:T(8,128)}, u32[]{:S(2)}) copy-start(f32[4,2,64,128]{3,2,1,0:T(8,128)} %metric.1) | copy-start | bytes 786436
  8.5 27.9 %copy-start.4 = (f32[64,64]{1,0:T(8,128)S(1)}, f32[64,64]{1,0:T(8,128)}, u32[]{:S(2)}) copy-start(f32[64,64]{1,0:T(8,128)} %modulation.1) | copy-start | bytes 49156
  8.5 25.6 %collective-permute-start.3 = (bf16[3,2,17,16,128]{4,3,2,1,0:T(8,128)(2,1)S(1)}, bf16[3,2,17,16,128]{4,3,2,1,0:T(8,128)(2,1)S(1)}, u32[]{:S(2)}, u32[]{:S(2)}) collective-permute-start(bf16[3,2,17,16,128]{4,3,2,1,0:T(8,128)(2,1)S(1)} %get-tuple-element.29.refs_1_), channel_id=1, source_target_pairs={{4,8},{12,16},{20,24},{8,4},{16,12},{24,20},{5,9},{13,17},{21,25},... | collective-permute-start | bytes 1253384 | tf_op jit(solution)/shard_map/ppermute | solution.py:490
  10.3 12.2 %collective-permute-start.5 = (bf16[3,16,32,128]{3,2,1,0:T(8,128)(2,1)}, bf16[3,16,32,128]{3,2,1,0:T(8,128)(2,1)S(1)}, u32[]{:S(2)}, u32[]{:S(2)}) collective-permute-start(bf16[3,16,32,128]{3,2,1,0:T(8,128)(2,1)} %get-tuple-element.43), channel_id=1, source_target_pairs={{0,2},{1,3},{2,0},{3,1},{4,6},{5,7},{6,4},{7,5},{8,10},{9,11},{10,... | collective-permute-start | bytes 1179656 | tf_op jit(solution)/shard_map/ppermute | solution.py:480
  11.8 18.3 %collective-permute-start.4 = (bf16[3,16,32,128]{3,2,1,0:T(8,128)(2,1)}, bf16[3,16,32,128]{3,2,1,0:T(8,128)(2,1)S(1)}, u32[]{:S(2)}, u32[]{:S(2)}) collective-permute-start(bf16[3,16,32,128]{3,2,1,0:T(8,128)(2,1)} %get-tuple-element.44), channel_id=1, source_target_pairs={{0,2},{1,3},{2,0},{3,1},{4,6},{5,7},{6,4},{7,5},{8,10},{9,11},{10,... | collective-permute-start | bytes 1179656 | tf_op jit(solution)/shard_map/ppermute | solution.py:480
  12.4 22.5 %collective-permute-start = (bf16[3,2,18,16,128]{4,3,2,1,0:T(8,128)(2,1)}, bf16[3,2,18,16,128]{4,3,2,1,0:T(8,128)(2,1)S(1)}, u32[]{:S(2)}, u32[]{:S(2)}) collective-permute-start(bf16[3,2,18,16,128]{4,3,2,1,0:T(8,128)(2,1)} %get-tuple-element.27), channel_id=1, source_target_pairs={{0,1},{1,0},{2,3},{3,2},{4,5},{5,4},{6,7},{7,6},{8,9},{9,8},{10,11... | collective-permute-start | bytes 1327112 | tf_op jit(solution)/shard_map/ppermute | solution.py:484
  22.5 17.2 %collective-permute-start.9 = (bf16[3,16,32,128]{3,2,1,0:T(8,128)(2,1)S(1)}, bf16[3,16,32,128]{3,2,1,0:T(8,128)(2,1)S(1)}, u32[]{:S(2)}, u32[]{:S(2)}) collective-permute-start(bf16[3,16,32,128]{3,2,1,0:T(8,128)(2,1)S(1)} %collective-permute-done.5.refs_1_), channel_id=1, source_target_pairs={{4,8},{12,16},{20,24},{8,4},{16,12},{24,20},{5,9},{13,17},{21,25},... | collective-permute-start | bytes 1179656 | tf_op jit(solution)/shard_map/ppermute | solution.py:490
  30.2 14.3 %collective-permute-start.10 = (bf16[3,16,32,128]{3,2,1,0:T(8,128)(2,1)S(1)}, bf16[3,16,32,128]{3,2,1,0:T(8,128)(2,1)S(1)}, u32[]{:S(2)}, u32[]{:S(2)}) collective-permute-start(bf16[3,16,32,128]{3,2,1,0:T(8,128)(2,1)S(1)} %collective-permute-done.4.refs_0_), channel_id=1, source_target_pairs={{0,4},{8,12},{16,20},{24,28},{4,0},{12,8},{20,16},{28,24},{1,5},{9... | collective-permute-start | bytes 1179656 | tf_op jit(solution)/shard_map/ppermute | solution.py:490
  34.2 2.3 %collective-permute-start.7 = (bf16[3,17,16,128]{3,2,1,0:T(8,128)(2,1)S(1)}, bf16[3,17,16,128]{3,2,1,0:T(8,128)(2,1)S(1)}, u32[]{:S(2)}, u32[]{:S(2)}) collective-permute-start(bf16[3,17,16,128]{3,2,1,0:T(8,128)(2,1)S(1)} %dynamic-slice_bitcast_fusion), channel_id=1, source_target_pairs={{0,1},{1,0},{2,3},{3,2},{4,5},{5,4},{6,7},{7,6},{8,9},{9,8},{10,11... | collective-permute-start | bytes 626696 | tf_op jit(solution)/shard_map/ppermute | solution.py:484
  34.3 2.1 %collective-permute-start.6 = (bf16[3,17,16,128]{3,2,1,0:T(8,128)(2,1)S(1)}, bf16[3,17,16,128]{3,2,1,0:T(8,128)(2,1)S(1)}, u32[]{:S(2)}, u32[]{:S(2)}) collective-permute-start(bf16[3,17,16,128]{3,2,1,0:T(8,128)(2,1)S(1)} %dynamic-slice_bitcast_fusion.1), channel_id=1, source_target_pairs={{0,1},{1,0},{2,3},{3,2},{4,5},{5,4},{6,7},{7,6},{8,9},{9,8},{10,11... | collective-permute-start | bytes 626696 | tf_op jit(solution)/shard_map/ppermute | solution.py:484
  34.9 4.8 %collective-permute-start.8 = (bf16[3,4,32,128]{3,2,1,0:T(8,128)(2,1)S(1)}, bf16[3,4,32,128]{3,2,1,0:T(8,128)(2,1)S(1)}, u32[]{:S(2)}, u32[]{:S(2)}) collective-permute-start(bf16[3,4,32,128]{3,2,1,0:T(8,128)(2,1)S(1)} %bitcast.9), channel_id=1, source_target_pairs={{0,2},{1,3},{2,0},{3,1},{4,6},{5,7},{6,4},{7,5},{8,10},{9,11},{10,... | collective-permute-start | bytes 294920 | tf_op jit(solution)/shard_map/ppermute | solution.py:480
  46.0 1.3 %collective-permute-start.11 = (f32[64,64]{1,0:T(8,128)S(1)}, f32[64,64]{1,0:T(8,128)S(1)}, u32[]{:S(2)}, u32[]{:S(2)}) collective-permute-start(f32[64,64]{1,0:T(8,128)S(1)} %get-tuple-element.38), channel_id=1, source_target_pairs={{0,1},{1,0},{2,3},{3,2},{4,5},{5,4},{6,7},{7,6},{8,9},{9,8},{10,11... | collective-permute-start | bytes 49160 | tf_op jit(solution)/shard_map/ppermute | solution.py:502
  47.3 3.9 %collective-permute-start.12 = (f32[64,64]{1,0:T(8,128)S(1)}, f32[64,64]{1,0:T(8,128)S(1)}, u32[]{:S(2)}, u32[]{:S(2)}) collective-permute-start(f32[64,64]{1,0:T(8,128)S(1)} %add.22), channel_id=1, source_target_pairs={{0,2},{1,3},{2,0},{3,1},{4,6},{5,7},{6,4},{7,5},{8,10},{9,11},{10,... | collective-permute-start | bytes 49160 | tf_op jit(solution)/shard_map/ppermute | solution.py:502
  51.2 4.4 %collective-permute-start.13 = (f32[64,64]{1,0:T(8,128)S(1)}, f32[64,64]{1,0:T(8,128)S(1)}, u32[]{:S(2)}, u32[]{:S(2)}) collective-permute-start(f32[64,64]{1,0:T(8,128)S(1)} %add.23), channel_id=1, source_target_pairs={{0,4},{4,0},{8,12},{12,8},{16,20},{20,16},{24,28},{28,24},{1,5},{5... | collective-permute-start | bytes 49160 | tf_op jit(solution)/shard_map/ppermute | solution.py:502
  55.6 3.9 %collective-permute-start.14 = (f32[64,64]{1,0:T(8,128)S(1)}, f32[64,64]{1,0:T(8,128)S(1)}, u32[]{:S(2)}, u32[]{:S(2)}) collective-permute-start(f32[64,64]{1,0:T(8,128)S(1)} %add.24), channel_id=1, source_target_pairs={{0,8},{4,12},{8,0},{12,4},{16,24},{20,28},{24,16},{28,20},{1,9},{5... | collective-permute-start | bytes 49160 | tf_op jit(solution)/shard_map/ppermute | solution.py:502
  59.5 4.8 %collective-permute-start.15 = (f32[64,64]{1,0:T(8,128)S(1)}, f32[64,64]{1,0:T(8,128)S(1)}, u32[]{:S(2)}, u32[]{:S(2)}) collective-permute-start(f32[64,64]{1,0:T(8,128)S(1)} %add.25), channel_id=1, source_target_pairs={{0,16},{4,20},{8,24},{12,28},{16,0},{20,4},{24,8},{28,12},{1,17},{... | collective-permute-start | bytes 49160 | tf_op jit(solution)/shard_map/ppermute | solution.py:502

commit v4 on v3

--- a/solution.py
+++ b/solution.py
@@ -10,6 +10,7 @@
 NSITER = 6
 CORES = 2
 VMEM_BYTES = 16 * 1024 * 1024
+PACK_BYTES = 58 * 1024 * 1024
 
 
 def whereabouts():
@@ -31,11 +32,10 @@
     return (1 - upper if slot == 0 else upper) * (planes + 1)
 
 
-def pack_columns(flow, flat, plane):
-    snaps, width = flow.shape[0], flow.shape[3]
-    pitch = width + 1
+def spread(flat, pitch, snaps, values_of):
     for snap in range(snaps):
-        flat[pl.ds(snap * pitch, width), :] = flow[snap, 0, plane].astype(jnp.float32)
+        values = values_of(snap)
+        flat[pl.ds(snap * pitch, values.shape[0]), :] = values.astype(jnp.float32)
 
     def column(col):
         return flat[pl.ds(col, snaps, stride=pitch), :].astype(jnp.bfloat16)
@@ -44,40 +44,51 @@
 
 
 def pack_own_kernel(planes, cols, flow, large, *refs):
-    own, (flat, near, large_rows, sem) = refs[:-4], refs[-4:]
-    snaps = flow.shape[0]
-    extra = own[0].shape[2] - cols
-    chip, _ = whereabouts()
-    comp = pl.program_id(0)
-    fetch = pltpu.make_async_copy(large.at[comp], near, sem.at[0])
+    own, (near, flat, near_large, rows, sems) = refs[:-5], refs[-5:]
+    snaps, comps, span = flow.shape[0], flow.shape[1], CORES * cols
+    chip, core = whereabouts()
+    first = pl.multiple_of(chip * span, span)
+    copies = {}
+    for slot in range(planes):
+        for comp in range(comps):
+            index = slot * comps + comp
+            copies[index] = pltpu.make_async_copy(
+                flow.at[:, comp, plane_at(slot, planes), pl.ds(first, span)],
+                near.at[index],
+                sems.at[index],
+            )
+            copies[index].start()
+    fetch = pltpu.make_async_copy(large, near_large, sems.at[planes * comps])
     fetch.start()
     for slot in range(planes):
-        column = pack_columns(flow, flat, plane_at(slot, planes))
-        for part in range(CORES):
-            start = chip * (CORES * cols) + part * cols
-            for col in range(cols):
-                own[slot][0, part, col] = column(start + col)
+        for comp in range(comps):
+            index = slot * comps + comp
+            copies[index].wait()
+            column = spread(flat, span + 1, snaps, lambda snap: near[index, snap])
+            for col in range(span):
+                own[slot][comp, col] = column(col)
     fetch.wait()
-    large_rows[...] = near[...].astype(jnp.float32)
+    rows[...] = near_large[...].astype(jnp.float32)
+    start = pl.multiple_of(first + core * cols, 8)
     for slot in range(planes):
-        for part in range(CORES):
-            start = chip * (CORES * cols) + part * cols
-            rows = large_rows[plane_at(slot, planes), pl.ds(pl.multiple_of(start, 8), cols), :]
-            if cols < extra * snaps:
-                rows = jnp.concatenate([rows] * (extra * snaps // cols), axis=0)
-            for piece in range(extra):
-                tile = rows[piece * snaps : (piece + 1) * snaps]
-                own[slot][0, part, cols + piece] = tile.astype(jnp.bfloat16)
-
-
-def pack_windows_kernel(chips, planes, cols, mine, flow, first, *refs):
+        for comp in range(comps):
+            values = rows[comp, plane_at(slot, planes), pl.ds(start, cols), :]
+            if cols % snaps:
+                values = jnp.concatenate([values] * (snaps // cols), axis=0)
+            for piece in range(values.shape[0] // snaps):
+                tile = values[piece * snaps : (piece + 1) * snaps]
+                own[slot][comp, span + piece] = tile.astype(jnp.bfloat16)
+
+
+def pack_windows_kernel(chips, planes, cols, kinds, flow, *refs):
     outs, flat = refs[:-1], refs[-1]
-    width = flow.shape[3]
+    snaps, width = flow.shape[0], flow.shape[3]
     chip, core = whereabouts()
-    part = core if mine else 1 - core
     for slot in range(planes):
-        column = pack_columns(flow, flat, plane_at(slot, planes))
-        for target, step in zip(outs, [*range(1, chips), 0]):
+        plane = plane_at(slot, planes)
+        column = spread(flat, width + 1, snaps, lambda snap: flow[snap, 0, plane])
+        for target, (mine, step) in zip(outs, kinds):
+            part = core if mine else 1 - core
             start = lax.rem(chip + step, chips) * (CORES * cols) + part * cols
             left = column(lax.rem(start - 1 + width, width))
             right = column(lax.rem(start + cols, width))
@@ -93,57 +104,55 @@
 
 def pack(flow, large, chips, cols):
     snaps, comps, planes, width, depth = flow.shape
-    extra = -(-cols // snaps)
-
-    def spec(shape):
-        tail = len(shape) - 1
-        return pl.BlockSpec((1,) + shape[1:], lambda comp: (comp,) + (0,) * tail)
-
-    def call(kernel, shapes, second, scratch, name):
-        return list(
-            pl.pallas_call(
-                kernel,
-                grid=(comps,),
-                in_specs=[
-                    pl.BlockSpec((snaps, 1, planes, width, depth), lambda comp: (0, comp, 0, 0, 0)),
-                    pl.BlockSpec(memory_space=pl.ANY),
-                ],
-                out_specs=[spec(shape) for shape in shapes],
-                out_shape=[jax.ShapeDtypeStruct(shape, flow.dtype) for shape in shapes],
-                scratch_shapes=[pltpu.VMEM((snaps * (width + 1), depth), jnp.float32)] + scratch,
-                compiler_params=pltpu.CompilerParams(vmem_limit_bytes=VMEM_BYTES),
-                name=name,
-            )(flow, second)
-        )
-
-    own = call(
+    extra, span = -(-cols // snaps), CORES * cols
+    kind = flow.dtype
+    params = pltpu.CompilerParams(vmem_limit_bytes=VMEM_BYTES)
+    own = pl.pallas_call(
         functools.partial(pack_own_kernel, planes, cols),
-        [(comps, CORES, cols + extra, snaps, depth)] * planes,
-        large,
-        [
-            pltpu.VMEM((planes, width, depth), large.dtype),
-            pltpu.VMEM((planes, width, depth), jnp.float32),
-            pltpu.SemaphoreType.DMA((1,)),
+        in_specs=[pl.BlockSpec(memory_space=pltpu.HBM)] * 2,
+        out_specs=[pl.BlockSpec(memory_space=pltpu.VMEM)] * planes,
+        out_shape=[jax.ShapeDtypeStruct((comps, span + extra, snaps, depth), kind)] * planes,
+        scratch_shapes=[
+            pltpu.VMEM((planes * comps, snaps, span, depth), kind),
+            pltpu.VMEM((snaps * (span + 1), depth), jnp.float32),
+            pltpu.VMEM(large.shape, kind),
+            pltpu.VMEM(large.shape, jnp.float32),
+            pltpu.SemaphoreType.DMA((planes * comps + 1,)),
         ],
-        "pack_own",
-    )
-    window = (comps, planes, cols + 2, snaps, depth)
-    edge = (comps, 2 * planes, snaps, depth)
-    other = call(
-        functools.partial(pack_windows_kernel, chips, planes, cols, False),
-        [window] * chips,
-        own[0],
-        [],
-        "pack_other",
-    )
-    mine = call(
-        functools.partial(pack_windows_kernel, chips, planes, cols, True),
-        [window] * (chips - 1) + [edge],
-        other[0],
-        [],
-        "pack_mine",
-    )
-    return own, mine, other
+        compiler_params=pltpu.CompilerParams(vmem_limit_bytes=PACK_BYTES),
+        name="pack_own",
+    )(flow, large)
+
+    def windows(kinds, after, name):
+        here, _ = lax.optimization_barrier((flow, after))
+
+        def shape(mine, step):
+            edge = mine and step == 0
+            return (comps, 2 * planes) if edge else (comps, planes, cols + 2)
+
+        shapes = [shape(*item) + (snaps, depth) for item in kinds]
+        specs = [
+            pl.BlockSpec((1,) + item[1:], lambda comp, tail=len(item) - 1: (comp,) + (0,) * tail)
+            for item in shapes
+        ]
+        return pl.pallas_call(
+            functools.partial(pack_windows_kernel, chips, planes, cols, kinds),
+            grid=(comps,),
+            in_specs=[
+                pl.BlockSpec((snaps, 1, planes, width, depth), lambda comp: (0, comp, 0, 0, 0)),
+            ],
+            out_specs=specs,
+            out_shape=[jax.ShapeDtypeStruct(item, kind) for item in shapes],
+            scratch_shapes=[pltpu.VMEM((snaps * (width + 1), depth), jnp.float32)],
+            compiler_params=params,
+            name=name,
+        )(here)
+
+    away = range(1, chips)
+    other = windows([(False, step) for step in away], own[0], "pack_other")
+    mine = windows([(True, step) for step in away], other[0], "pack_mine")
+    near = windows([(True, 0), (False, 0)], mine[0], "pack_near")
+    return list(own), list(other), list(mine), list(near)
 
 
 def coefficients(wide, metric, large, coef, first):
@@ -245,6 +254,7 @@
     chip, core = whereabouts()
     first = pl.multiple_of((chip * CORES + core) * cols, 8)
     middle, left, right = pl.ds(1, cols), pl.ds(0, 1), pl.ds(cols + 1, 1)
+    mine = pl.ds(core * cols, cols)
     moves = [
         (modulation, mod),
         (metric.at[:, :, pl.ds(first, cols)], metric_mine),
@@ -253,7 +263,7 @@
     for slot in range(planes):
         plane = plane_at(slot, planes) + 1
         moves += [
-            (own[slot].at[:, core, pl.ds(0, cols)], field.at[0, plane, :, middle]),
+            (own[slot].at[:, mine], field.at[0, plane, :, middle]),
             (edge.at[:, pl.ds(2 * slot, 1)], field.at[0, plane, :, left]),
             (edge.at[:, pl.ds(2 * slot + 1, 1)], field.at[0, plane, :, right]),
             (other.at[:, slot], field.at[1, plane]),
@@ -261,9 +271,9 @@
     for slot, (close, far) in enumerate(((pair, pair_other), (away, away_other))):
         halo = halo_at(slot, planes)
         moves += [
-            (close.at[:, core, pl.ds(0, cols)], field.at[0, halo, :, middle]),
-            (far.at[:, pl.ds(0, cols)], field.at[1, halo, :, middle]),
-            (close.at[:, core, pl.ds(cols, extra)], wide.at[jnp.minimum(halo, 1)]),
+            (close.at[:, mine], field.at[0, halo, :, middle]),
+            (far, field.at[1, halo, :, middle]),
+            (close.at[:, pl.ds(CORES * cols, extra)], wide.at[jnp.minimum(halo, 1)]),
         ]
     fetch_all(moves, sem.at[0])
 
@@ -297,7 +307,7 @@
     everyone, _ = modulation.shape
     comps, planes, _, depth = large.shape
     snaps = everyone // (chips * CORES)
-    extra = sources[0].shape[2] - cols
+    extra = sources[0].shape[1] - CORES * cols
     whole = pl.BlockSpec(memory_space=pltpu.VMEM)
     return pl.pallas_call(
         functools.partial(near_kernel, chips, planes),
@@ -398,6 +408,10 @@
     )(coef, amplitude, early, before, *sources)
 
 
+def product(a, b):
+    return jnp.dot(a, b, preferred_element_type=jnp.float32)
+
+
 def whiten_kernel(count, gram, *refs):
     pieces, (out, slots, sems) = refs[:-3], refs[-3:]
     everyone = gram.shape[0]
@@ -405,7 +419,9 @@
     pitch = slots.shape[1] // everyone
 
     def dot(a, b):
-        return jnp.dot(a, b, precision=lax.Precision.HIGHEST, preferred_element_type=jnp.float32)
+        (a_top, a_rest), (b_top, b_rest) = split(a), split(b)
+        cross = product(a_top, b_rest) + product(a_rest, b_top)
+        return product(a_top, b_top) + cross
 
     correlation = gram[...] / count
     frob_scale = jnp.sqrt(jnp.sum(correlation * correlation, keepdims=True) + 1e-06)
@@ -420,7 +436,8 @@
         factor = 0.5 * (diagonal - dot(inverse, approx))
         inverse = dot(factor, inverse)
     top, rest = split(inverse / jnp.sqrt(frob_scale))
-    left = jnp.concatenate([top, top, rest, rest], axis=1)
+    left = jnp.concatenate([top, rest], axis=0)
+    left = jnp.concatenate([left, left], axis=1)
     slot, copies = 0, []
     planes = sum(piece.shape[1] for piece in pieces)
     order = [1] + list(range(2, planes)) + [0]
@@ -431,11 +448,8 @@
                 for first in range(0, cols, 2):
                     both = [piece[comp, index, first], piece[comp, index, first + 1]]
                     both = jnp.concatenate(both, axis=1)
-                    mixed = jnp.dot(
-                        left,
-                        jnp.concatenate([both, both], axis=0),
-                        preferred_element_type=jnp.float32,
-                    )
+                    mixed = product(left, both)
+                    mixed = mixed[:everyone] + mixed[everyone:]
                     for sub in range(2):
                         slots[slot, pl.ds(first + sub, everyone, stride=pitch), :] = mixed[
                             :, sub * depth : (sub + 1) * depth
@@ -498,9 +512,12 @@
             continue
         stride = 1
         while stride < count:
-            pairs = [(i, i ^ stride) for i in range(count)]
-            value = value + lax.ppermute(value, axis, pairs)
-            stride *= 2
+            partners = [stride] if 2 * stride == count else [stride, 2 * stride, 3 * stride]
+            received = [
+                lax.ppermute(value, axis, [(i, i ^ k) for i in range(count)]) for k in partners
+            ]
+            value = sum(received, value)
+            stride *= 1 + len(partners)
     return value
 
 
@@ -513,10 +530,10 @@
     core = lax.rem(lax.axis_index("snap"), CORES)
 
     def half(array):
-        return lax.dynamic_index_in_dim(array, 1 - core, 1, keepdims=False)
+        return lax.dynamic_slice_in_dim(array, (1 - core) * cols, cols, 1)
 
     assert planes >= 2
-    own, mine, other = pack(flow, large_scale, chips, cols)
+    own, other, mine, near = pack(flow, large_scale, chips, cols)
     pair = to_pair(own[0], 0)
     outer, arrays = own[1], []
     for step in range(1, chips):
@@ -529,7 +546,7 @@
         arrays.append((here + [to_chip(edge, step)], to_pair(here[0], 0), to_pair(here[1], 1)))
     away = to_pair(outer, 1)
     pair, away, _ = lax.optimization_barrier((pair, away, [here[:planes] for here, *_ in arrays]))
-    sources = own + [mine[-1], to_core(other[-1]), pair, away]
+    sources = own + [near[0], to_core(near[1]), pair, away]
     sources += [to_core(half(pair)), to_core(half(away))]
     early, coef, amplitude = near_stage(modulation, metric, large_scale, sources, chips, cols)
     gram = jnp.zeros(modulation.shape[:1] * 2, jnp.float32)

time: 68.9 us -> 65.7 us (0.954)
  waiting for transfers between devices: 30.4 us -> 27.3 us
  local copies, waits for them, and re-layouts: 4.21 us -> 1.93 us
  Pallas kernels: 12.6 us -> 14.2 us
    unnamed x12 -> x14, local copies, waits for them, and re-layouts: 2.32 us -> 0.03 us
    pallas_call x3 -> x4, Pallas kernels: 2.94 us -> 5.01 us  [the longest x3 2.69 us: windows(): pl.pallas_call(functools.partial(pack_windows_kernel, chips, planes, cols...]
    ppermute x3, waiting for transfers between devices: 17.2 us -> 15.3 us  [to_chip(): return lax.ppermute(array, 'snap', pairs)]
    ppermute x5 -> x7, waiting for transfers between devices: 9.9 us -> 9.1 us  [all_sum(): lax.ppermute(value, axis, [(i, i ^ k) for i in range(count)])]
    ppermute x5 -> x7, starting transfers between devices: 8.38 us -> 8.78 us  [all_sum(): lax.ppermute(value, axis, [(i, i ^ k) for i in range(count)])]
  transfers between devices with their start and end apart: 16 -> 18, of which waited for: 9 -> 10; matrix products, arithmetic and copies ran while one was open for 3% -> 3% of each run, Pallas kernels for 6% -> 9%
where the time goes in v4:
time: 65.7 us; the launch traced here: 65.5 us
  waiting for transfers between devices  27.3 us (42%)
  starting transfers between devices  21.7 us (33%)
  Pallas kernels  14.2 us (22%)
  local copies, waits for them, and re-layouts  1.93 us (3%)
    ppermute x3, waiting for transfers between devices, to_chip(): return lax.ppermute(array, 'snap', pairs)  15.3 us
    ppermute x7, waiting for transfers between devices, all_sum(): lax.ppermute(value, axis, [(i, i ^ k) for i in range(count)])  9.1 us
    ppermute x7, starting transfers between devices, all_sum(): lax.ppermute(value, axis, [(i, i ^ k) for i in range(count)])  8.78 us
    ppermute x4, starting transfers between devices, to_pair(): return lax.ppermute(array, 'slab', pairs + [(j, i) for i, j in pairs])  8.18 us
    pallas_call x1, Pallas kernels, whiten(): pl.pallas_call(functools.partial(whiten_kernel, count), in_specs=[whole]...  3.84 us
    ppermute x3, starting transfers between devices, to_chip(): return lax.ppermute(array, 'snap', pairs)  3.58 us
    pallas_call x2, Pallas kernels, far_stage(): pl.pallas_call(functools.partial(far_kernel, chips, planes, slots, halo),...  3.07 us
    ppermute x4, waiting for transfers between devices, to_pair(): return lax.ppermute(array, 'slab', pairs + [(j, i) for i, j in pairs])  2.96 us
  transfers between devices with their start and end apart: 18, of which 10 were waited for; matrix products, arithmetic and copies ran while one was open for 3% of the time, Pallas kernels for 9%

profile of v4, /device:TPU:0, one launch (start us, length us, event | category | flops | bytes accessed | tf_op | source)
XLA Modules:
  0.0 65.5 jit_solution(14400012219353019867)
XLA Ops:
  0.0 2.3 %pack_own.1 = (bf16[3,33,16,128]{3,2,1,0:T(8,128)(2,1)}, bf16[3,33,16,128]{3,2,1,0:T(8,128)(2,1)}) custom-call(bf16[16,3,2,64,128]{4,3,2,1,0:T(8,128)(2,1)} %flow.4, bf16[3,2,64,128]{3,2,1,0:T(8,128)(2,1)} %large.3), custom_call_target="tpu_custom_call" | custom-call | tf_op jit(solution)/shard_map/pack_own/pallas_call | solution.py:110
  2.3 0.0 copy-start.1
  2.4 0.5 pack_other.1
  2.9 0.5 collective-permute-start.2
  3.5 2.8 %collective-permute-start.1 = (bf16[3,33,16,128]{3,2,1,0:T(8,128)(2,1)S(1)}, bf16[3,33,16,128]{3,2,1,0:T(8,128)(2,1)S(1)}, u32[]{:S(2)}, u32[]{:S(2)}) collective-permute-start(bf16[3,33,16,128]{3,2,1,0:T(8,128)(2,1)S(1)} %copy-done.1), channel_id=1, source_target_pairs={{0,4},{8,12},{16,20},{24,28},{4,0},{12,8},{20,16},{28,24},{1,5},{9... | collective-permute-start | bytes 1216520 | tf_op jit(solution)/shard_map/ppermute | solution.py:504
  6.3 0.5 pack_mine.1
  6.8 0.0 collective-permute-done.2
  6.8 0.1 pad_maximum_fusion
  6.9 0.0 copy-start.6
  6.9 0.7 %collective-permute-start.3 = (bf16[3,33,16,128]{3,2,1,0:T(8,128)(2,1)S(1)}, bf16[3,33,16,128]{3,2,1,0:T(8,128)(2,1)S(1)}, u32[]{:S(2)}, u32[]{:S(2)}) collective-permute-start(bf16[3,33,16,128]{3,2,1,0:T(8,128)(2,1)S(1)} %copy-done.2), channel_id=1, source_target_pairs={{4,8},{12,16},{20,24},{8,4},{16,12},{24,20},{5,9},{13,17},{21,25},... | collective-permute-start | bytes 1216520 | tf_op jit(solution)/shard_map/ppermute | solution.py:504
  7.6 1.0 %slice_bitcast_fusion = (bf16[3,16,32,128]{3,2,1,0:T(8,128)(2,1)}, bf16[3,16,32,128]{3,2,1,0:T(8,128)(2,1)}) fusion(bf16[3,2,18,32,128]{4,3,2,0,1:T(8,128)(2,1)S(1)} %pad_maximum_fusion), kind=kLoop, calls=%fused_computation.1 | loop fusion | bytes 1572864 | tf_op jit(solution)/shard_map/squeeze | solution.py:542
  8.6 1.5 %collective-permute-start.5 = (bf16[3,16,32,128]{3,2,1,0:T(8,128)(2,1)}, bf16[3,16,32,128]{3,2,1,0:T(8,128)(2,1)S(1)}, u32[]{:S(2)}, u32[]{:S(2)}) collective-permute-start(bf16[3,16,32,128]{3,2,1,0:T(8,128)(2,1)} %get-tuple-element.45), channel_id=1, source_target_pairs={{0,2},{1,3},{2,0},{3,1},{4,6},{5,7},{6,4},{7,5},{8,10},{9,11},{10,... | collective-permute-start | bytes 1179656 | tf_op jit(solution)/shard_map/ppermute | solution.py:494
  10.1 0.5 collective-permute-start.4
  10.7 1.6 %pack_near.1 = (bf16[3,4,16,128]{3,2,1,0:T(8,128)(2,1)S(1)}, bf16[3,2,18,16,128]{4,3,2,1,0:T(8,128)(2,1)}) custom-call(bf16[16,3,2,64,128]{4,3,2,1,0:T(8,128)(2,1)S(1)} %copy-done), custom_call_target="tpu_custom_call" | custom-call | tf_op jit(solution)/shard_map/pack_near/pallas_call | solution.py:138
  12.3 0.0 collective-permute-start
  12.3 0.8 %fusion = (bf16[3,2,1,32,128]{4,3,2,0,1:T(8,128)(2,1)S(1)}, bf16[3,2,1,32,128]{4,3,2,0,1:T(8,128)(2,1)S(1)}) fusion(bf16[3,2,18,32,128]{4,3,2,0,1:T(8,128)(2,1)} %copy-done.6), kind=kLoop, calls=%fused_computation.8 | loop fusion | bytes 196608 | tf_op jit(solution)/shard_map/slice | solution.py:543
  13.1 7.7 %collective-permute-done.5.refs_1_ = bf16[3,16,32,128]{3,2,1,0:T(8,128)(2,1)S(1)} collective-permute-done((bf16[3,16,32,128]{3,2,1,0:T(8,128)(2,1)}, bf16[3,16,32,128]{3,2,1,0:T(8,128)(2,1)S(1)}, u32[]{:S(2)}, u32[]{:S(2)}) %collective-permute-start.5) | collective-permute-done | bytes 393248 | tf_op jit(solution)/shard_map/ppermute | solution.py:494
  20.8 0.7 %collective-permute-start.9 = (bf16[3,16,32,128]{3,2,1,0:T(8,128)(2,1)S(1)}, bf16[3,16,32,128]{3,2,1,0:T(8,128)(2,1)S(1)}, u32[]{:S(2)}, u32[]{:S(2)}) collective-permute-start(bf16[3,16,32,128]{3,2,1,0:T(8,128)(2,1)S(1)} %collective-permute-done.5.refs_1_), channel_id=1, source_target_pairs={{4,8},{12,16},{20,24},{8,4},{16,12},{24,20},{5,9},{13,17},{21,25},... | collective-permute-start | bytes 1179656 | tf_op jit(solution)/shard_map/ppermute | solution.py:504
  21.5 6.7 %collective-permute-done.4.refs_0_ = bf16[3,16,32,128]{3,2,1,0:T(8,128)(2,1)S(1)} collective-permute-done((bf16[3,16,32,128]{3,2,1,0:T(8,128)(2,1)}, bf16[3,16,32,128]{3,2,1,0:T(8,128)(2,1)S(1)}, u32[]{:S(2)}, u32[]{:S(2)}) %collective-permute-start.4) | collective-permute-done | bytes 393248 | tf_op jit(solution)/shard_map/ppermute | solution.py:494
  28.2 4.0 %collective-permute-start.10 = (bf16[3,16,32,128]{3,2,1,0:T(8,128)(2,1)S(1)}, bf16[3,16,32,128]{3,2,1,0:T(8,128)(2,1)S(1)}, u32[]{:S(2)}, u32[]{:S(2)}) collective-permute-start(bf16[3,16,32,128]{3,2,1,0:T(8,128)(2,1)S(1)} %collective-permute-done.4.refs_0_), channel_id=1, source_target_pairs={{0,4},{8,12},{16,20},{24,28},{4,0},{12,8},{20,16},{28,24},{1,5},{9... | collective-permute-start | bytes 1179656 | tf_op jit(solution)/shard_map/ppermute | solution.py:504
  32.2 0.0 collective-permute-done.1.refs_4_
  32.2 0.0 collective-permute-done.3.refs_5_
  32.2 0.1 collective-permute-start.7
  32.3 0.5 collective-permute-start.6
  32.9 0.0 collective-permute-done.refs_3_
  32.9 1.6 %collective-permute-start.8 = (bf16[3,4,32,128]{3,2,1,0:T(8,128)(2,1)S(1)}, bf16[3,4,32,128]{3,2,1,0:T(8,128)(2,1)S(1)}, u32[]{:S(2)}, u32[]{:S(2)}) collective-permute-start(bf16[3,4,32,128]{3,2,1,0:T(8,128)(2,1)S(1)} %bitcast.5), channel_id=1, source_target_pairs={{0,2},{1,3},{2,0},{3,1},{4,6},{5,7},{6,4},{7,5},{8,10},{9,11},{10,... | collective-permute-start | bytes 294920 | tf_op jit(solution)/shard_map/ppermute | solution.py:494
  34.4 0.0 collective-permute-done.7.refs_7_
  34.5 0.0 collective-permute-done.6.refs_6_
  34.5 2.3 %near_stage.1 = (bf16[3,2,16,2,2,16,128]{6,5,4,3,2,1,0:T(8,128)(2,1)S(1)}, f32[2,11,16,128]{3,2,1,0:T(8,128)S(1)}, f32[18,64,128]{2,1,0:T(8,128)S(1)}) custom-call(f32[64,64]{1,0:T(8,128)S(1)} %copy-done.5, f32[4,2,64,128]{3,2,1,0:T(8,128)S(1)} %copy-done.4, bf16[3,2,64,128]{3,2,1,0:T(8,128)(2,1)S(1)} %copy-done.3, bf16[3,33,16,128]{3,2,1,0:T(8,128)(2,1)S(1)} %copy-done.1, ...), custom_call_target="tpu_custom_call" | custom-call | bytes 8388608 | tf_op jit(solution)/shard_map/near_stage/pallas_call | solution.py:312
  36.8 0.9 %collective-permute-done.8.refs_2_ = bf16[3,4,32,128]{3,2,1,0:T(8,128)(2,1)S(1)} collective-permute-done((bf16[3,4,32,128]{3,2,1,0:T(8,128)(2,1)S(1)}, bf16[3,4,32,128]{3,2,1,0:T(8,128)(2,1)S(1)}, u32[]{:S(2)}, u32[]{:S(2)}) %collective-permute-start.8) | collective-permute-done | bytes 98336 | tf_op jit(solution)/shard_map/ppermute | solution.py:494
  37.7 0.0 collective-permute-done.9.refs_3_
  37.7 1.5 %far_stage.2 = (bf16[3,1,16,128,128]{4,3,2,1,0:T(8,128)(2,1)S(1)}, f32[64,64]{1,0:T(8,128)S(1)}) custom-call(f32[2,11,16,128]{3,2,1,0:T(8,128)S(1)} %get-tuple-element.35.coef, f32[18,64,128]{2,1,0:T(8,128)S(1)} %get-tuple-element.36.amplitude, bf16[3,2,16,2,2,16,128]{6,5,4,3,2,1,0:T(8,128)(2,1)S(1)} %get-tuple-element.37.early, ...), custom_call_target="tpu_custom_call" | custom-call | bytes 8388608 | tf_op jit(solution)/shard_map/far_stage/pallas_call | solution.py:390
  39.3 3.0 %collective-permute-done.10.refs_3_ = bf16[3,16,32,128]{3,2,1,0:T(8,128)(2,1)S(1)} collective-permute-done((bf16[3,16,32,128]{3,2,1,0:T(8,128)(2,1)S(1)}, bf16[3,16,32,128]{3,2,1,0:T(8,128)(2,1)S(1)}, u32[]{:S(2)}, u32[]{:S(2)}) %collective-permute-start.10) | collective-permute-done | bytes 393248 | tf_op jit(solution)/shard_map/ppermute | solution.py:504
  42.2 1.5 %far_stage.3 = (bf16[3,1,16,128,128]{4,3,2,1,0:T(8,128)(2,1)S(1)}, f32[64,64]{1,0:T(8,128)S(1)}) custom-call(f32[2,11,16,128]{3,2,1,0:T(8,128)S(1)} %get-tuple-element.35.coef, f32[18,64,128]{2,1,0:T(8,128)S(1)} %get-tuple-element.36.amplitude, bf16[3,2,16,2,2,16,128]{6,5,4,3,2,1,0:T(8,128)(2,1)S(1)} %get-tuple-element.37.early, ...), custom_call_target="tpu_custom_call" | custom-call | bytes 8388608 | tf_op jit(solution)/shard_map/far_stage/pallas_call | solution.py:390
  43.7 1.2 %collective-permute-start.13 = (f32[64,64]{1,0:T(8,128)S(1)}, f32[64,64]{1,0:T(8,128)S(1)}, u32[]{:S(2)}, u32[]{:S(2)}) collective-permute-start(f32[64,64]{1,0:T(8,128)S(1)} %get-tuple-element.40), channel_id=1, source_target_pairs={{0,3},{1,2},{2,1},{3,0},{4,7},{5,6},{6,5},{7,4},{8,11},{9,10},{10,... | collective-permute-start | bytes 49160 | tf_op jit(solution)/shard_map/ppermute | solution.py:517
  44.9 0.5 collective-permute-start.12
  45.4 0.2 collective-permute-start.11
  45.7 1.6 %collective-permute-done.13 = f32[64,64]{1,0:T(8,128)S(1)} collective-permute-done((f32[64,64]{1,0:T(8,128)S(1)}, f32[64,64]{1,0:T(8,128)S(1)}, u32[]{:S(2)}, u32[]{:S(2)}) %collective-permute-start.13) | collective-permute-done | bytes 16416 | tf_op jit(solution)/shard_map/ppermute | solution.py:517
  47.3 1.5 %collective-permute-done.12 = f32[64,64]{1,0:T(8,128)S(1)} collective-permute-done((f32[64,64]{1,0:T(8,128)S(1)}, f32[64,64]{1,0:T(8,128)S(1)}, u32[]{:S(2)}, u32[]{:S(2)}) %collective-permute-start.12) | collective-permute-done | bytes 16416 | tf_op jit(solution)/shard_map/ppermute | solution.py:517
  48.8 3.6 %collective-permute-start.16 = (f32[64,64]{1,0:T(8,128)S(1)}, f32[64,64]{1,0:T(8,128)S(1)}, u32[]{:S(2)}, u32[]{:S(2)}) collective-permute-start(f32[64,64]{1,0:T(8,128)S(1)} %add_add_fusion.1), channel_id=1, source_target_pairs={{0,12},{4,8},{8,4},{12,0},{16,28},{20,24},{24,20},{28,16},{1,13},{... | collective-permute-start | bytes 49160 | tf_op jit(solution)/shard_map/ppermute | solution.py:517
  52.4 0.4 collective-permute-start.15
  52.8 0.2 collective-permute-start.14
  53.0 1.6 %collective-permute-done.16 = f32[64,64]{1,0:T(8,128)S(1)} collective-permute-done((f32[64,64]{1,0:T(8,128)S(1)}, f32[64,64]{1,0:T(8,128)S(1)}, u32[]{:S(2)}, u32[]{:S(2)}) %collective-permute-start.16) | collective-permute-done | bytes 16416 | tf_op jit(solution)/shard_map/ppermute | solution.py:517
  54.6 1.7 %collective-permute-done.15 = f32[64,64]{1,0:T(8,128)S(1)} collective-permute-done((f32[64,64]{1,0:T(8,128)S(1)}, f32[64,64]{1,0:T(8,128)S(1)}, u32[]{:S(2)}, u32[]{:S(2)}) %collective-permute-start.15) | collective-permute-done | bytes 16416 | tf_op jit(solution)/shard_map/ppermute | solution.py:517
  56.3 0.4 collective-permute-done.14
  56.8 2.7 %collective-permute-start.17 = (f32[64,64]{1,0:T(8,128)S(1)}, f32[64,64]{1,0:T(8,128)S(1)}, u32[]{:S(2)}, u32[]{:S(2)}) collective-permute-start(f32[64,64]{1,0:T(8,128)S(1)} %add_add_fusion), channel_id=1, source_target_pairs={{0,16},{4,20},{8,24},{12,28},{16,0},{20,4},{24,8},{28,12},{1,17},{... | collective-permute-start | bytes 49160 | tf_op jit(solution)/shard_map/ppermute | solution.py:517
  59.4 2.2 %collective-permute-done.17 = f32[64,64]{1,0:T(8,128)S(1)} collective-permute-done((f32[64,64]{1,0:T(8,128)S(1)}, f32[64,64]{1,0:T(8,128)S(1)}, u32[]{:S(2)}, u32[]{:S(2)}) %collective-permute-start.17) | collective-permute-done | bytes 16416 | tf_op jit(solution)/shard_map/ppermute | solution.py:517
  61.7 3.8 %whiten.1 = f32[64,3,2,16,128]{4,3,2,1,0:T(8,128)} custom-call(f32[64,64]{1,0:T(8,128)S(1)} %add.32.gram, bf16[3,1,16,128,128]{4,3,2,1,0:T(8,128)(2,1)S(1)} %get-tuple-element.41.refs_0_, bf16[3,1,16,128,128]{4,3,2,1,0:T(8,128)(2,1)S(1)} %get-tuple-element.42.refs_1_), custom_call_target="tpu_custom_call" | custom-call | tf_op jit(solution)/shard_map/whiten/pallas_call | solution.py:477
  (22 shorter events, 0.1 us)
Async XLA Ops:
  0.0 2.4 %copy-start = (bf16[16,3,2,64,128]{4,3,2,1,0:T(8,128)(2,1)S(1)}, bf16[16,3,2,64,128]{4,3,2,1,0:T(8,128)(2,1)}, u32[]{:S(2)}) copy-start(bf16[16,3,2,64,128]{4,3,2,1,0:T(8,128)(2,1)} %flow.4) | copy-start | bytes 4718596
  2.3 1.1 %copy-start.1 = (bf16[3,33,16,128]{3,2,1,0:T(8,128)(2,1)S(1)}, bf16[3,33,16,128]{3,2,1,0:T(8,128)(2,1)}, u32[]{:S(2)}) copy-start(bf16[3,33,16,128]{3,2,1,0:T(8,128)(2,1)} %get-tuple-element.24.refs_0_) | copy-start | bytes 1216516
  2.9 4.0 %copy-start.2 = (bf16[3,33,16,128]{3,2,1,0:T(8,128)(2,1)S(1)}, bf16[3,33,16,128]{3,2,1,0:T(8,128)(2,1)}, u32[]{:S(2)}) copy-start(bf16[3,33,16,128]{3,2,1,0:T(8,128)(2,1)} %get-tuple-element.31.refs_1_) | copy-start | bytes 1216516
  2.9 3.9 %collective-permute-start.2 = (bf16[3,2,18,16,128]{4,3,2,0,1:T(8,128)(2,1)S(1)}, bf16[3,2,18,16,128]{4,3,2,0,1:T(8,128)(2,1)S(1)}, u32[]{:S(2)}, u32[]{:S(2)}) collective-permute-start(bf16[3,2,18,16,128]{4,3,2,0,1:T(8,128)(2,1)S(1)} %copy.7), channel_id=1, source_target_pairs={{0,1},{1,0},{2,3},{3,2},{4,5},{5,4},{6,7},{7,6},{8,9},{9,8},{10,11... | collective-permute-start | bytes 1327112 | tf_op jit(solution)/shard_map/ppermute | solution.py:498
  3.5 28.7 %collective-permute-start.1 = (bf16[3,33,16,128]{3,2,1,0:T(8,128)(2,1)S(1)}, bf16[3,33,16,128]{3,2,1,0:T(8,128)(2,1)S(1)}, u32[]{:S(2)}, u32[]{:S(2)}) collective-permute-start(bf16[3,33,16,128]{3,2,1,0:T(8,128)(2,1)S(1)} %copy-done.1), channel_id=1, source_target_pairs={{0,4},{8,12},{16,20},{24,28},{4,0},{12,8},{20,16},{28,24},{1,5},{9... | collective-permute-start | bytes 1216520 | tf_op jit(solution)/shard_map/ppermute | solution.py:504
  6.9 3.2 %copy-start.6 = (bf16[3,2,18,32,128]{4,3,2,0,1:T(8,128)(2,1)}, bf16[3,2,18,32,128]{4,3,2,0,1:T(8,128)(2,1)S(1)}, u32[]{:S(2)}) copy-start(bf16[3,2,18,32,128]{4,3,2,0,1:T(8,128)(2,1)S(1)} %pad_maximum_fusion) | copy-start | bytes 2654212
  6.9 25.2 %collective-permute-start.3 = (bf16[3,33,16,128]{3,2,1,0:T(8,128)(2,1)S(1)}, bf16[3,33,16,128]{3,2,1,0:T(8,128)(2,1)S(1)}, u32[]{:S(2)}, u32[]{:S(2)}) collective-permute-start(bf16[3,33,16,128]{3,2,1,0:T(8,128)(2,1)S(1)} %copy-done.2), channel_id=1, source_target_pairs={{4,8},{12,16},{20,24},{8,4},{16,12},{24,20},{5,9},{13,17},{21,25},... | collective-permute-start | bytes 1216520 | tf_op jit(solution)/shard_map/ppermute | solution.py:504
  8.6 25.8 %copy-start.3 = (bf16[3,2,64,128]{3,2,1,0:T(8,128)(2,1)S(1)}, bf16[3,2,64,128]{3,2,1,0:T(8,128)(2,1)}, u32[]{:S(2)}) copy-start(bf16[3,2,64,128]{3,2,1,0:T(8,128)(2,1)} %large.3) | copy-start | bytes 294916
  8.6 25.8 %copy-start.4 = (f32[4,2,64,128]{3,2,1,0:T(8,128)S(1)}, f32[4,2,64,128]{3,2,1,0:T(8,128)}, u32[]{:S(2)}) copy-start(f32[4,2,64,128]{3,2,1,0:T(8,128)} %metric.1) | copy-start | bytes 786436
  8.6 25.8 %copy-start.5 = (f32[64,64]{1,0:T(8,128)S(1)}, f32[64,64]{1,0:T(8,128)}, u32[]{:S(2)}) copy-start(f32[64,64]{1,0:T(8,128)} %modulation.1) | copy-start | bytes 49156
  8.6 12.2 %collective-permute-start.5 = (bf16[3,16,32,128]{3,2,1,0:T(8,128)(2,1)}, bf16[3,16,32,128]{3,2,1,0:T(8,128)(2,1)S(1)}, u32[]{:S(2)}, u32[]{:S(2)}) collective-permute-start(bf16[3,16,32,128]{3,2,1,0:T(8,128)(2,1)} %get-tuple-element.45), channel_id=1, source_target_pairs={{0,2},{1,3},{2,0},{3,1},{4,6},{5,7},{6,4},{7,5},{8,10},{9,11},{10,... | collective-permute-start | bytes 1179656 | tf_op jit(solution)/shard_map/ppermute | solution.py:494
  10.1 18.1 %collective-permute-start.4 = (bf16[3,16,32,128]{3,2,1,0:T(8,128)(2,1)}, bf16[3,16,32,128]{3,2,1,0:T(8,128)(2,1)S(1)}, u32[]{:S(2)}, u32[]{:S(2)}) collective-permute-start(bf16[3,16,32,128]{3,2,1,0:T(8,128)(2,1)} %get-tuple-element.46), channel_id=1, source_target_pairs={{0,2},{1,3},{2,0},{3,1},{4,6},{5,7},{6,4},{7,5},{8,10},{9,11},{10,... | collective-permute-start | bytes 1179656 | tf_op jit(solution)/shard_map/ppermute | solution.py:494
  12.3 20.6 %collective-permute-start = (bf16[3,2,18,16,128]{4,3,2,1,0:T(8,128)(2,1)}, bf16[3,2,18,16,128]{4,3,2,1,0:T(8,128)(2,1)S(1)}, u32[]{:S(2)}, u32[]{:S(2)}) collective-permute-start(bf16[3,2,18,16,128]{4,3,2,1,0:T(8,128)(2,1)} %get-tuple-element.30), channel_id=1, source_target_pairs={{0,1},{1,0},{2,3},{3,2},{4,5},{5,4},{6,7},{7,6},{8,9},{9,8},{10,11... | collective-permute-start | bytes 1327112 | tf_op jit(solution)/shard_map/ppermute | solution.py:498
  20.8 16.9 %collective-permute-start.9 = (bf16[3,16,32,128]{3,2,1,0:T(8,128)(2,1)S(1)}, bf16[3,16,32,128]{3,2,1,0:T(8,128)(2,1)S(1)}, u32[]{:S(2)}, u32[]{:S(2)}) collective-permute-start(bf16[3,16,32,128]{3,2,1,0:T(8,128)(2,1)S(1)} %collective-permute-done.5.refs_1_), channel_id=1, source_target_pairs={{4,8},{12,16},{20,24},{8,4},{16,12},{24,20},{5,9},{13,17},{21,25},... | collective-permute-start | bytes 1179656 | tf_op jit(solution)/shard_map/ppermute | solution.py:504
  28.2 14.0 %collective-permute-start.10 = (bf16[3,16,32,128]{3,2,1,0:T(8,128)(2,1)S(1)}, bf16[3,16,32,128]{3,2,1,0:T(8,128)(2,1)S(1)}, u32[]{:S(2)}, u32[]{:S(2)}) collective-permute-start(bf16[3,16,32,128]{3,2,1,0:T(8,128)(2,1)S(1)} %collective-permute-done.4.refs_0_), channel_id=1, source_target_pairs={{0,4},{8,12},{16,20},{24,28},{4,0},{12,8},{20,16},{28,24},{1,5},{9... | collective-permute-start | bytes 1179656 | tf_op jit(solution)/shard_map/ppermute | solution.py:504
  32.2 2.3 %collective-permute-start.7 = (bf16[3,16,16,128]{3,2,1,0:T(8,128)(2,1)S(1)}, bf16[3,16,16,128]{3,2,1,0:T(8,128)(2,1)S(1)}, u32[]{:S(2)}, u32[]{:S(2)}) collective-permute-start(bf16[3,16,16,128]{3,2,1,0:T(8,128)(2,1)S(1)} %constant_dynamic-slice_fusion), channel_id=1, source_target_pairs={{0,1},{1,0},{2,3},{3,2},{4,5},{5,4},{6,7},{7,6},{8,9},{9,8},{10,11... | collective-permute-start | bytes 589832 | tf_op jit(solution)/shard_map/ppermute | solution.py:498
  32.3 2.1 %collective-permute-start.6 = (bf16[3,16,16,128]{3,2,1,0:T(8,128)(2,1)S(1)}, bf16[3,16,16,128]{3,2,1,0:T(8,128)(2,1)S(1)}, u32[]{:S(2)}, u32[]{:S(2)}) collective-permute-start(bf16[3,16,16,128]{3,2,1,0:T(8,128)(2,1)S(1)} %constant_dynamic-slice_fusion.1), channel_id=1, source_target_pairs={{0,1},{1,0},{2,3},{3,2},{4,5},{5,4},{6,7},{7,6},{8,9},{9,8},{10,11... | collective-permute-start | bytes 589832 | tf_op jit(solution)/shard_map/ppermute | solution.py:498
  32.9 4.8 %collective-permute-start.8 = (bf16[3,4,32,128]{3,2,1,0:T(8,128)(2,1)S(1)}, bf16[3,4,32,128]{3,2,1,0:T(8,128)(2,1)S(1)}, u32[]{:S(2)}, u32[]{:S(2)}) collective-permute-start(bf16[3,4,32,128]{3,2,1,0:T(8,128)(2,1)S(1)} %bitcast.5), channel_id=1, source_target_pairs={{0,2},{1,3},{2,0},{3,1},{4,6},{5,7},{6,4},{7,5},{8,10},{9,11},{10,... | collective-permute-start | bytes 294920 | tf_op jit(solution)/shard_map/ppermute | solution.py:494
  43.7 3.6 %collective-permute-start.13 = (f32[64,64]{1,0:T(8,128)S(1)}, f32[64,64]{1,0:T(8,128)S(1)}, u32[]{:S(2)}, u32[]{:S(2)}) collective-permute-start(f32[64,64]{1,0:T(8,128)S(1)} %get-tuple-element.40), channel_id=1, source_target_pairs={{0,3},{1,2},{2,1},{3,0},{4,7},{5,6},{6,5},{7,4},{8,11},{9,10},{10,... | collective-permute-start | bytes 49160 | tf_op jit(solution)/shard_map/ppermute | solution.py:517
  44.9 3.9 %collective-permute-start.12 = (f32[64,64]{1,0:T(8,128)S(1)}, f32[64,64]{1,0:T(8,128)S(1)}, u32[]{:S(2)}, u32[]{:S(2)}) collective-permute-start(f32[64,64]{1,0:T(8,128)S(1)} %get-tuple-element.40), channel_id=1, source_target_pairs={{0,2},{1,3},{2,0},{3,1},{4,6},{5,7},{6,4},{7,5},{8,10},{9,11},{10,... | collective-permute-start | bytes 49160 | tf_op jit(solution)/shard_map/ppermute | solution.py:517
  45.4 3.4 %collective-permute-start.11 = (f32[64,64]{1,0:T(8,128)S(1)}, f32[64,64]{1,0:T(8,128)S(1)}, u32[]{:S(2)}, u32[]{:S(2)}) collective-permute-start(f32[64,64]{1,0:T(8,128)S(1)} %get-tuple-element.40), channel_id=1, source_target_pairs={{0,1},{1,0},{2,3},{3,2},{4,5},{5,4},{6,7},{7,6},{8,9},{9,8},{10,11... | collective-permute-start | bytes 49160 | tf_op jit(solution)/shard_map/ppermute | solution.py:517
  48.8 5.8 %collective-permute-start.16 = (f32[64,64]{1,0:T(8,128)S(1)}, f32[64,64]{1,0:T(8,128)S(1)}, u32[]{:S(2)}, u32[]{:S(2)}) collective-permute-start(f32[64,64]{1,0:T(8,128)S(1)} %add_add_fusion.1), channel_id=1, source_target_pairs={{0,12},{4,8},{8,4},{12,0},{16,28},{20,24},{24,20},{28,16},{1,13},{... | collective-permute-start | bytes 49160 | tf_op jit(solution)/shard_map/ppermute | solution.py:517
  52.4 3.9 %collective-permute-start.15 = (f32[64,64]{1,0:T(8,128)S(1)}, f32[64,64]{1,0:T(8,128)S(1)}, u32[]{:S(2)}, u32[]{:S(2)}) collective-permute-start(f32[64,64]{1,0:T(8,128)S(1)} %add_add_fusion.1), channel_id=1, source_target_pairs={{0,8},{4,12},{8,0},{12,4},{16,24},{20,28},{24,16},{28,20},{1,9},{5... | collective-permute-start | bytes 49160 | tf_op jit(solution)/shard_map/ppermute | solution.py:517
  52.8 3.9 %collective-permute-start.14 = (f32[64,64]{1,0:T(8,128)S(1)}, f32[64,64]{1,0:T(8,128)S(1)}, u32[]{:S(2)}, u32[]{:S(2)}) collective-permute-start(f32[64,64]{1,0:T(8,128)S(1)} %add_add_fusion.1), channel_id=1, source_target_pairs={{0,4},{4,0},{8,12},{12,8},{16,20},{20,16},{24,28},{28,24},{1,5},{5... | collective-permute-start | bytes 49160 | tf_op jit(solution)/shard_map/ppermute | solution.py:517
  56.8 4.9 %collective-permute-start.17 = (f32[64,64]{1,0:T(8,128)S(1)}, f32[64,64]{1,0:T(8,128)S(1)}, u32[]{:S(2)}, u32[]{:S(2)}) collective-permute-start(f32[64,64]{1,0:T(8,128)S(1)} %add_add_fusion), channel_id=1, source_target_pairs={{0,16},{4,20},{8,24},{12,28},{16,0},{20,4},{24,8},{28,12},{1,17},{... | collective-permute-start | bytes 49160 | tf_op jit(solution)/shard_map/ppermute | solution.py:517

commit v5 on v4

--- a/solution.py
+++ b/solution.py
@@ -10,7 +10,6 @@
 NSITER = 6
 CORES = 2
 VMEM_BYTES = 16 * 1024 * 1024
-PACK_BYTES = 58 * 1024 * 1024
 
 
 def whereabouts():
@@ -107,24 +106,8 @@
     extra, span = -(-cols // snaps), CORES * cols
     kind = flow.dtype
     params = pltpu.CompilerParams(vmem_limit_bytes=VMEM_BYTES)
-    own = pl.pallas_call(
-        functools.partial(pack_own_kernel, planes, cols),
-        in_specs=[pl.BlockSpec(memory_space=pltpu.HBM)] * 2,
-        out_specs=[pl.BlockSpec(memory_space=pltpu.VMEM)] * planes,
-        out_shape=[jax.ShapeDtypeStruct((comps, span + extra, snaps, depth), kind)] * planes,
-        scratch_shapes=[
-            pltpu.VMEM((planes * comps, snaps, span, depth), kind),
-            pltpu.VMEM((snaps * (span + 1), depth), jnp.float32),
-            pltpu.VMEM(large.shape, kind),
-            pltpu.VMEM(large.shape, jnp.float32),
-            pltpu.SemaphoreType.DMA((planes * comps + 1,)),
-        ],
-        compiler_params=pltpu.CompilerParams(vmem_limit_bytes=PACK_BYTES),
-        name="pack_own",
-    )(flow, large)
-
     def windows(kinds, after, name):
-        here, _ = lax.optimization_barrier((flow, after))
+        here = flow if after is None else lax.optimization_barrier((flow, after))[0]
 
         def shape(mine, step):
             edge = mine and step == 0
@@ -149,8 +132,24 @@
         )(here)
 
     away = range(1, chips)
-    other = windows([(False, step) for step in away], own[0], "pack_other")
-    mine = windows([(True, step) for step in away], other[0], "pack_mine")
+    other = windows([(False, step) for step in away], None, "pack_other")
+    lengths = [span + extra + 2] + [span + extra] * (planes - 1)
+    own = pl.pallas_call(
+        functools.partial(pack_own_kernel, planes, cols),
+        in_specs=[pl.BlockSpec(memory_space=pltpu.HBM)] * 2,
+        out_specs=[pl.BlockSpec(memory_space=pltpu.VMEM)] * planes,
+        out_shape=[jax.ShapeDtypeStruct((comps, item, snaps, depth), kind) for item in lengths],
+        scratch_shapes=[
+            pltpu.VMEM((planes * comps, snaps, span, depth), kind),
+            pltpu.VMEM((snaps * (span + 1), depth), jnp.float32),
+            pltpu.VMEM(large.shape, kind),
+            pltpu.VMEM(large.shape, jnp.float32),
+            pltpu.SemaphoreType.DMA((planes * comps + 1,)),
+        ],
+        compiler_params=pltpu.CompilerParams(vmem_limit_bytes=VMEM_BYTES),
+        name="pack_own",
+    )(lax.optimization_barrier((flow, other[0]))[0], large)
+    mine = windows([(True, step) for step in away], own[0], "pack_mine")
     near = windows([(True, 0), (False, 0)], mine[0], "pack_near")
     return list(own), list(other), list(mine), list(near)
 
@@ -307,7 +306,7 @@
     everyone, _ = modulation.shape
     comps, planes, _, depth = large.shape
     snaps = everyone // (chips * CORES)
-    extra = sources[0].shape[1] - CORES * cols
+    extra = sources[1].shape[1] - CORES * cols
     whole = pl.BlockSpec(memory_space=pltpu.VMEM)
     return pl.pallas_call(
         functools.partial(near_kernel, chips, planes),
@@ -376,10 +375,13 @@
                 total[...] += lax.dot_general(
                     both, both, (((1,), (1,)), ((), ())), preferred_element_type=jnp.float32
                 )
-    gram[...] = before[...] + (
+    whole = (
         total[:everyone, :everyone]
         + total[everyone:, everyone:]
         + (total[:everyone, everyone:] + total[everyone:, :everyone])
+    )
+    gram[...] = before[...] + jnp.concatenate(
+        [whole[: everyone // 2], whole[everyone // 2 :]], axis=1
     )
 
 
@@ -393,7 +395,7 @@
         out_specs=[whole, whole],
         out_shape=[
             jax.ShapeDtypeStruct((comps, len(slots), cols, 2 * everyone, depth), jnp.bfloat16),
-            jax.ShapeDtypeStruct((everyone, everyone), jnp.float32),
+            jax.ShapeDtypeStruct((everyone // 2, 2 * everyone), jnp.float32),
         ],
         scratch_shapes=[
             pltpu.VMEM(
@@ -414,7 +416,7 @@
 
 def whiten_kernel(count, gram, *refs):
     pieces, (out, slots, sems) = refs[:-3], refs[-3:]
-    everyone = gram.shape[0]
+    everyone = 2 * gram.shape[0]
     comps, cols, depth = pieces[0].shape[0], pieces[0].shape[2], pieces[0].shape[4]
     pitch = slots.shape[1] // everyone
 
@@ -423,7 +425,7 @@
         cross = product(a_top, b_rest) + product(a_rest, b_top)
         return product(a_top, b_top) + cross
 
-    correlation = gram[...] / count
+    correlation = jnp.concatenate([gram[:, :everyone], gram[:, everyone:]], axis=0) / count
     frob_scale = jnp.sqrt(jnp.sum(correlation * correlation, keepdims=True) + 1e-06)
     approx = correlation / frob_scale
     row = lax.broadcasted_iota(jnp.int32, (everyone, everyone), 0)
@@ -469,7 +471,7 @@
 
 
 def whiten(gram, pieces, count):
-    everyone = gram.shape[0]
+    everyone = 2 * gram.shape[0]
     comps, _, cols, _, depth = pieces[0].shape
     planes = sum(piece.shape[1] for piece in pieces)
     pitch = cols + 8 if (cols // 8) % 2 == 0 else cols
@@ -549,7 +551,8 @@
     sources = own + [near[0], to_core(near[1]), pair, away]
     sources += [to_core(half(pair)), to_core(half(away))]
     early, coef, amplitude = near_stage(modulation, metric, large_scale, sources, chips, cols)
-    gram = jnp.zeros(modulation.shape[:1] * 2, jnp.float32)
+    everyone = modulation.shape[0]
+    gram = jnp.zeros((everyone // 2, 2 * everyone), jnp.float32)
     pieces = []
     for slots, halo in (((1,) + tuple(range(2, planes)), 1), ((0,), 0)):
         sources = []

time: 65.7 us -> 65 us (0.989)
  Pallas kernels: 14.2 us -> 12.6 us
  local copies, waits for them, and re-layouts: 1.93 us -> 3.3 us
    pallas_call x1, Pallas kernels: 2.33 us -> 0.55 us  [pack(): pl.pallas_call(functools.partial(pack_own_kernel, planes, cols), in_specs...]
    unnamed x14 -> x10, local copies, waits for them, and re-layouts: 0.03 us -> 1.42 us
  transfers between devices with their start and end apart: 18 -> 18, of which waited for: 10 -> 10; matrix products, arithmetic and copies ran while one was open for 3% -> 3% of each run, Pallas kernels for 9% -> 10%
where the time goes in v5:
time: 65 us; the launch traced here: 64.7 us
  waiting for transfers between devices  26.9 us (41%)
  starting transfers between devices  21.6 us (33%)
  Pallas kernels  12.6 us (19%)
  local copies, waits for them, and re-layouts  3.3 us (5%)
    ppermute x3, waiting for transfers between devices, to_chip(): return lax.ppermute(array, 'snap', pairs)  15.3 us
    ppermute x7, starting transfers between devices, all_sum(): lax.ppermute(value, axis, [(i, i ^ k) for i in range(count)])  8.72 us
    ppermute x7, waiting for transfers between devices, all_sum(): lax.ppermute(value, axis, [(i, i ^ k) for i in range(count)])  8.57 us
    ppermute x4, starting transfers between devices, to_pair(): return lax.ppermute(array, 'slab', pairs + [(j, i) for i, j in pairs])  8.18 us
    pallas_call x1, Pallas kernels, whiten(): pl.pallas_call(functools.partial(whiten_kernel, count), in_specs=[whole]...  3.89 us
    ppermute x3, starting transfers between devices, to_chip(): return lax.ppermute(array, 'snap', pairs)  3.58 us
    pallas_call x2, Pallas kernels, far_stage(): pl.pallas_call(functools.partial(far_kernel, chips, planes, slots, halo),...  3.2 us
    ppermute x4, waiting for transfers between devices, to_pair(): return lax.ppermute(array, 'slab', pairs + [(j, i) for i, j in pairs])  2.98 us
  transfers between devices with their start and end apart: 18, of which 10 were waited for; matrix products, arithmetic and copies ran while one was open for 3% of the time, Pallas kernels for 10%

profile of v5, /device:TPU:0, one launch (start us, length us, event | category | flops | bytes accessed | tf_op | source)
XLA Modules:
  0.0 64.7 jit_solution(17094933021062459239)
XLA Ops:
  0.0 1.4 %copy-done = bf16[16,3,2,64,128]{4,3,2,1,0:T(8,128)(2,1)S(1)} copy-done((bf16[16,3,2,64,128]{4,3,2,1,0:T(8,128)(2,1)S(1)}, bf16[16,3,2,64,128]{4,3,2,1,0:T(8,128)(2,1)}, u32[]{:S(2)}) %copy-start) | copy-done | bytes 1572888
  1.4 0.5 pack_other.1
  2.0 0.5 collective-permute-start.2
  2.5 0.6 pack_own.1
  3.1 2.8 %collective-permute-start.1 = (bf16[3,35,16,128]{3,2,1,0:T(8,128)(2,1)S(1)}, bf16[3,35,16,128]{3,2,1,0:T(8,128)(2,1)S(1)}, u32[]{:S(2)}, u32[]{:S(2)}) collective-permute-start(bf16[3,35,16,128]{3,2,1,0:T(8,128)(2,1)S(1)} %get-tuple-element.25.refs_0_), channel_id=1, source_target_pairs={{0,4},{8,12},{16,20},{24,28},{4,0},{12,8},{20,16},{28,24},{1,5},{9... | collective-permute-start | bytes 1290248 | tf_op jit(solution)/shard_map/ppermute | solution.py:506
  5.9 0.5 pack_mine.1
  6.4 0.0 collective-permute-done.2
  6.4 0.1 pad_maximum_fusion
  6.5 0.0 copy-start.4
  6.5 0.7 %collective-permute-start.3 = (bf16[3,33,16,128]{3,2,1,0:T(8,128)(2,1)S(1)}, bf16[3,33,16,128]{3,2,1,0:T(8,128)(2,1)S(1)}, u32[]{:S(2)}, u32[]{:S(2)}) collective-permute-start(bf16[3,33,16,128]{3,2,1,0:T(8,128)(2,1)S(1)} %get-tuple-element.31.refs_1_), channel_id=1, source_target_pairs={{4,8},{12,16},{20,24},{8,4},{16,12},{24,20},{5,9},{13,17},{21,25},... | collective-permute-start | bytes 1216520 | tf_op jit(solution)/shard_map/ppermute | solution.py:506
  7.2 1.0 %slice_bitcast_fusion = (bf16[3,16,32,128]{3,2,1,0:T(8,128)(2,1)}, bf16[3,16,32,128]{3,2,1,0:T(8,128)(2,1)}) fusion(bf16[3,2,18,32,128]{4,3,2,0,1:T(8,128)(2,1)S(1)} %pad_maximum_fusion), kind=kLoop, calls=%fused_computation.1 | loop fusion | bytes 1572864 | tf_op jit(solution)/shard_map/squeeze | solution.py:544
  8.2 1.5 %collective-permute-start.5 = (bf16[3,16,32,128]{3,2,1,0:T(8,128)(2,1)}, bf16[3,16,32,128]{3,2,1,0:T(8,128)(2,1)S(1)}, u32[]{:S(2)}, u32[]{:S(2)}) collective-permute-start(bf16[3,16,32,128]{3,2,1,0:T(8,128)(2,1)} %get-tuple-element.45), channel_id=1, source_target_pairs={{0,2},{1,3},{2,0},{3,1},{4,6},{5,7},{6,4},{7,5},{8,10},{9,11},{10,... | collective-permute-start | bytes 1179656 | tf_op jit(solution)/shard_map/ppermute | solution.py:496
  9.7 0.5 collective-permute-start.4
  10.2 1.7 %pack_near.1 = (bf16[3,4,16,128]{3,2,1,0:T(8,128)(2,1)S(1)}, bf16[3,2,18,16,128]{4,3,2,1,0:T(8,128)(2,1)}) custom-call(bf16[16,3,2,64,128]{4,3,2,1,0:T(8,128)(2,1)S(1)} %copy-done), custom_call_target="tpu_custom_call" | custom-call | tf_op jit(solution)/shard_map/pack_near/pallas_call | solution.py:121
  11.9 0.0 collective-permute-start
  11.9 0.8 %fusion = (bf16[3,2,1,32,128]{4,3,2,0,1:T(8,128)(2,1)S(1)}, bf16[3,2,1,32,128]{4,3,2,0,1:T(8,128)(2,1)S(1)}) fusion(bf16[3,2,18,32,128]{4,3,2,0,1:T(8,128)(2,1)} %copy-done.4), kind=kLoop, calls=%fused_computation.8 | loop fusion | bytes 196608 | tf_op jit(solution)/shard_map/slice | solution.py:545
  12.7 7.7 %collective-permute-done.5.refs_1_ = bf16[3,16,32,128]{3,2,1,0:T(8,128)(2,1)S(1)} collective-permute-done((bf16[3,16,32,128]{3,2,1,0:T(8,128)(2,1)}, bf16[3,16,32,128]{3,2,1,0:T(8,128)(2,1)S(1)}, u32[]{:S(2)}, u32[]{:S(2)}) %collective-permute-start.5) | collective-permute-done | bytes 393248 | tf_op jit(solution)/shard_map/ppermute | solution.py:496
  20.4 0.7 %collective-permute-start.9 = (bf16[3,16,32,128]{3,2,1,0:T(8,128)(2,1)S(1)}, bf16[3,16,32,128]{3,2,1,0:T(8,128)(2,1)S(1)}, u32[]{:S(2)}, u32[]{:S(2)}) collective-permute-start(bf16[3,16,32,128]{3,2,1,0:T(8,128)(2,1)S(1)} %collective-permute-done.5.refs_1_), channel_id=1, source_target_pairs={{4,8},{12,16},{20,24},{8,4},{16,12},{24,20},{5,9},{13,17},{21,25},... | collective-permute-start | bytes 1179656 | tf_op jit(solution)/shard_map/ppermute | solution.py:506
  21.1 6.7 %collective-permute-done.4.refs_0_ = bf16[3,16,32,128]{3,2,1,0:T(8,128)(2,1)S(1)} collective-permute-done((bf16[3,16,32,128]{3,2,1,0:T(8,128)(2,1)}, bf16[3,16,32,128]{3,2,1,0:T(8,128)(2,1)S(1)}, u32[]{:S(2)}, u32[]{:S(2)}) %collective-permute-start.4) | collective-permute-done | bytes 393248 | tf_op jit(solution)/shard_map/ppermute | solution.py:496
  27.8 4.0 %collective-permute-start.10 = (bf16[3,16,32,128]{3,2,1,0:T(8,128)(2,1)S(1)}, bf16[3,16,32,128]{3,2,1,0:T(8,128)(2,1)S(1)}, u32[]{:S(2)}, u32[]{:S(2)}) collective-permute-start(bf16[3,16,32,128]{3,2,1,0:T(8,128)(2,1)S(1)} %collective-permute-done.4.refs_0_), channel_id=1, source_target_pairs={{0,4},{8,12},{16,20},{24,28},{4,0},{12,8},{20,16},{28,24},{1,5},{9... | collective-permute-start | bytes 1179656 | tf_op jit(solution)/shard_map/ppermute | solution.py:506
  31.8 0.0 collective-permute-done.1.refs_4_
  31.8 0.0 collective-permute-done.3.refs_5_
  31.8 0.1 collective-permute-start.7
  31.9 0.5 collective-permute-start.6
  32.5 1.6 %collective-permute-start.8 = (bf16[3,4,32,128]{3,2,1,0:T(8,128)(2,1)S(1)}, bf16[3,4,32,128]{3,2,1,0:T(8,128)(2,1)S(1)}, u32[]{:S(2)}, u32[]{:S(2)}) collective-permute-start(bf16[3,4,32,128]{3,2,1,0:T(8,128)(2,1)S(1)} %bitcast.5), channel_id=1, source_target_pairs={{0,2},{1,3},{2,0},{3,1},{4,6},{5,7},{6,4},{7,5},{8,10},{9,11},{10,... | collective-permute-start | bytes 294920 | tf_op jit(solution)/shard_map/ppermute | solution.py:496
  34.1 0.0 collective-permute-done.7.refs_7_
  34.1 0.0 collective-permute-done.6.refs_6_
  34.1 2.3 %near_stage.1 = (bf16[3,2,16,2,2,16,128]{6,5,4,3,2,1,0:T(8,128)(2,1)S(1)}, f32[2,11,16,128]{3,2,1,0:T(8,128)S(1)}, f32[18,64,128]{2,1,0:T(8,128)S(1)}) custom-call(f32[64,64]{1,0:T(8,128)S(1)} %copy-done.3, f32[4,2,64,128]{3,2,1,0:T(8,128)S(1)} %copy-done.2, bf16[3,2,64,128]{3,2,1,0:T(8,128)(2,1)S(1)} %copy-done.1, ...), custom_call_target="tpu_custom_call" | custom-call | bytes 8388608 | tf_op jit(solution)/shard_map/near_stage/pallas_call | solution.py:311
  36.4 0.9 %collective-permute-done.8.refs_2_ = bf16[3,4,32,128]{3,2,1,0:T(8,128)(2,1)S(1)} collective-permute-done((bf16[3,4,32,128]{3,2,1,0:T(8,128)(2,1)S(1)}, bf16[3,4,32,128]{3,2,1,0:T(8,128)(2,1)S(1)}, u32[]{:S(2)}, u32[]{:S(2)}) %collective-permute-start.8) | collective-permute-done | bytes 98336 | tf_op jit(solution)/shard_map/ppermute | solution.py:496
  37.3 0.0 collective-permute-done.9.refs_3_
  37.3 1.6 %far_stage.2 = (bf16[3,1,16,128,128]{4,3,2,1,0:T(8,128)(2,1)S(1)}, f32[32,128]{1,0:T(8,128)S(1)}) custom-call(f32[2,11,16,128]{3,2,1,0:T(8,128)S(1)} %get-tuple-element.35.coef, f32[18,64,128]{2,1,0:T(8,128)S(1)} %get-tuple-element.36.amplitude, bf16[3,2,16,2,2,16,128]{6,5,4,3,2,1,0:T(8,128)(2,1)S(1)} %get-tuple-element.37.early, ...), custom_call_target="tpu_custom_call" | custom-call | bytes 8388608 | tf_op jit(solution)/shard_map/far_stage/pallas_call | solution.py:392
  38.9 3.0 %collective-permute-done.10.refs_3_ = bf16[3,16,32,128]{3,2,1,0:T(8,128)(2,1)S(1)} collective-permute-done((bf16[3,16,32,128]{3,2,1,0:T(8,128)(2,1)S(1)}, bf16[3,16,32,128]{3,2,1,0:T(8,128)(2,1)S(1)}, u32[]{:S(2)}, u32[]{:S(2)}) %collective-permute-start.10) | collective-permute-done | bytes 393248 | tf_op jit(solution)/shard_map/ppermute | solution.py:506
  41.9 1.6 %far_stage.3 = (bf16[3,1,16,128,128]{4,3,2,1,0:T(8,128)(2,1)S(1)}, f32[32,128]{1,0:T(8,128)S(1)}) custom-call(f32[2,11,16,128]{3,2,1,0:T(8,128)S(1)} %get-tuple-element.35.coef, f32[18,64,128]{2,1,0:T(8,128)S(1)} %get-tuple-element.36.amplitude, bf16[3,2,16,2,2,16,128]{6,5,4,3,2,1,0:T(8,128)(2,1)S(1)} %get-tuple-element.37.early, ...), custom_call_target="tpu_custom_call" | custom-call | bytes 8388608 | tf_op jit(solution)/shard_map/far_stage/pallas_call | solution.py:392
  43.5 1.2 %collective-permute-start.13 = (f32[32,128]{1,0:T(8,128)S(1)}, f32[32,128]{1,0:T(8,128)S(1)}, u32[]{:S(2)}, u32[]{:S(2)}) collective-permute-start(f32[32,128]{1,0:T(8,128)S(1)} %get-tuple-element.40), channel_id=1, source_target_pairs={{0,3},{1,2},{2,1},{3,0},{4,7},{5,6},{6,5},{7,4},{8,11},{9,10},{10,... | collective-permute-start | bytes 49160 | tf_op jit(solution)/shard_map/ppermute | solution.py:519
  44.7 0.5 collective-permute-start.12
  45.2 0.2 collective-permute-start.11
  45.4 1.3 %collective-permute-done.13 = f32[32,128]{1,0:T(8,128)S(1)} collective-permute-done((f32[32,128]{1,0:T(8,128)S(1)}, f32[32,128]{1,0:T(8,128)S(1)}, u32[]{:S(2)}, u32[]{:S(2)}) %collective-permute-start.13) | collective-permute-done | bytes 16416 | tf_op jit(solution)/shard_map/ppermute | solution.py:519
  46.7 1.7 %collective-permute-done.12 = f32[32,128]{1,0:T(8,128)S(1)} collective-permute-done((f32[32,128]{1,0:T(8,128)S(1)}, f32[32,128]{1,0:T(8,128)S(1)}, u32[]{:S(2)}, u32[]{:S(2)}) %collective-permute-start.12) | collective-permute-done | bytes 16416 | tf_op jit(solution)/shard_map/ppermute | solution.py:519
  48.4 0.0 collective-permute-done.11
  48.4 3.6 %collective-permute-start.16 = (f32[32,128]{1,0:T(8,128)S(1)}, f32[32,128]{1,0:T(8,128)S(1)}, u32[]{:S(2)}, u32[]{:S(2)}) collective-permute-start(f32[32,128]{1,0:T(8,128)S(1)} %add_add_fusion.1), channel_id=1, source_target_pairs={{0,12},{4,8},{8,4},{12,0},{16,28},{20,24},{24,20},{28,16},{1,13},{... | collective-permute-start | bytes 49160 | tf_op jit(solution)/shard_map/ppermute | solution.py:519
  52.0 0.4 collective-permute-start.15
  52.4 0.2 collective-permute-start.14
  52.6 1.1 %collective-permute-done.16 = f32[32,128]{1,0:T(8,128)S(1)} collective-permute-done((f32[32,128]{1,0:T(8,128)S(1)}, f32[32,128]{1,0:T(8,128)S(1)}, u32[]{:S(2)}, u32[]{:S(2)}) %collective-permute-start.16) | collective-permute-done | bytes 16416 | tf_op jit(solution)/shard_map/ppermute | solution.py:519
  53.7 2.0 %collective-permute-done.15 = f32[32,128]{1,0:T(8,128)S(1)} collective-permute-done((f32[32,128]{1,0:T(8,128)S(1)}, f32[32,128]{1,0:T(8,128)S(1)}, u32[]{:S(2)}, u32[]{:S(2)}) %collective-permute-start.15) | collective-permute-done | bytes 16416 | tf_op jit(solution)/shard_map/ppermute | solution.py:519
  55.7 0.4 collective-permute-done.14
  56.2 2.6 %collective-permute-start.17 = (f32[32,128]{1,0:T(8,128)S(1)}, f32[32,128]{1,0:T(8,128)S(1)}, u32[]{:S(2)}, u32[]{:S(2)}) collective-permute-start(f32[32,128]{1,0:T(8,128)S(1)} %add_add_fusion), channel_id=1, source_target_pairs={{0,16},{4,20},{8,24},{12,28},{16,0},{20,4},{24,8},{28,12},{1,17},{... | collective-permute-start | bytes 49160 | tf_op jit(solution)/shard_map/ppermute | solution.py:519
  58.8 2.0 %collective-permute-done.17 = f32[32,128]{1,0:T(8,128)S(1)} collective-permute-done((f32[32,128]{1,0:T(8,128)S(1)}, f32[32,128]{1,0:T(8,128)S(1)}, u32[]{:S(2)}, u32[]{:S(2)}) %collective-permute-start.17) | collective-permute-done | bytes 16416 | tf_op jit(solution)/shard_map/ppermute | solution.py:519
  60.8 3.9 %whiten.1 = f32[64,3,2,16,128]{4,3,2,1,0:T(8,128)} custom-call(f32[32,128]{1,0:T(8,128)S(1)} %add.35.gram, bf16[3,1,16,128,128]{4,3,2,1,0:T(8,128)(2,1)S(1)} %get-tuple-element.41.refs_0_, bf16[3,1,16,128,128]{4,3,2,1,0:T(8,128)(2,1)S(1)} %get-tuple-element.42.refs_1_), custom_call_target="tpu_custom_call" | custom-call | tf_op jit(solution)/shard_map/whiten/pallas_call | solution.py:479
  (18 shorter events, 0.1 us)
Async XLA Ops:
  0.0 1.4 %copy-start = (bf16[16,3,2,64,128]{4,3,2,1,0:T(8,128)(2,1)S(1)}, bf16[16,3,2,64,128]{4,3,2,1,0:T(8,128)(2,1)}, u32[]{:S(2)}) copy-start(bf16[16,3,2,64,128]{4,3,2,1,0:T(8,128)(2,1)} %flow.4) | copy-start | bytes 4718596
  1.4 1.1 %copy-start.1 = (bf16[3,2,64,128]{3,2,1,0:T(8,128)(2,1)S(1)}, bf16[3,2,64,128]{3,2,1,0:T(8,128)(2,1)}, u32[]{:S(2)}) copy-start(bf16[3,2,64,128]{3,2,1,0:T(8,128)(2,1)} %large.3) | copy-start | bytes 294916
  2.0 4.4 %collective-permute-start.2 = (bf16[3,2,18,16,128]{4,3,2,0,1:T(8,128)(2,1)S(1)}, bf16[3,2,18,16,128]{4,3,2,0,1:T(8,128)(2,1)S(1)}, u32[]{:S(2)}, u32[]{:S(2)}) collective-permute-start(bf16[3,2,18,16,128]{4,3,2,0,1:T(8,128)(2,1)S(1)} %copy.7), channel_id=1, source_target_pairs={{0,1},{1,0},{2,3},{3,2},{4,5},{5,4},{6,7},{7,6},{8,9},{9,8},{10,11... | collective-permute-start | bytes 1327112 | tf_op jit(solution)/shard_map/ppermute | solution.py:500
  3.1 28.7 %collective-permute-start.1 = (bf16[3,35,16,128]{3,2,1,0:T(8,128)(2,1)S(1)}, bf16[3,35,16,128]{3,2,1,0:T(8,128)(2,1)S(1)}, u32[]{:S(2)}, u32[]{:S(2)}) collective-permute-start(bf16[3,35,16,128]{3,2,1,0:T(8,128)(2,1)S(1)} %get-tuple-element.25.refs_0_), channel_id=1, source_target_pairs={{0,4},{8,12},{16,20},{24,28},{4,0},{12,8},{20,16},{28,24},{1,5},{9... | collective-permute-start | bytes 1290248 | tf_op jit(solution)/shard_map/ppermute | solution.py:506
  6.5 3.2 %copy-start.4 = (bf16[3,2,18,32,128]{4,3,2,0,1:T(8,128)(2,1)}, bf16[3,2,18,32,128]{4,3,2,0,1:T(8,128)(2,1)S(1)}, u32[]{:S(2)}) copy-start(bf16[3,2,18,32,128]{4,3,2,0,1:T(8,128)(2,1)S(1)} %pad_maximum_fusion) | copy-start | bytes 2654212
  6.5 25.3 %collective-permute-start.3 = (bf16[3,33,16,128]{3,2,1,0:T(8,128)(2,1)S(1)}, bf16[3,33,16,128]{3,2,1,0:T(8,128)(2,1)S(1)}, u32[]{:S(2)}, u32[]{:S(2)}) collective-permute-start(bf16[3,33,16,128]{3,2,1,0:T(8,128)(2,1)S(1)} %get-tuple-element.31.refs_1_), channel_id=1, source_target_pairs={{4,8},{12,16},{20,24},{8,4},{16,12},{24,20},{5,9},{13,17},{21,25},... | collective-permute-start | bytes 1216520 | tf_op jit(solution)/shard_map/ppermute | solution.py:506
  8.2 25.9 %copy-start.2 = (f32[4,2,64,128]{3,2,1,0:T(8,128)S(1)}, f32[4,2,64,128]{3,2,1,0:T(8,128)}, u32[]{:S(2)}) copy-start(f32[4,2,64,128]{3,2,1,0:T(8,128)} %metric.1) | copy-start | bytes 786436
  8.2 25.9 %copy-start.3 = (f32[64,64]{1,0:T(8,128)S(1)}, f32[64,64]{1,0:T(8,128)}, u32[]{:S(2)}) copy-start(f32[64,64]{1,0:T(8,128)} %modulation.1) | copy-start | bytes 49156
  8.2 12.2 %collective-permute-start.5 = (bf16[3,16,32,128]{3,2,1,0:T(8,128)(2,1)}, bf16[3,16,32,128]{3,2,1,0:T(8,128)(2,1)S(1)}, u32[]{:S(2)}, u32[]{:S(2)}) collective-permute-start(bf16[3,16,32,128]{3,2,1,0:T(8,128)(2,1)} %get-tuple-element.45), channel_id=1, source_target_pairs={{0,2},{1,3},{2,0},{3,1},{4,6},{5,7},{6,4},{7,5},{8,10},{9,11},{10,... | collective-permute-start | bytes 1179656 | tf_op jit(solution)/shard_map/ppermute | solution.py:496
  9.7 18.1 %collective-permute-start.4 = (bf16[3,16,32,128]{3,2,1,0:T(8,128)(2,1)}, bf16[3,16,32,128]{3,2,1,0:T(8,128)(2,1)S(1)}, u32[]{:S(2)}, u32[]{:S(2)}) collective-permute-start(bf16[3,16,32,128]{3,2,1,0:T(8,128)(2,1)} %get-tuple-element.46), channel_id=1, source_target_pairs={{0,2},{1,3},{2,0},{3,1},{4,6},{5,7},{6,4},{7,5},{8,10},{9,11},{10,... | collective-permute-start | bytes 1179656 | tf_op jit(solution)/shard_map/ppermute | solution.py:496
  11.9 20.6 %collective-permute-start = (bf16[3,2,18,16,128]{4,3,2,1,0:T(8,128)(2,1)}, bf16[3,2,18,16,128]{4,3,2,1,0:T(8,128)(2,1)S(1)}, u32[]{:S(2)}, u32[]{:S(2)}) collective-permute-start(bf16[3,2,18,16,128]{4,3,2,1,0:T(8,128)(2,1)} %get-tuple-element.30), channel_id=1, source_target_pairs={{0,1},{1,0},{2,3},{3,2},{4,5},{5,4},{6,7},{7,6},{8,9},{9,8},{10,11... | collective-permute-start | bytes 1327112 | tf_op jit(solution)/shard_map/ppermute | solution.py:500
  20.4 16.9 %collective-permute-start.9 = (bf16[3,16,32,128]{3,2,1,0:T(8,128)(2,1)S(1)}, bf16[3,16,32,128]{3,2,1,0:T(8,128)(2,1)S(1)}, u32[]{:S(2)}, u32[]{:S(2)}) collective-permute-start(bf16[3,16,32,128]{3,2,1,0:T(8,128)(2,1)S(1)} %collective-permute-done.5.refs_1_), channel_id=1, source_target_pairs={{4,8},{12,16},{20,24},{8,4},{16,12},{24,20},{5,9},{13,17},{21,25},... | collective-permute-start | bytes 1179656 | tf_op jit(solution)/shard_map/ppermute | solution.py:506
  27.8 14.1 %collective-permute-start.10 = (bf16[3,16,32,128]{3,2,1,0:T(8,128)(2,1)S(1)}, bf16[3,16,32,128]{3,2,1,0:T(8,128)(2,1)S(1)}, u32[]{:S(2)}, u32[]{:S(2)}) collective-permute-start(bf16[3,16,32,128]{3,2,1,0:T(8,128)(2,1)S(1)} %collective-permute-done.4.refs_0_), channel_id=1, source_target_pairs={{0,4},{8,12},{16,20},{24,28},{4,0},{12,8},{20,16},{28,24},{1,5},{9... | collective-permute-start | bytes 1179656 | tf_op jit(solution)/shard_map/ppermute | solution.py:506
  31.8 2.3 %collective-permute-start.7 = (bf16[3,16,16,128]{3,2,1,0:T(8,128)(2,1)S(1)}, bf16[3,16,16,128]{3,2,1,0:T(8,128)(2,1)S(1)}, u32[]{:S(2)}, u32[]{:S(2)}) collective-permute-start(bf16[3,16,16,128]{3,2,1,0:T(8,128)(2,1)S(1)} %constant_dynamic-slice_fusion), channel_id=1, source_target_pairs={{0,1},{1,0},{2,3},{3,2},{4,5},{5,4},{6,7},{7,6},{8,9},{9,8},{10,11... | collective-permute-start | bytes 589832 | tf_op jit(solution)/shard_map/ppermute | solution.py:500
  31.9 2.1 %collective-permute-start.6 = (bf16[3,16,16,128]{3,2,1,0:T(8,128)(2,1)S(1)}, bf16[3,16,16,128]{3,2,1,0:T(8,128)(2,1)S(1)}, u32[]{:S(2)}, u32[]{:S(2)}) collective-permute-start(bf16[3,16,16,128]{3,2,1,0:T(8,128)(2,1)S(1)} %constant_dynamic-slice_fusion.1), channel_id=1, source_target_pairs={{0,1},{1,0},{2,3},{3,2},{4,5},{5,4},{6,7},{7,6},{8,9},{9,8},{10,11... | collective-permute-start | bytes 589832 | tf_op jit(solution)/shard_map/ppermute | solution.py:500
  32.5 4.8 %collective-permute-start.8 = (bf16[3,4,32,128]{3,2,1,0:T(8,128)(2,1)S(1)}, bf16[3,4,32,128]{3,2,1,0:T(8,128)(2,1)S(1)}, u32[]{:S(2)}, u32[]{:S(2)}) collective-permute-start(bf16[3,4,32,128]{3,2,1,0:T(8,128)(2,1)S(1)} %bitcast.5), channel_id=1, source_target_pairs={{0,2},{1,3},{2,0},{3,1},{4,6},{5,7},{6,4},{7,5},{8,10},{9,11},{10,... | collective-permute-start | bytes 294920 | tf_op jit(solution)/shard_map/ppermute | solution.py:496
  43.5 3.2 %collective-permute-start.13 = (f32[32,128]{1,0:T(8,128)S(1)}, f32[32,128]{1,0:T(8,128)S(1)}, u32[]{:S(2)}, u32[]{:S(2)}) collective-permute-start(f32[32,128]{1,0:T(8,128)S(1)} %get-tuple-element.40), channel_id=1, source_target_pairs={{0,3},{1,2},{2,1},{3,0},{4,7},{5,6},{6,5},{7,4},{8,11},{9,10},{10,... | collective-permute-start | bytes 49160 | tf_op jit(solution)/shard_map/ppermute | solution.py:519
  44.7 3.7 %collective-permute-start.12 = (f32[32,128]{1,0:T(8,128)S(1)}, f32[32,128]{1,0:T(8,128)S(1)}, u32[]{:S(2)}, u32[]{:S(2)}) collective-permute-start(f32[32,128]{1,0:T(8,128)S(1)} %get-tuple-element.40), channel_id=1, source_target_pairs={{0,2},{1,3},{2,0},{3,1},{4,6},{5,7},{6,4},{7,5},{8,10},{9,11},{10,... | collective-permute-start | bytes 49160 | tf_op jit(solution)/shard_map/ppermute | solution.py:519
  45.2 3.2 %collective-permute-start.11 = (f32[32,128]{1,0:T(8,128)S(1)}, f32[32,128]{1,0:T(8,128)S(1)}, u32[]{:S(2)}, u32[]{:S(2)}) collective-permute-start(f32[32,128]{1,0:T(8,128)S(1)} %get-tuple-element.40), channel_id=1, source_target_pairs={{0,1},{1,0},{2,3},{3,2},{4,5},{5,4},{6,7},{7,6},{8,9},{9,8},{10,11... | collective-permute-start | bytes 49160 | tf_op jit(solution)/shard_map/ppermute | solution.py:519
  48.4 5.3 %collective-permute-start.16 = (f32[32,128]{1,0:T(8,128)S(1)}, f32[32,128]{1,0:T(8,128)S(1)}, u32[]{:S(2)}, u32[]{:S(2)}) collective-permute-start(f32[32,128]{1,0:T(8,128)S(1)} %add_add_fusion.1), channel_id=1, source_target_pairs={{0,12},{4,8},{8,4},{12,0},{16,28},{20,24},{24,20},{28,16},{1,13},{... | collective-permute-start | bytes 49160 | tf_op jit(solution)/shard_map/ppermute | solution.py:519
  52.0 3.7 %collective-permute-start.15 = (f32[32,128]{1,0:T(8,128)S(1)}, f32[32,128]{1,0:T(8,128)S(1)}, u32[]{:S(2)}, u32[]{:S(2)}) collective-permute-start(f32[32,128]{1,0:T(8,128)S(1)} %add_add_fusion.1), channel_id=1, source_target_pairs={{0,8},{4,12},{8,0},{12,4},{16,24},{20,28},{24,16},{28,20},{1,9},{5... | collective-permute-start | bytes 49160 | tf_op jit(solution)/shard_map/ppermute | solution.py:519
  52.4 3.7 %collective-permute-start.14 = (f32[32,128]{1,0:T(8,128)S(1)}, f32[32,128]{1,0:T(8,128)S(1)}, u32[]{:S(2)}, u32[]{:S(2)}) collective-permute-start(f32[32,128]{1,0:T(8,128)S(1)} %add_add_fusion.1), channel_id=1, source_target_pairs={{0,4},{4,0},{8,12},{12,8},{16,20},{20,16},{24,28},{28,24},{1,5},{5... | collective-permute-start | bytes 49160 | tf_op jit(solution)/shard_map/ppermute | solution.py:519
  56.2 4.6 %collective-permute-start.17 = (f32[32,128]{1,0:T(8,128)S(1)}, f32[32,128]{1,0:T(8,128)S(1)}, u32[]{:S(2)}, u32[]{:S(2)}) collective-permute-start(f32[32,128]{1,0:T(8,128)S(1)} %add_add_fusion), channel_id=1, source_target_pairs={{0,16},{4,20},{8,24},{12,28},{16,0},{20,4},{24,8},{28,12},{1,17},{... | collective-permute-start | bytes 49160 | tf_op jit(solution)/shard_map/ppermute | solution.py:519

commit v6 on v5

--- a/solution.py
+++ b/solution.py
@@ -197,13 +197,17 @@
     return pltpu.roll(values, depth - 1, 1) - pltpu.roll(values, 1, 1)
 
 
-def curl(get, row, mods, plane, col):
+def curl(get, row, mods, plane, col, inner=None):
     def value(comp, plane_at, col_at):
         return get(comp, plane_at, col_at).astype(jnp.float32)
 
     gx, shear, gy, gz, ax, ay, az, v_after, v_before, w_after, w_before = row
     mod_before, mod_here, mod_after = mods
-    dy_u, dy_v, dy_w = [value(k, plane + 1, col) - value(k, plane - 1, col) for k in range(3)]
+    if inner is None:
+        steps = [value(k, plane + 1, col) - value(k, plane - 1, col) for k in range(3)]
+    else:
+        steps = [-value(k, inner, col) for k in range(3)]
+    dy_u, dy_v, dy_w = steps
     dz_u, dz_v = [along_z(value(k, plane, col)) for k in range(2)]
     dx_v, dx_w = [value(k, plane, col + 1) - value(k, plane, col - 1) for k in (1, 2)]
     around_x = gy * dy_w - gz * dz_v + mod_here * ax
@@ -229,20 +233,29 @@
     return pl.multiple_of(owner * snaps, snaps)
 
 
-def curls(chips, field, steps, coef, amplitude, plane, cols, snaps, store):
-    depth = amplitude.shape[2]
+def metric_rows(coef, plane, col, indices, snaps):
+    depth = coef.shape[3]
+    return [
+        jnp.broadcast_to(coef[plane, index, pl.ds(col, 1), :], (snaps, depth)) for index in indices
+    ]
+
+
+def curls(chips, field, steps, coef, amplitude, plane, cols, snaps, store, upper=None):
     for col in range(cols):
-        row = [
-            jnp.broadcast_to(coef[plane, index, pl.ds(col, 1), :], (snaps, depth))
-            for index in range(11)
-        ]
+        row = metric_rows(coef, plane, col, range(11), snaps)
+        inner = None
+        if upper is not None:
+            sign = (1 - 2 * upper).astype(jnp.float32)
+            row[1], row[2] = row[1] * sign, row[2] * sign
+            inner = plane + 2 * upper
         for step in steps:
             for part in range(CORES):
                 start = rows_of(chips, step, part, snaps)
                 mods = [amplitude[col + k, pl.ds(start, snaps), :] for k in range(3)]
                 get = functools.partial(field, step, part)
-                for comp, value in enumerate(curl(get, row, mods, plane + 1, col + 1)):
-                    store(comp, col, step, part, start, split(value))
+                values = curl(get, row, mods, plane + 1, col + 1, inner)
+                for comp, value in enumerate(values):
+                    store(comp, col, step, part, start, value)
 
 
 def near_kernel(chips, planes, modulation, metric, large, *refs):
@@ -287,9 +300,9 @@
 
     for slot in range(planes):
 
-        def store(comp, col, step, part, start, halves):
-            for level in range(2):
-                early[comp, slot, col, level, part] = halves[level]
+        def store(comp, col, step, part, start, value):
+            for level, half in enumerate(split(value)):
+                early[comp, slot, col, level, part] = half
 
         curls(chips, tile, [0], coef, amplitude, plane_at(slot, planes), cols, snaps, store)
 
@@ -331,10 +344,45 @@
     )(modulation, metric, large, *sources)
 
 
-def far_kernel(chips, planes, slots, halo, coef, amplitude, early, before, *refs):
-    sources, (parts, gram, field, total, sem) = list(refs[:-5]), refs[-5:]
+def put(parts, index, comp, col, start, halves):
+    everyone = parts.shape[3] // 2
+    for level, half in enumerate(halves):
+        rows = pl.ds(start + level * everyone, half.shape[0])
+        parts[comp, index, col, rows, :] = half
+
+
+def put_early(chips, early, slot, parts, index):
     cols, snaps = early.shape[2], early.shape[5]
-    everyone = amplitude.shape[1]
+    for part in range(CORES):
+        start = rows_of(chips, 0, part, snaps)
+        for comp in range(3):
+            for col in range(cols):
+                halves = [early[comp, slot, col, level, part] for level in range(2)]
+                put(parts, index, comp, col, start, halves)
+
+
+def add_products(parts, index, total):
+    for comp in range(3):
+        columns = [parts[comp, index, col] for col in range(parts.shape[2])]
+        both = jnp.concatenate(columns, axis=1)
+        total[...] += lax.dot_general(
+            both,
+            both[: total.shape[1]],
+            (((1,), (1,)), ((), ())),
+            preferred_element_type=jnp.float32,
+        )
+
+
+def folded(total):
+    everyone = total.shape[1]
+    cross = total[everyone:]
+    whole = total[:everyone] + (cross + cross.T)
+    return jnp.concatenate([whole[: everyone // 2], whole[everyone // 2 :]], axis=1)
+
+
+def far_kernel(chips, planes, coef, amplitude, early, *refs):
+    sources, (parts, gram, base, field, total, sem) = list(refs[:-6]), refs[-6:]
+    cols, snaps = early.shape[2], early.shape[5]
     middle, left, right = pl.ds(1, cols), pl.ds(0, 1), pl.ds(cols + 1, 1)
     moves = []
     for step in range(1, chips):
@@ -347,67 +395,107 @@
                 (edge.at[:, pl.ds(2 * slot, 1)], target.at[:, left]),
                 (edge.at[:, pl.ds(2 * slot + 1, 1)], target.at[:, right]),
             ]
-        moves.append((beyond, field.at[step - 1, halo_at(halo, planes), :, middle]))
+        moves.append((beyond, field.at[step - 1, halo_at(1, planes), :, middle]))
     fetch_all(moves, sem.at[0])
 
     def tile(step, part, comp, plane, col):
         return field[step - 1, plane, comp, col, part * snaps : (part + 1) * snaps]
 
     total[...] = jnp.zeros_like(total)
-    for index, slot in enumerate(slots):
-
-        def store(comp, col, step, part, start, halves):
-            for level in range(2):
-                parts[comp, index, col, pl.ds(start + level * everyone, snaps), :] = halves[level]
-
-        for part in range(CORES):
-            start = rows_of(chips, 0, part, snaps)
-            for comp in range(3):
-                for col in range(cols):
-                    halves = [early[comp, slot, col, level, part] for level in range(2)]
-                    store(comp, col, 0, part, start, halves)
-        steps = range(1, chips)
+    steps = range(1, chips)
+    for index, slot in enumerate(range(1, planes)):
+
+        def store(comp, col, step, part, start, value):
+            put(parts, index, comp, col, start, split(value))
+
+        put_early(chips, early, slot, parts, index)
         plane = plane_at(slot, planes)
         curls(chips, tile, steps, coef, amplitude, plane, cols, snaps, store)
-        for comp in range(3):
-            for col in range(0, cols, 2):
-                both = jnp.concatenate([parts[comp, index, col], parts[comp, index, col + 1]], 1)
-                total[...] += lax.dot_general(
-                    both, both, (((1,), (1,)), ((), ())), preferred_element_type=jnp.float32
-                )
-    whole = (
-        total[:everyone, :everyone]
-        + total[everyone:, everyone:]
-        + (total[:everyone, everyone:] + total[everyone:, :everyone])
-    )
-    gram[...] = before[...] + jnp.concatenate(
-        [whole[: everyone // 2], whole[everyone // 2 :]], axis=1
-    )
-
-
-def far_stage(coef, amplitude, early, before, sources, chips, slots, halo):
-    comps, planes, cols, _, _, snaps, depth = early.shape
-    everyone = snaps * chips * CORES
+        add_products(parts, index, total)
+    gram[...] = folded(total)
+
+    def store(comp, col, step, part, start, value):
+        base[comp, step - 1, col, part * snaps : (part + 1) * snaps, :] = value
+
+    upper = lax.rem(lax.axis_index("slab"), 2)
+    plane = plane_at(0, planes)
+    curls(chips, tile, steps, coef, amplitude, plane, cols, snaps, store, upper)
+
+
+def last_kernel(chips, planes, coef, early, before, base, *refs):
+    sources, (parts, gram, beyond, total, sem) = refs[:-5], refs[-5:]
+    cols, snaps = early.shape[2], early.shape[5]
+    fetch_all([(source, beyond.at[k]) for k, source in enumerate(sources)], sem.at[0])
+    put_early(chips, early, 0, parts, 0)
+    upper = lax.rem(lax.axis_index("slab"), 2)
+    sign = (1 - 2 * upper).astype(jnp.float32)
+    plane = plane_at(0, planes)
+    for col in range(cols):
+        shear, gy = [row * sign for row in metric_rows(coef, plane, col, (1, 2), snaps)]
+        for step in range(1, chips):
+            for part in range(CORES):
+                rows = slice(part * snaps, (part + 1) * snaps)
+                u, v, w = [beyond[step - 1, k, col, rows].astype(jnp.float32) for k in range(3)]
+                added = (gy * w, -(shear * w), shear * v - gy * u)
+                start = rows_of(chips, step, part, snaps)
+                for comp in range(3):
+                    value = base[comp, step - 1, col, rows, :] + added[comp]
+                    put(parts, 0, comp, col, start, split(value))
+    total[...] = jnp.zeros_like(total)
+    add_products(parts, 0, total)
+    gram[...] = before[...] + folded(total)
+
+
+def stage(kernel, wholes, sources, outs, scratch, name):
     whole = pl.BlockSpec(memory_space=pltpu.VMEM)
     return pl.pallas_call(
-        functools.partial(far_kernel, chips, planes, slots, halo),
-        in_specs=[whole] * 4 + [pl.BlockSpec(memory_space=pl.ANY)] * len(sources),
-        out_specs=[whole, whole],
-        out_shape=[
-            jax.ShapeDtypeStruct((comps, len(slots), cols, 2 * everyone, depth), jnp.bfloat16),
-            jax.ShapeDtypeStruct((everyone // 2, 2 * everyone), jnp.float32),
-        ],
-        scratch_shapes=[
-            pltpu.VMEM(
-                (chips - 1, planes + 2, comps, cols + 2, CORES * snaps, depth), jnp.bfloat16
-            ),
-            pltpu.VMEM((2 * everyone, 2 * everyone), jnp.float32),
-            pltpu.SemaphoreType.DMA((1,)),
-        ],
+        kernel,
+        in_specs=[whole] * len(wholes) + [pl.BlockSpec(memory_space=pl.ANY)] * len(sources),
+        out_specs=[whole] * len(outs),
+        out_shape=[jax.ShapeDtypeStruct(*item) for item in outs],
+        scratch_shapes=scratch + [pltpu.SemaphoreType.DMA((1,))],
         compiler_params=pltpu.CompilerParams(vmem_limit_bytes=VMEM_BYTES),
         cost_estimate=pl.CostEstimate(flops=0, bytes_accessed=8 << 20, transcendentals=0),
-        name="far_stage",
-    )(coef, amplitude, early, before, *sources)
+        name=name,
+    )(*wholes, *sources)
+
+
+def far_stage(coef, amplitude, early, sources, chips):
+    comps, planes, cols, _, _, snaps, depth = early.shape
+    group, everyone = CORES * snaps, snaps * chips * CORES
+    kind = jnp.bfloat16
+    return stage(
+        functools.partial(far_kernel, chips, planes),
+        [coef, amplitude, early],
+        sources,
+        [
+            ((comps, planes - 1, cols, 2 * everyone, depth), kind),
+            ((everyone // 2, 2 * everyone), jnp.float32),
+            ((comps, chips - 1, cols, group, depth), jnp.float32),
+        ],
+        [
+            pltpu.VMEM((chips - 1, planes + 2, comps, cols + 2, group, depth), kind),
+            pltpu.VMEM((2 * everyone, everyone), jnp.float32),
+        ],
+        "far_stage",
+    )
+
+
+def last_stage(coef, early, gram, base, sources, chips):
+    comps, planes, cols, _, _, snaps, depth = early.shape
+    group, everyone = CORES * snaps, snaps * chips * CORES
+    kind = jnp.bfloat16
+    return stage(
+        functools.partial(last_kernel, chips, planes),
+        [coef, early, gram, base],
+        sources,
+        [((comps, 1, cols, 2 * everyone, depth), kind), (gram.shape, jnp.float32)],
+        [
+            pltpu.VMEM((chips - 1, comps, cols, group, depth), kind),
+            pltpu.VMEM((2 * everyone, everyone), jnp.float32),
+        ],
+        "last_stage",
+    )
 
 
 def product(a, b):
@@ -551,15 +639,13 @@
     sources = own + [near[0], to_core(near[1]), pair, away]
     sources += [to_core(half(pair)), to_core(half(away))]
     early, coef, amplitude = near_stage(modulation, metric, large_scale, sources, chips, cols)
-    everyone = modulation.shape[0]
-    gram = jnp.zeros((everyone // 2, 2 * everyone), jnp.float32)
-    pieces = []
-    for slots, halo in (((1,) + tuple(range(2, planes)), 1), ((0,), 0)):
-        sources = []
-        for here, *halos in arrays:
-            sources += here + [halos[halo]]
-        piece, gram = far_stage(coef, amplitude, early, gram, sources, chips, slots, halo)
-        pieces.append(piece)
+    sources = []
+    for here, _, outer_halo in arrays:
+        sources += here + [outer_halo]
+    far, gram, base = far_stage(coef, amplitude, early, sources, chips)
+    sources = [inner_halo for _, inner_halo, _ in arrays]
+    last, gram = last_stage(coef, early, gram, base, sources, chips)
+    pieces = [far, last]
     return whiten(all_sum(gram), pieces, float(comps * planes * slab_count * width * depth))
 
 

time: 65 us -> 64.7 us (level)
  no operation moved by 1% of the time
where the time goes in v6:
time: 64.7 us; the launch traced here: 64.5 us
  waiting for transfers between devices  26.8 us (41%)
  starting transfers between devices  21.6 us (33%)
  Pallas kernels  12.5 us (19%)
  local copies, waits for them, and re-layouts  3.3 us (5%)
    ppermute x3, waiting for transfers between devices, to_chip(): return lax.ppermute(array, 'snap', pairs)  15.3 us
    ppermute x7, starting transfers between devices, all_sum(): lax.ppermute(value, axis, [(i, i ^ k) for i in range(count)])  8.71 us
    ppermute x7, waiting for transfers between devices, all_sum(): lax.ppermute(value, axis, [(i, i ^ k) for i in range(count)])  8.58 us
    ppermute x4, starting transfers between devices, to_pair(): return lax.ppermute(array, 'slab', pairs + [(j, i) for i, j in pairs])  8.18 us
    pallas_call x1, Pallas kernels, whiten(): pl.pallas_call(functools.partial(whiten_kernel, count), in_specs=[whole]...  3.9 us
    ppermute x3, starting transfers between devices, to_chip(): return lax.ppermute(array, 'snap', pairs)  3.58 us
    pallas_call x2, Pallas kernels, stage(): pl.pallas_call(kernel, in_specs=[whole] * len(wholes) + [pl.BlockSpec(mem...  3.08 us
    ppermute x4, waiting for transfers between devices, to_pair(): return lax.ppermute(array, 'slab', pairs + [(j, i) for i, j in pairs])  2.86 us
  transfers between devices with their start and end apart: 18, of which 10 were waited for; matrix products, arithmetic and copies ran while one was open for 3% of the time, Pallas kernels for 10%

profile of v6, /device:TPU:0, one launch (start us, length us, event | category | flops | bytes accessed | tf_op | source)
XLA Modules:
  0.0 64.5 jit_solution(6816558053792249615)
XLA Ops:
  0.0 1.4 %copy-done = bf16[16,3,2,64,128]{4,3,2,1,0:T(8,128)(2,1)S(1)} copy-done((bf16[16,3,2,64,128]{4,3,2,1,0:T(8,128)(2,1)S(1)}, bf16[16,3,2,64,128]{4,3,2,1,0:T(8,128)(2,1)}, u32[]{:S(2)}) %copy-start) | copy-done | bytes 1572888
  1.4 0.5 pack_other.1
  2.0 0.5 collective-permute-start.2
  2.5 0.6 pack_own.1
  3.1 2.8 %collective-permute-start.1 = (bf16[3,35,16,128]{3,2,1,0:T(8,128)(2,1)S(1)}, bf16[3,35,16,128]{3,2,1,0:T(8,128)(2,1)S(1)}, u32[]{:S(2)}, u32[]{:S(2)}) collective-permute-start(bf16[3,35,16,128]{3,2,1,0:T(8,128)(2,1)S(1)} %get-tuple-element.26.refs_0_), channel_id=1, source_target_pairs={{0,4},{8,12},{16,20},{24,28},{4,0},{12,8},{20,16},{28,24},{1,5},{9... | collective-permute-start | bytes 1290248 | tf_op jit(solution)/shard_map/ppermute | solution.py:594
  5.9 0.5 pack_mine.1
  6.4 0.0 collective-permute-done.2
  6.4 0.1 pad_maximum_fusion
  6.5 0.0 copy-start.4
  6.5 0.7 %collective-permute-start.3 = (bf16[3,33,16,128]{3,2,1,0:T(8,128)(2,1)S(1)}, bf16[3,33,16,128]{3,2,1,0:T(8,128)(2,1)S(1)}, u32[]{:S(2)}, u32[]{:S(2)}) collective-permute-start(bf16[3,33,16,128]{3,2,1,0:T(8,128)(2,1)S(1)} %get-tuple-element.32.refs_1_), channel_id=1, source_target_pairs={{4,8},{12,16},{20,24},{8,4},{16,12},{24,20},{5,9},{13,17},{21,25},... | collective-permute-start | bytes 1216520 | tf_op jit(solution)/shard_map/ppermute | solution.py:594
  7.2 1.0 %slice_bitcast_fusion = (bf16[3,16,32,128]{3,2,1,0:T(8,128)(2,1)}, bf16[3,16,32,128]{3,2,1,0:T(8,128)(2,1)}) fusion(bf16[3,2,18,32,128]{4,3,2,0,1:T(8,128)(2,1)S(1)} %pad_maximum_fusion), kind=kLoop, calls=%fused_computation.1 | loop fusion | bytes 1572864 | tf_op jit(solution)/shard_map/squeeze | solution.py:632
  8.2 1.5 %collective-permute-start.5 = (bf16[3,16,32,128]{3,2,1,0:T(8,128)(2,1)}, bf16[3,16,32,128]{3,2,1,0:T(8,128)(2,1)S(1)}, u32[]{:S(2)}, u32[]{:S(2)}) collective-permute-start(bf16[3,16,32,128]{3,2,1,0:T(8,128)(2,1)} %get-tuple-element.47), channel_id=1, source_target_pairs={{0,2},{1,3},{2,0},{3,1},{4,6},{5,7},{6,4},{7,5},{8,10},{9,11},{10,... | collective-permute-start | bytes 1179656 | tf_op jit(solution)/shard_map/ppermute | solution.py:584
  9.7 0.5 collective-permute-start.4
  10.2 1.7 %pack_near.1 = (bf16[3,4,16,128]{3,2,1,0:T(8,128)(2,1)S(1)}, bf16[3,2,18,16,128]{4,3,2,1,0:T(8,128)(2,1)}) custom-call(bf16[16,3,2,64,128]{4,3,2,1,0:T(8,128)(2,1)S(1)} %copy-done), custom_call_target="tpu_custom_call" | custom-call | tf_op jit(solution)/shard_map/pack_near/pallas_call | solution.py:121
  11.9 0.0 collective-permute-start
  11.9 0.8 %fusion = (bf16[3,2,1,32,128]{4,3,2,0,1:T(8,128)(2,1)S(1)}, bf16[3,2,1,32,128]{4,3,2,0,1:T(8,128)(2,1)S(1)}) fusion(bf16[3,2,18,32,128]{4,3,2,0,1:T(8,128)(2,1)} %copy-done.4), kind=kLoop, calls=%fused_computation.8 | loop fusion | bytes 196608 | tf_op jit(solution)/shard_map/slice | solution.py:633
  12.7 7.7 %collective-permute-done.5.refs_1_ = bf16[3,16,32,128]{3,2,1,0:T(8,128)(2,1)S(1)} collective-permute-done((bf16[3,16,32,128]{3,2,1,0:T(8,128)(2,1)}, bf16[3,16,32,128]{3,2,1,0:T(8,128)(2,1)S(1)}, u32[]{:S(2)}, u32[]{:S(2)}) %collective-permute-start.5) | collective-permute-done | bytes 393248 | tf_op jit(solution)/shard_map/ppermute | solution.py:584
  20.4 0.7 %collective-permute-start.9 = (bf16[3,16,32,128]{3,2,1,0:T(8,128)(2,1)S(1)}, bf16[3,16,32,128]{3,2,1,0:T(8,128)(2,1)S(1)}, u32[]{:S(2)}, u32[]{:S(2)}) collective-permute-start(bf16[3,16,32,128]{3,2,1,0:T(8,128)(2,1)S(1)} %collective-permute-done.5.refs_1_), channel_id=1, source_target_pairs={{4,8},{12,16},{20,24},{8,4},{16,12},{24,20},{5,9},{13,17},{21,25},... | collective-permute-start | bytes 1179656 | tf_op jit(solution)/shard_map/ppermute | solution.py:594
  21.1 6.7 %collective-permute-done.4.refs_0_ = bf16[3,16,32,128]{3,2,1,0:T(8,128)(2,1)S(1)} collective-permute-done((bf16[3,16,32,128]{3,2,1,0:T(8,128)(2,1)}, bf16[3,16,32,128]{3,2,1,0:T(8,128)(2,1)S(1)}, u32[]{:S(2)}, u32[]{:S(2)}) %collective-permute-start.4) | collective-permute-done | bytes 393248 | tf_op jit(solution)/shard_map/ppermute | solution.py:584
  27.8 4.0 %collective-permute-start.10 = (bf16[3,16,32,128]{3,2,1,0:T(8,128)(2,1)S(1)}, bf16[3,16,32,128]{3,2,1,0:T(8,128)(2,1)S(1)}, u32[]{:S(2)}, u32[]{:S(2)}) collective-permute-start(bf16[3,16,32,128]{3,2,1,0:T(8,128)(2,1)S(1)} %collective-permute-done.4.refs_0_), channel_id=1, source_target_pairs={{0,4},{8,12},{16,20},{24,28},{4,0},{12,8},{20,16},{28,24},{1,5},{9... | collective-permute-start | bytes 1179656 | tf_op jit(solution)/shard_map/ppermute | solution.py:594
  31.8 0.0 collective-permute-done.1.refs_4_
  31.8 0.0 collective-permute-done.3.refs_5_
  31.8 0.1 collective-permute-start.7
  31.9 0.5 collective-permute-start.6
  32.5 0.0 collective-permute-done.refs_3_
  32.5 1.6 %collective-permute-start.8 = (bf16[3,4,32,128]{3,2,1,0:T(8,128)(2,1)S(1)}, bf16[3,4,32,128]{3,2,1,0:T(8,128)(2,1)S(1)}, u32[]{:S(2)}, u32[]{:S(2)}) collective-permute-start(bf16[3,4,32,128]{3,2,1,0:T(8,128)(2,1)S(1)} %bitcast.5), channel_id=1, source_target_pairs={{0,2},{1,3},{2,0},{3,1},{4,6},{5,7},{6,4},{7,5},{8,10},{9,11},{10,... | collective-permute-start | bytes 294920 | tf_op jit(solution)/shard_map/ppermute | solution.py:584
  34.1 0.0 collective-permute-done.7.refs_7_
  34.1 0.0 collective-permute-done.6.refs_6_
  34.1 2.3 %near_stage.1 = (bf16[3,2,16,2,2,16,128]{6,5,4,3,2,1,0:T(8,128)(2,1)S(1)}, f32[2,11,16,128]{3,2,1,0:T(8,128)S(1)}, f32[18,64,128]{2,1,0:T(8,128)S(1)}) custom-call(f32[64,64]{1,0:T(8,128)S(1)} %copy-done.3, f32[4,2,64,128]{3,2,1,0:T(8,128)S(1)} %copy-done.2, bf16[3,2,64,128]{3,2,1,0:T(8,128)(2,1)S(1)} %copy-done.1, ...), custom_call_target="tpu_custom_call" | custom-call | bytes 8388608 | tf_op jit(solution)/shard_map/near_stage/pallas_call | solution.py:324
  36.4 0.9 %collective-permute-done.8.refs_2_ = bf16[3,4,32,128]{3,2,1,0:T(8,128)(2,1)S(1)} collective-permute-done((bf16[3,4,32,128]{3,2,1,0:T(8,128)(2,1)S(1)}, bf16[3,4,32,128]{3,2,1,0:T(8,128)(2,1)S(1)}, u32[]{:S(2)}, u32[]{:S(2)}) %collective-permute-start.8) | collective-permute-done | bytes 98336 | tf_op jit(solution)/shard_map/ppermute | solution.py:584
  37.3 1.7 %far_stage.1 = (bf16[3,1,16,128,128]{4,3,2,1,0:T(8,128)(2,1)S(1)}, f32[32,128]{1,0:T(8,128)S(1)}, f32[3,1,16,32,128]{4,3,2,1,0:T(8,128)S(1)}) custom-call(f32[2,11,16,128]{3,2,1,0:T(8,128)S(1)} %get-tuple-element.36.coef, f32[18,64,128]{2,1,0:T(8,128)S(1)} %get-tuple-element.38.amplitude, bf16[3,2,16,2,2,16,128]{6,5,4,3,2,1,0:T(8,128)(2,1)S(1)} %get-tuple-element.37.early, ...), custom_call_target="tpu_custom_call" | custom-call | bytes 8388608 | tf_op jit(solution)/shard_map/far_stage/pallas_call | solution.py:451
  39.1 2.8 %collective-permute-done.10.refs_0_ = bf16[3,16,32,128]{3,2,1,0:T(8,128)(2,1)S(1)} collective-permute-done((bf16[3,16,32,128]{3,2,1,0:T(8,128)(2,1)S(1)}, bf16[3,16,32,128]{3,2,1,0:T(8,128)(2,1)S(1)}, u32[]{:S(2)}, u32[]{:S(2)}) %collective-permute-start.10) | collective-permute-done | bytes 393248 | tf_op jit(solution)/shard_map/ppermute | solution.py:594
  41.9 1.3 %last_stage.1 = (bf16[3,1,16,128,128]{4,3,2,1,0:T(8,128)(2,1)S(1)}, f32[32,128]{1,0:T(8,128)S(1)}) custom-call(f32[2,11,16,128]{3,2,1,0:T(8,128)S(1)} %get-tuple-element.36.coef, bf16[3,2,16,2,2,16,128]{6,5,4,3,2,1,0:T(8,128)(2,1)S(1)} %get-tuple-element.37.early, f32[32,128]{1,0:T(8,128)S(1)} %get-tuple-element.40.before, ...), custom_call_target="tpu_custom_call" | custom-call | bytes 8388608 | tf_op jit(solution)/shard_map/last_stage/pallas_call | solution.py:451
  43.3 1.2 %collective-permute-start.13 = (f32[32,128]{1,0:T(8,128)S(1)}, f32[32,128]{1,0:T(8,128)S(1)}, u32[]{:S(2)}, u32[]{:S(2)}) collective-permute-start(f32[32,128]{1,0:T(8,128)S(1)} %get-tuple-element.42), channel_id=1, source_target_pairs={{0,3},{1,2},{2,1},{3,0},{4,7},{5,6},{6,5},{7,4},{8,11},{9,10},{10,... | collective-permute-start | bytes 49160 | tf_op jit(solution)/shard_map/ppermute | solution.py:607
  44.4 0.5 collective-permute-start.12
  45.0 0.2 collective-permute-start.11
  45.2 1.3 %collective-permute-done.13 = f32[32,128]{1,0:T(8,128)S(1)} collective-permute-done((f32[32,128]{1,0:T(8,128)S(1)}, f32[32,128]{1,0:T(8,128)S(1)}, u32[]{:S(2)}, u32[]{:S(2)}) %collective-permute-start.13) | collective-permute-done | bytes 16416 | tf_op jit(solution)/shard_map/ppermute | solution.py:607
  46.5 1.7 %collective-permute-done.12 = f32[32,128]{1,0:T(8,128)S(1)} collective-permute-done((f32[32,128]{1,0:T(8,128)S(1)}, f32[32,128]{1,0:T(8,128)S(1)}, u32[]{:S(2)}, u32[]{:S(2)}) %collective-permute-start.12) | collective-permute-done | bytes 16416 | tf_op jit(solution)/shard_map/ppermute | solution.py:607
  48.2 0.0 collective-permute-done.11
  48.2 3.5 %collective-permute-start.16 = (f32[32,128]{1,0:T(8,128)S(1)}, f32[32,128]{1,0:T(8,128)S(1)}, u32[]{:S(2)}, u32[]{:S(2)}) collective-permute-start(f32[32,128]{1,0:T(8,128)S(1)} %add_add_fusion.1), channel_id=1, source_target_pairs={{0,12},{4,8},{8,4},{12,0},{16,28},{20,24},{24,20},{28,16},{1,13},{... | collective-permute-start | bytes 49160 | tf_op jit(solution)/shard_map/ppermute | solution.py:607
  51.7 0.5 collective-permute-start.15
  52.2 0.2 collective-permute-start.14
  52.4 1.1 %collective-permute-done.16 = f32[32,128]{1,0:T(8,128)S(1)} collective-permute-done((f32[32,128]{1,0:T(8,128)S(1)}, f32[32,128]{1,0:T(8,128)S(1)}, u32[]{:S(2)}, u32[]{:S(2)}) %collective-permute-start.16) | collective-permute-done | bytes 16416 | tf_op jit(solution)/shard_map/ppermute | solution.py:607
  53.5 2.0 %collective-permute-done.15 = f32[32,128]{1,0:T(8,128)S(1)} collective-permute-done((f32[32,128]{1,0:T(8,128)S(1)}, f32[32,128]{1,0:T(8,128)S(1)}, u32[]{:S(2)}, u32[]{:S(2)}) %collective-permute-start.15) | collective-permute-done | bytes 16416 | tf_op jit(solution)/shard_map/ppermute | solution.py:607
  55.5 0.5 collective-permute-done.14
  55.9 2.6 %collective-permute-start.17 = (f32[32,128]{1,0:T(8,128)S(1)}, f32[32,128]{1,0:T(8,128)S(1)}, u32[]{:S(2)}, u32[]{:S(2)}) collective-permute-start(f32[32,128]{1,0:T(8,128)S(1)} %add_add_fusion), channel_id=1, source_target_pairs={{0,16},{4,20},{8,24},{12,28},{16,0},{20,4},{24,8},{28,12},{1,17},{... | collective-permute-start | bytes 49160 | tf_op jit(solution)/shard_map/ppermute | solution.py:607
  58.5 2.0 %collective-permute-done.17 = f32[32,128]{1,0:T(8,128)S(1)} collective-permute-done((f32[32,128]{1,0:T(8,128)S(1)}, f32[32,128]{1,0:T(8,128)S(1)}, u32[]{:S(2)}, u32[]{:S(2)}) %collective-permute-start.17) | collective-permute-done | bytes 16416 | tf_op jit(solution)/shard_map/ppermute | solution.py:607
  60.6 3.9 %whiten.1 = f32[64,3,2,16,128]{4,3,2,1,0:T(8,128)} custom-call(f32[32,128]{1,0:T(8,128)S(1)} %add.35.gram, bf16[3,1,16,128,128]{4,3,2,1,0:T(8,128)(2,1)S(1)} %get-tuple-element.43.refs_0_, bf16[3,1,16,128,128]{4,3,2,1,0:T(8,128)(2,1)S(1)} %get-tuple-element.44.refs_1_), custom_call_target="tpu_custom_call" | custom-call | tf_op jit(solution)/shard_map/whiten/pallas_call | solution.py:567
  (17 shorter events, 0.1 us)
Async XLA Ops:
  0.0 1.4 %copy-start = (bf16[16,3,2,64,128]{4,3,2,1,0:T(8,128)(2,1)S(1)}, bf16[16,3,2,64,128]{4,3,2,1,0:T(8,128)(2,1)}, u32[]{:S(2)}) copy-start(bf16[16,3,2,64,128]{4,3,2,1,0:T(8,128)(2,1)} %flow.4) | copy-start | bytes 4718596
  1.4 1.1 %copy-start.1 = (bf16[3,2,64,128]{3,2,1,0:T(8,128)(2,1)S(1)}, bf16[3,2,64,128]{3,2,1,0:T(8,128)(2,1)}, u32[]{:S(2)}) copy-start(bf16[3,2,64,128]{3,2,1,0:T(8,128)(2,1)} %large.3) | copy-start | bytes 294916
  2.0 4.4 %collective-permute-start.2 = (bf16[3,2,18,16,128]{4,3,2,0,1:T(8,128)(2,1)S(1)}, bf16[3,2,18,16,128]{4,3,2,0,1:T(8,128)(2,1)S(1)}, u32[]{:S(2)}, u32[]{:S(2)}) collective-permute-start(bf16[3,2,18,16,128]{4,3,2,0,1:T(8,128)(2,1)S(1)} %copy.7), channel_id=1, source_target_pairs={{0,1},{1,0},{2,3},{3,2},{4,5},{5,4},{6,7},{7,6},{8,9},{9,8},{10,11... | collective-permute-start | bytes 1327112 | tf_op jit(solution)/shard_map/ppermute | solution.py:588
  3.1 28.7 %collective-permute-start.1 = (bf16[3,35,16,128]{3,2,1,0:T(8,128)(2,1)S(1)}, bf16[3,35,16,128]{3,2,1,0:T(8,128)(2,1)S(1)}, u32[]{:S(2)}, u32[]{:S(2)}) collective-permute-start(bf16[3,35,16,128]{3,2,1,0:T(8,128)(2,1)S(1)} %get-tuple-element.26.refs_0_), channel_id=1, source_target_pairs={{0,4},{8,12},{16,20},{24,28},{4,0},{12,8},{20,16},{28,24},{1,5},{9... | collective-permute-start | bytes 1290248 | tf_op jit(solution)/shard_map/ppermute | solution.py:594
  6.5 3.2 %copy-start.4 = (bf16[3,2,18,32,128]{4,3,2,0,1:T(8,128)(2,1)}, bf16[3,2,18,32,128]{4,3,2,0,1:T(8,128)(2,1)S(1)}, u32[]{:S(2)}) copy-start(bf16[3,2,18,32,128]{4,3,2,0,1:T(8,128)(2,1)S(1)} %pad_maximum_fusion) | copy-start | bytes 2654212
  6.5 25.3 %collective-permute-start.3 = (bf16[3,33,16,128]{3,2,1,0:T(8,128)(2,1)S(1)}, bf16[3,33,16,128]{3,2,1,0:T(8,128)(2,1)S(1)}, u32[]{:S(2)}, u32[]{:S(2)}) collective-permute-start(bf16[3,33,16,128]{3,2,1,0:T(8,128)(2,1)S(1)} %get-tuple-element.32.refs_1_), channel_id=1, source_target_pairs={{4,8},{12,16},{20,24},{8,4},{16,12},{24,20},{5,9},{13,17},{21,25},... | collective-permute-start | bytes 1216520 | tf_op jit(solution)/shard_map/ppermute | solution.py:594
  8.2 25.9 %copy-start.2 = (f32[4,2,64,128]{3,2,1,0:T(8,128)S(1)}, f32[4,2,64,128]{3,2,1,0:T(8,128)}, u32[]{:S(2)}) copy-start(f32[4,2,64,128]{3,2,1,0:T(8,128)} %metric.1) | copy-start | bytes 786436
  8.2 25.9 %copy-start.3 = (f32[64,64]{1,0:T(8,128)S(1)}, f32[64,64]{1,0:T(8,128)}, u32[]{:S(2)}) copy-start(f32[64,64]{1,0:T(8,128)} %modulation.1) | copy-start | bytes 49156
  8.2 12.2 %collective-permute-start.5 = (bf16[3,16,32,128]{3,2,1,0:T(8,128)(2,1)}, bf16[3,16,32,128]{3,2,1,0:T(8,128)(2,1)S(1)}, u32[]{:S(2)}, u32[]{:S(2)}) collective-permute-start(bf16[3,16,32,128]{3,2,1,0:T(8,128)(2,1)} %get-tuple-element.47), channel_id=1, source_target_pairs={{0,2},{1,3},{2,0},{3,1},{4,6},{5,7},{6,4},{7,5},{8,10},{9,11},{10,... | collective-permute-start | bytes 1179656 | tf_op jit(solution)/shard_map/ppermute | solution.py:584
  9.7 18.1 %collective-permute-start.4 = (bf16[3,16,32,128]{3,2,1,0:T(8,128)(2,1)}, bf16[3,16,32,128]{3,2,1,0:T(8,128)(2,1)S(1)}, u32[]{:S(2)}, u32[]{:S(2)}) collective-permute-start(bf16[3,16,32,128]{3,2,1,0:T(8,128)(2,1)} %get-tuple-element.48), channel_id=1, source_target_pairs={{0,2},{1,3},{2,0},{3,1},{4,6},{5,7},{6,4},{7,5},{8,10},{9,11},{10,... | collective-permute-start | bytes 1179656 | tf_op jit(solution)/shard_map/ppermute | solution.py:584
  11.9 20.6 %collective-permute-start = (bf16[3,2,18,16,128]{4,3,2,1,0:T(8,128)(2,1)}, bf16[3,2,18,16,128]{4,3,2,1,0:T(8,128)(2,1)S(1)}, u32[]{:S(2)}, u32[]{:S(2)}) collective-permute-start(bf16[3,2,18,16,128]{4,3,2,1,0:T(8,128)(2,1)} %get-tuple-element.31), channel_id=1, source_target_pairs={{0,1},{1,0},{2,3},{3,2},{4,5},{5,4},{6,7},{7,6},{8,9},{9,8},{10,11... | collective-permute-start | bytes 1327112 | tf_op jit(solution)/shard_map/ppermute | solution.py:588
  20.4 16.9 %collective-permute-start.9 = (bf16[3,16,32,128]{3,2,1,0:T(8,128)(2,1)S(1)}, bf16[3,16,32,128]{3,2,1,0:T(8,128)(2,1)S(1)}, u32[]{:S(2)}, u32[]{:S(2)}) collective-permute-start(bf16[3,16,32,128]{3,2,1,0:T(8,128)(2,1)S(1)} %collective-permute-done.5.refs_1_), channel_id=1, source_target_pairs={{4,8},{12,16},{20,24},{8,4},{16,12},{24,20},{5,9},{13,17},{21,25},... | collective-permute-start | bytes 1179656 | tf_op jit(solution)/shard_map/ppermute | solution.py:594
  27.8 14.1 %collective-permute-start.10 = (bf16[3,16,32,128]{3,2,1,0:T(8,128)(2,1)S(1)}, bf16[3,16,32,128]{3,2,1,0:T(8,128)(2,1)S(1)}, u32[]{:S(2)}, u32[]{:S(2)}) collective-permute-start(bf16[3,16,32,128]{3,2,1,0:T(8,128)(2,1)S(1)} %collective-permute-done.4.refs_0_), channel_id=1, source_target_pairs={{0,4},{8,12},{16,20},{24,28},{4,0},{12,8},{20,16},{28,24},{1,5},{9... | collective-permute-start | bytes 1179656 | tf_op jit(solution)/shard_map/ppermute | solution.py:594
  31.8 2.3 %collective-permute-start.7 = (bf16[3,16,16,128]{3,2,1,0:T(8,128)(2,1)S(1)}, bf16[3,16,16,128]{3,2,1,0:T(8,128)(2,1)S(1)}, u32[]{:S(2)}, u32[]{:S(2)}) collective-permute-start(bf16[3,16,16,128]{3,2,1,0:T(8,128)(2,1)S(1)} %constant_dynamic-slice_fusion), channel_id=1, source_target_pairs={{0,1},{1,0},{2,3},{3,2},{4,5},{5,4},{6,7},{7,6},{8,9},{9,8},{10,11... | collective-permute-start | bytes 589832 | tf_op jit(solution)/shard_map/ppermute | solution.py:588
  31.9 2.1 %collective-permute-start.6 = (bf16[3,16,16,128]{3,2,1,0:T(8,128)(2,1)S(1)}, bf16[3,16,16,128]{3,2,1,0:T(8,128)(2,1)S(1)}, u32[]{:S(2)}, u32[]{:S(2)}) collective-permute-start(bf16[3,16,16,128]{3,2,1,0:T(8,128)(2,1)S(1)} %constant_dynamic-slice_fusion.1), channel_id=1, source_target_pairs={{0,1},{1,0},{2,3},{3,2},{4,5},{5,4},{6,7},{7,6},{8,9},{9,8},{10,11... | collective-permute-start | bytes 589832 | tf_op jit(solution)/shard_map/ppermute | solution.py:588
  32.5 4.8 %collective-permute-start.8 = (bf16[3,4,32,128]{3,2,1,0:T(8,128)(2,1)S(1)}, bf16[3,4,32,128]{3,2,1,0:T(8,128)(2,1)S(1)}, u32[]{:S(2)}, u32[]{:S(2)}) collective-permute-start(bf16[3,4,32,128]{3,2,1,0:T(8,128)(2,1)S(1)} %bitcast.5), channel_id=1, source_target_pairs={{0,2},{1,3},{2,0},{3,1},{4,6},{5,7},{6,4},{7,5},{8,10},{9,11},{10,... | collective-permute-start | bytes 294920 | tf_op jit(solution)/shard_map/ppermute | solution.py:584
  43.3 3.2 %collective-permute-start.13 = (f32[32,128]{1,0:T(8,128)S(1)}, f32[32,128]{1,0:T(8,128)S(1)}, u32[]{:S(2)}, u32[]{:S(2)}) collective-permute-start(f32[32,128]{1,0:T(8,128)S(1)} %get-tuple-element.42), channel_id=1, source_target_pairs={{0,3},{1,2},{2,1},{3,0},{4,7},{5,6},{6,5},{7,4},{8,11},{9,10},{10,... | collective-permute-start | bytes 49160 | tf_op jit(solution)/shard_map/ppermute | solution.py:607
  44.4 3.7 %collective-permute-start.12 = (f32[32,128]{1,0:T(8,128)S(1)}, f32[32,128]{1,0:T(8,128)S(1)}, u32[]{:S(2)}, u32[]{:S(2)}) collective-permute-start(f32[32,128]{1,0:T(8,128)S(1)} %get-tuple-element.42), channel_id=1, source_target_pairs={{0,2},{1,3},{2,0},{3,1},{4,6},{5,7},{6,4},{7,5},{8,10},{9,11},{10,... | collective-permute-start | bytes 49160 | tf_op jit(solution)/shard_map/ppermute | solution.py:607
  45.0 3.2 %collective-permute-start.11 = (f32[32,128]{1,0:T(8,128)S(1)}, f32[32,128]{1,0:T(8,128)S(1)}, u32[]{:S(2)}, u32[]{:S(2)}) collective-permute-start(f32[32,128]{1,0:T(8,128)S(1)} %get-tuple-element.42), channel_id=1, source_target_pairs={{0,1},{1,0},{2,3},{3,2},{4,5},{5,4},{6,7},{7,6},{8,9},{9,8},{10,11... | collective-permute-start | bytes 49160 | tf_op jit(solution)/shard_map/ppermute | solution.py:607
  48.2 5.3 %collective-permute-start.16 = (f32[32,128]{1,0:T(8,128)S(1)}, f32[32,128]{1,0:T(8,128)S(1)}, u32[]{:S(2)}, u32[]{:S(2)}) collective-permute-start(f32[32,128]{1,0:T(8,128)S(1)} %add_add_fusion.1), channel_id=1, source_target_pairs={{0,12},{4,8},{8,4},{12,0},{16,28},{20,24},{24,20},{28,16},{1,13},{... | collective-permute-start | bytes 49160 | tf_op jit(solution)/shard_map/ppermute | solution.py:607
  51.7 3.7 %collective-permute-start.15 = (f32[32,128]{1,0:T(8,128)S(1)}, f32[32,128]{1,0:T(8,128)S(1)}, u32[]{:S(2)}, u32[]{:S(2)}) collective-permute-start(f32[32,128]{1,0:T(8,128)S(1)} %add_add_fusion.1), channel_id=1, source_target_pairs={{0,8},{4,12},{8,0},{12,4},{16,24},{20,28},{24,16},{28,20},{1,9},{5... | collective-permute-start | bytes 49160 | tf_op jit(solution)/shard_map/ppermute | solution.py:607
  52.2 3.7 %collective-permute-start.14 = (f32[32,128]{1,0:T(8,128)S(1)}, f32[32,128]{1,0:T(8,128)S(1)}, u32[]{:S(2)}, u32[]{:S(2)}) collective-permute-start(f32[32,128]{1,0:T(8,128)S(1)} %add_add_fusion.1), channel_id=1, source_target_pairs={{0,4},{4,0},{8,12},{12,8},{16,20},{20,16},{24,28},{28,24},{1,5},{5... | collective-permute-start | bytes 49160 | tf_op jit(solution)/shard_map/ppermute | solution.py:607
  55.9 4.6 %collective-permute-start.17 = (f32[32,128]{1,0:T(8,128)S(1)}, f32[32,128]{1,0:T(8,128)S(1)}, u32[]{:S(2)}, u32[]{:S(2)}) collective-permute-start(f32[32,128]{1,0:T(8,128)S(1)} %add_add_fusion), channel_id=1, source_target_pairs={{0,16},{4,20},{8,24},{12,28},{16,0},{20,4},{24,8},{28,12},{1,17},{... | collective-permute-start | bytes 49160 | tf_op jit(solution)/shard_map/ppermute | solution.py:607

commit v7 on v6

--- a/solution.py
+++ b/solution.py
@@ -133,7 +133,7 @@
 
     away = range(1, chips)
     other = windows([(False, step) for step in away], None, "pack_other")
-    lengths = [span + extra + 2] + [span + extra] * (planes - 1)
+    lengths = [span + extra] + [span + extra] * (planes - 1)
     own = pl.pallas_call(
         functools.partial(pack_own_kernel, planes, cols),
         in_specs=[pl.BlockSpec(memory_space=pltpu.HBM)] * 2,
@@ -595,19 +595,19 @@
 
 
 def all_sum(value):
-    for axis in ("snap", "slab"):
+    for axis in ("slab", "snap"):
         count = lax.axis_size(axis)
         if count & (count - 1):
             value = lax.psum(value, axis)
             continue
-        stride = 1
-        while stride < count:
-            partners = [stride] if 2 * stride == count else [stride, 2 * stride, 3 * stride]
+        while count > 1:
+            step = count // 4 if count > 2 else 1
             received = [
-                lax.ppermute(value, axis, [(i, i ^ k) for i in range(count)]) for k in partners
+                lax.ppermute(value, axis, [(i, i ^ k) for i in range(lax.axis_size(axis))])
+                for k in range(step, count, step)
             ]
             value = sum(received, value)
-            stride *= 1 + len(partners)
+            count = step
     return value
 
 

time: 64.7 us -> 63.2 us (0.977)
  starting transfers between devices: 21.6 us -> 20.3 us
    ppermute x7, starting transfers between devices: 8.71 us -> 7.43 us  [all_sum(): lax.ppermute(value, axis, [(i, i ^ k) for i in range(lax.axis_size(axis))])]
  transfers between devices with their start and end apart: 18 -> 18, of which waited for: 10 -> 9; matrix products, arithmetic and copies ran while one was open for 3% -> 3% of each run, Pallas kernels for 10% -> 11%
where the time goes in v7:
time: 63.2 us; the launch traced here: 63 us
  waiting for transfers between devices  26.6 us (42%)
  starting transfers between devices  20.3 us (32%)
  Pallas kernels  12.5 us (20%)
  local copies, waits for them, and re-layouts  3.3 us (5%)
    ppermute x3, waiting for transfers between devices, to_chip(): return lax.ppermute(array, 'snap', pairs)  15.3 us
    ppermute x7, waiting for transfers between devices, all_sum(): lax.ppermute(value, axis, [(i, i ^ k) for i in range(lax.axis_size(axis))])  8.39 us
    ppermute x4, starting transfers between devices, to_pair(): return lax.ppermute(array, 'slab', pairs + [(j, i) for i, j in pairs])  8.18 us
    ppermute x7, starting transfers between devices, all_sum(): lax.ppermute(value, axis, [(i, i ^ k) for i in range(lax.axis_size(axis))])  7.43 us
    pallas_call x1, Pallas kernels, whiten(): pl.pallas_call(functools.partial(whiten_kernel, count), in_specs=[whole]...  3.89 us
    ppermute x3, starting transfers between devices, to_chip(): return lax.ppermute(array, 'snap', pairs)  3.58 us
    pallas_call x2, Pallas kernels, stage(): pl.pallas_call(kernel, in_specs=[whole] * len(wholes) + [pl.BlockSpec(mem...  3.07 us
    ppermute x4, waiting for transfers between devices, to_pair(): return lax.ppermute(array, 'slab', pairs + [(j, i) for i, j in pairs])  2.86 us
  transfers between devices with their start and end apart: 18, of which 9 were waited for; matrix products, arithmetic and copies ran while one was open for 3% of the time, Pallas kernels for 11%

profile of v7, /device:TPU:0, one launch (start us, length us, event | category | flops | bytes accessed | tf_op | source)
XLA Modules:
  0.0 63.0 jit_solution(17834860406558902834)
XLA Ops:
  0.0 1.4 %copy-done = bf16[16,3,2,64,128]{4,3,2,1,0:T(8,128)(2,1)S(1)} copy-done((bf16[16,3,2,64,128]{4,3,2,1,0:T(8,128)(2,1)S(1)}, bf16[16,3,2,64,128]{4,3,2,1,0:T(8,128)(2,1)}, u32[]{:S(2)}) %copy-start) | copy-done | bytes 1572888
  1.4 0.5 pack_other.1
  2.0 0.5 collective-permute-start.2
  2.5 0.6 pack_own.1
  3.1 2.8 %collective-permute-start.1 = (bf16[3,33,16,128]{3,2,1,0:T(8,128)(2,1)S(1)}, bf16[3,33,16,128]{3,2,1,0:T(8,128)(2,1)S(1)}, u32[]{:S(2)}, u32[]{:S(2)}) collective-permute-start(bf16[3,33,16,128]{3,2,1,0:T(8,128)(2,1)S(1)} %get-tuple-element.26.refs_0_), channel_id=1, source_target_pairs={{0,4},{8,12},{16,20},{24,28},{4,0},{12,8},{20,16},{28,24},{1,5},{9... | collective-permute-start | bytes 1216520 | tf_op jit(solution)/shard_map/ppermute | solution.py:594
  5.9 0.5 pack_mine.1
  6.4 0.0 collective-permute-done.2
  6.4 0.1 pad_maximum_fusion
  6.5 0.0 copy-start.4
  6.5 0.7 %collective-permute-start.3 = (bf16[3,33,16,128]{3,2,1,0:T(8,128)(2,1)S(1)}, bf16[3,33,16,128]{3,2,1,0:T(8,128)(2,1)S(1)}, u32[]{:S(2)}, u32[]{:S(2)}) collective-permute-start(bf16[3,33,16,128]{3,2,1,0:T(8,128)(2,1)S(1)} %get-tuple-element.32.refs_1_), channel_id=1, source_target_pairs={{4,8},{12,16},{20,24},{8,4},{16,12},{24,20},{5,9},{13,17},{21,25},... | collective-permute-start | bytes 1216520 | tf_op jit(solution)/shard_map/ppermute | solution.py:594
  7.2 1.0 %slice_bitcast_fusion = (bf16[3,16,32,128]{3,2,1,0:T(8,128)(2,1)}, bf16[3,16,32,128]{3,2,1,0:T(8,128)(2,1)}) fusion(bf16[3,2,18,32,128]{4,3,2,0,1:T(8,128)(2,1)S(1)} %pad_maximum_fusion), kind=kLoop, calls=%fused_computation.1 | loop fusion | bytes 1572864 | tf_op jit(solution)/shard_map/squeeze | solution.py:632
  8.2 1.5 %collective-permute-start.5 = (bf16[3,16,32,128]{3,2,1,0:T(8,128)(2,1)}, bf16[3,16,32,128]{3,2,1,0:T(8,128)(2,1)S(1)}, u32[]{:S(2)}, u32[]{:S(2)}) collective-permute-start(bf16[3,16,32,128]{3,2,1,0:T(8,128)(2,1)} %get-tuple-element.47), channel_id=1, source_target_pairs={{0,2},{1,3},{2,0},{3,1},{4,6},{5,7},{6,4},{7,5},{8,10},{9,11},{10,... | collective-permute-start | bytes 1179656 | tf_op jit(solution)/shard_map/ppermute | solution.py:584
  9.7 0.5 collective-permute-start.4
  10.2 1.7 %pack_near.1 = (bf16[3,4,16,128]{3,2,1,0:T(8,128)(2,1)S(1)}, bf16[3,2,18,16,128]{4,3,2,1,0:T(8,128)(2,1)}) custom-call(bf16[16,3,2,64,128]{4,3,2,1,0:T(8,128)(2,1)S(1)} %copy-done), custom_call_target="tpu_custom_call" | custom-call | tf_op jit(solution)/shard_map/pack_near/pallas_call | solution.py:121
  11.9 0.0 collective-permute-start
  11.9 0.8 %fusion = (bf16[3,2,1,32,128]{4,3,2,0,1:T(8,128)(2,1)S(1)}, bf16[3,2,1,32,128]{4,3,2,0,1:T(8,128)(2,1)S(1)}) fusion(bf16[3,2,18,32,128]{4,3,2,0,1:T(8,128)(2,1)} %copy-done.4), kind=kLoop, calls=%fused_computation.8 | loop fusion | bytes 196608 | tf_op jit(solution)/shard_map/slice | solution.py:633
  12.7 7.7 %collective-permute-done.5.refs_1_ = bf16[3,16,32,128]{3,2,1,0:T(8,128)(2,1)S(1)} collective-permute-done((bf16[3,16,32,128]{3,2,1,0:T(8,128)(2,1)}, bf16[3,16,32,128]{3,2,1,0:T(8,128)(2,1)S(1)}, u32[]{:S(2)}, u32[]{:S(2)}) %collective-permute-start.5) | collective-permute-done | bytes 393248 | tf_op jit(solution)/shard_map/ppermute | solution.py:584
  20.4 0.7 %collective-permute-start.9 = (bf16[3,16,32,128]{3,2,1,0:T(8,128)(2,1)S(1)}, bf16[3,16,32,128]{3,2,1,0:T(8,128)(2,1)S(1)}, u32[]{:S(2)}, u32[]{:S(2)}) collective-permute-start(bf16[3,16,32,128]{3,2,1,0:T(8,128)(2,1)S(1)} %collective-permute-done.5.refs_1_), channel_id=1, source_target_pairs={{4,8},{12,16},{20,24},{8,4},{16,12},{24,20},{5,9},{13,17},{21,25},... | collective-permute-start | bytes 1179656 | tf_op jit(solution)/shard_map/ppermute | solution.py:594
  21.1 6.7 %collective-permute-done.4.refs_0_ = bf16[3,16,32,128]{3,2,1,0:T(8,128)(2,1)S(1)} collective-permute-done((bf16[3,16,32,128]{3,2,1,0:T(8,128)(2,1)}, bf16[3,16,32,128]{3,2,1,0:T(8,128)(2,1)S(1)}, u32[]{:S(2)}, u32[]{:S(2)}) %collective-permute-start.4) | collective-permute-done | bytes 393248 | tf_op jit(solution)/shard_map/ppermute | solution.py:584
  27.8 4.0 %collective-permute-start.10 = (bf16[3,16,32,128]{3,2,1,0:T(8,128)(2,1)S(1)}, bf16[3,16,32,128]{3,2,1,0:T(8,128)(2,1)S(1)}, u32[]{:S(2)}, u32[]{:S(2)}) collective-permute-start(bf16[3,16,32,128]{3,2,1,0:T(8,128)(2,1)S(1)} %collective-permute-done.4.refs_0_), channel_id=1, source_target_pairs={{0,4},{8,12},{16,20},{24,28},{4,0},{12,8},{20,16},{28,24},{1,5},{9... | collective-permute-start | bytes 1179656 | tf_op jit(solution)/shard_map/ppermute | solution.py:594
  31.8 0.0 collective-permute-done.1.refs_4_
  31.8 0.0 collective-permute-done.3.refs_5_
  31.8 0.1 collective-permute-start.7
  31.9 0.5 collective-permute-start.6
  32.5 0.0 collective-permute-done.refs_3_
  32.5 1.6 %collective-permute-start.8 = (bf16[3,4,32,128]{3,2,1,0:T(8,128)(2,1)S(1)}, bf16[3,4,32,128]{3,2,1,0:T(8,128)(2,1)S(1)}, u32[]{:S(2)}, u32[]{:S(2)}) collective-permute-start(bf16[3,4,32,128]{3,2,1,0:T(8,128)(2,1)S(1)} %bitcast.5), channel_id=1, source_target_pairs={{0,2},{1,3},{2,0},{3,1},{4,6},{5,7},{6,4},{7,5},{8,10},{9,11},{10,... | collective-permute-start | bytes 294920 | tf_op jit(solution)/shard_map/ppermute | solution.py:584
  34.1 0.0 collective-permute-done.7.refs_7_
  34.1 0.0 collective-permute-done.6.refs_6_
  34.1 2.3 %near_stage.1 = (bf16[3,2,16,2,2,16,128]{6,5,4,3,2,1,0:T(8,128)(2,1)S(1)}, f32[2,11,16,128]{3,2,1,0:T(8,128)S(1)}, f32[18,64,128]{2,1,0:T(8,128)S(1)}) custom-call(f32[64,64]{1,0:T(8,128)S(1)} %copy-done.3, f32[4,2,64,128]{3,2,1,0:T(8,128)S(1)} %copy-done.2, bf16[3,2,64,128]{3,2,1,0:T(8,128)(2,1)S(1)} %copy-done.1, ...), custom_call_target="tpu_custom_call" | custom-call | bytes 8388608 | tf_op jit(solution)/shard_map/near_stage/pallas_call | solution.py:324
  36.4 0.9 %collective-permute-done.8.refs_2_ = bf16[3,4,32,128]{3,2,1,0:T(8,128)(2,1)S(1)} collective-permute-done((bf16[3,4,32,128]{3,2,1,0:T(8,128)(2,1)S(1)}, bf16[3,4,32,128]{3,2,1,0:T(8,128)(2,1)S(1)}, u32[]{:S(2)}, u32[]{:S(2)}) %collective-permute-start.8) | collective-permute-done | bytes 98336 | tf_op jit(solution)/shard_map/ppermute | solution.py:584
  37.3 0.0 collective-permute-done.9.refs_3_
  37.3 1.7 %far_stage.1 = (bf16[3,1,16,128,128]{4,3,2,1,0:T(8,128)(2,1)S(1)}, f32[32,128]{1,0:T(8,128)S(1)}, f32[3,1,16,32,128]{4,3,2,1,0:T(8,128)S(1)}) custom-call(f32[2,11,16,128]{3,2,1,0:T(8,128)S(1)} %get-tuple-element.36.coef, f32[18,64,128]{2,1,0:T(8,128)S(1)} %get-tuple-element.38.amplitude, bf16[3,2,16,2,2,16,128]{6,5,4,3,2,1,0:T(8,128)(2,1)S(1)} %get-tuple-element.37.early, ...), custom_call_target="tpu_custom_call" | custom-call | bytes 8388608 | tf_op jit(solution)/shard_map/far_stage/pallas_call | solution.py:451
  39.1 2.8 %collective-permute-done.10.refs_0_ = bf16[3,16,32,128]{3,2,1,0:T(8,128)(2,1)S(1)} collective-permute-done((bf16[3,16,32,128]{3,2,1,0:T(8,128)(2,1)S(1)}, bf16[3,16,32,128]{3,2,1,0:T(8,128)(2,1)S(1)}, u32[]{:S(2)}, u32[]{:S(2)}) %collective-permute-start.10) | collective-permute-done | bytes 393248 | tf_op jit(solution)/shard_map/ppermute | solution.py:594
  41.9 1.3 %last_stage.1 = (bf16[3,1,16,128,128]{4,3,2,1,0:T(8,128)(2,1)S(1)}, f32[32,128]{1,0:T(8,128)S(1)}) custom-call(f32[2,11,16,128]{3,2,1,0:T(8,128)S(1)} %get-tuple-element.36.coef, bf16[3,2,16,2,2,16,128]{6,5,4,3,2,1,0:T(8,128)(2,1)S(1)} %get-tuple-element.37.early, f32[32,128]{1,0:T(8,128)S(1)} %get-tuple-element.40.before, ...), custom_call_target="tpu_custom_call" | custom-call | bytes 8388608 | tf_op jit(solution)/shard_map/last_stage/pallas_call | solution.py:451
  43.3 3.6 %collective-permute-start.13 = (f32[32,128]{1,0:T(8,128)S(1)}, f32[32,128]{1,0:T(8,128)S(1)}, u32[]{:S(2)}, u32[]{:S(2)}) collective-permute-start(f32[32,128]{1,0:T(8,128)S(1)} %get-tuple-element.42), channel_id=1, source_target_pairs={{0,24},{4,28},{8,16},{12,20},{16,8},{20,12},{24,0},{28,4},{1,25},{... | collective-permute-start | bytes 49160 | tf_op jit(solution)/shard_map/ppermute | solution.py:606
  46.8 0.0 collective-permute-start.12
  46.8 0.9 %collective-permute-start.11 = (f32[32,128]{1,0:T(8,128)S(1)}, f32[32,128]{1,0:T(8,128)S(1)}, u32[]{:S(2)}, u32[]{:S(2)}) collective-permute-start(f32[32,128]{1,0:T(8,128)S(1)} %get-tuple-element.42), channel_id=1, source_target_pairs={{0,8},{4,12},{8,0},{12,4},{16,24},{20,28},{24,16},{28,20},{1,9},{5... | collective-permute-start | bytes 49160 | tf_op jit(solution)/shard_map/ppermute | solution.py:606
  47.7 1.1 %collective-permute-done.13 = f32[32,128]{1,0:T(8,128)S(1)} collective-permute-done((f32[32,128]{1,0:T(8,128)S(1)}, f32[32,128]{1,0:T(8,128)S(1)}, u32[]{:S(2)}, u32[]{:S(2)}) %collective-permute-start.13) | collective-permute-done | bytes 16416 | tf_op jit(solution)/shard_map/ppermute | solution.py:606
  48.9 2.6 %collective-permute-done.12 = f32[32,128]{1,0:T(8,128)S(1)} collective-permute-done((f32[32,128]{1,0:T(8,128)S(1)}, f32[32,128]{1,0:T(8,128)S(1)}, u32[]{:S(2)}, u32[]{:S(2)}) %collective-permute-start.12) | collective-permute-done | bytes 16416 | tf_op jit(solution)/shard_map/ppermute | solution.py:606
  51.5 0.0 collective-permute-done.11
  51.5 1.1 %collective-permute-start.14 = (f32[32,128]{1,0:T(8,128)S(1)}, f32[32,128]{1,0:T(8,128)S(1)}, u32[]{:S(2)}, u32[]{:S(2)}) collective-permute-start(f32[32,128]{1,0:T(8,128)S(1)} %add_add_fusion.1), channel_id=1, source_target_pairs={{0,4},{4,0},{8,12},{12,8},{16,20},{20,16},{24,28},{28,24},{1,5},{5... | collective-permute-start | bytes 49160 | tf_op jit(solution)/shard_map/ppermute | solution.py:606
  52.6 2.7 %collective-permute-done.14 = f32[32,128]{1,0:T(8,128)S(1)} collective-permute-done((f32[32,128]{1,0:T(8,128)S(1)}, f32[32,128]{1,0:T(8,128)S(1)}, u32[]{:S(2)}, u32[]{:S(2)}) %collective-permute-start.14) | collective-permute-done | bytes 16416 | tf_op jit(solution)/shard_map/ppermute | solution.py:606
  55.3 0.0 collective-permute-start.17
  55.3 1.6 %collective-permute-start.16 = (f32[32,128]{1,0:T(8,128)S(1)}, f32[32,128]{1,0:T(8,128)S(1)}, u32[]{:S(2)}, u32[]{:S(2)}) collective-permute-start(f32[32,128]{1,0:T(8,128)S(1)} %add.29), channel_id=1, source_target_pairs={{0,2},{1,3},{2,0},{3,1},{4,6},{5,7},{6,4},{7,5},{8,10},{9,11},{10,... | collective-permute-start | bytes 49160 | tf_op jit(solution)/shard_map/ppermute | solution.py:606
  56.9 0.3 collective-permute-start.15
  57.1 1.4 %collective-permute-done.17 = f32[32,128]{1,0:T(8,128)S(1)} collective-permute-done((f32[32,128]{1,0:T(8,128)S(1)}, f32[32,128]{1,0:T(8,128)S(1)}, u32[]{:S(2)}, u32[]{:S(2)}) %collective-permute-start.17) | collective-permute-done | bytes 16416 | tf_op jit(solution)/shard_map/ppermute | solution.py:606
  58.6 0.5 collective-permute-done.16
  59.1 3.9 %whiten.1 = f32[64,3,2,16,128]{4,3,2,1,0:T(8,128)} custom-call(f32[32,128]{1,0:T(8,128)S(1)} %add_add_fusion.gram, bf16[3,1,16,128,128]{4,3,2,1,0:T(8,128)(2,1)S(1)} %get-tuple-element.43.refs_0_, bf16[3,1,16,128,128]{4,3,2,1,0:T(8,128)(2,1)S(1)} %get-tuple-element.44.refs_1_), custom_call_target="tpu_custom_call" | custom-call | tf_op jit(solution)/shard_map/whiten/pallas_call | solution.py:567
  (17 shorter events, 0.1 us)
Async XLA Ops:
  0.0 1.4 %copy-start = (bf16[16,3,2,64,128]{4,3,2,1,0:T(8,128)(2,1)S(1)}, bf16[16,3,2,64,128]{4,3,2,1,0:T(8,128)(2,1)}, u32[]{:S(2)}) copy-start(bf16[16,3,2,64,128]{4,3,2,1,0:T(8,128)(2,1)} %flow.4) | copy-start | bytes 4718596
  1.4 1.1 %copy-start.1 = (bf16[3,2,64,128]{3,2,1,0:T(8,128)(2,1)S(1)}, bf16[3,2,64,128]{3,2,1,0:T(8,128)(2,1)}, u32[]{:S(2)}) copy-start(bf16[3,2,64,128]{3,2,1,0:T(8,128)(2,1)} %large.3) | copy-start | bytes 294916
  2.0 4.4 %collective-permute-start.2 = (bf16[3,2,18,16,128]{4,3,2,0,1:T(8,128)(2,1)S(1)}, bf16[3,2,18,16,128]{4,3,2,0,1:T(8,128)(2,1)S(1)}, u32[]{:S(2)}, u32[]{:S(2)}) collective-permute-start(bf16[3,2,18,16,128]{4,3,2,0,1:T(8,128)(2,1)S(1)} %copy.7), channel_id=1, source_target_pairs={{0,1},{1,0},{2,3},{3,2},{4,5},{5,4},{6,7},{7,6},{8,9},{9,8},{10,11... | collective-permute-start | bytes 1327112 | tf_op jit(solution)/shard_map/ppermute | solution.py:588
  3.1 28.7 %collective-permute-start.1 = (bf16[3,33,16,128]{3,2,1,0:T(8,128)(2,1)S(1)}, bf16[3,33,16,128]{3,2,1,0:T(8,128)(2,1)S(1)}, u32[]{:S(2)}, u32[]{:S(2)}) collective-permute-start(bf16[3,33,16,128]{3,2,1,0:T(8,128)(2,1)S(1)} %get-tuple-element.26.refs_0_), channel_id=1, source_target_pairs={{0,4},{8,12},{16,20},{24,28},{4,0},{12,8},{20,16},{28,24},{1,5},{9... | collective-permute-start | bytes 1216520 | tf_op jit(solution)/shard_map/ppermute | solution.py:594
  6.5 3.2 %copy-start.4 = (bf16[3,2,18,32,128]{4,3,2,0,1:T(8,128)(2,1)}, bf16[3,2,18,32,128]{4,3,2,0,1:T(8,128)(2,1)S(1)}, u32[]{:S(2)}) copy-start(bf16[3,2,18,32,128]{4,3,2,0,1:T(8,128)(2,1)S(1)} %pad_maximum_fusion) | copy-start | bytes 2654212
  6.5 25.3 %collective-permute-start.3 = (bf16[3,33,16,128]{3,2,1,0:T(8,128)(2,1)S(1)}, bf16[3,33,16,128]{3,2,1,0:T(8,128)(2,1)S(1)}, u32[]{:S(2)}, u32[]{:S(2)}) collective-permute-start(bf16[3,33,16,128]{3,2,1,0:T(8,128)(2,1)S(1)} %get-tuple-element.32.refs_1_), channel_id=1, source_target_pairs={{4,8},{12,16},{20,24},{8,4},{16,12},{24,20},{5,9},{13,17},{21,25},... | collective-permute-start | bytes 1216520 | tf_op jit(solution)/shard_map/ppermute | solution.py:594
  8.2 25.9 %copy-start.2 = (f32[4,2,64,128]{3,2,1,0:T(8,128)S(1)}, f32[4,2,64,128]{3,2,1,0:T(8,128)}, u32[]{:S(2)}) copy-start(f32[4,2,64,128]{3,2,1,0:T(8,128)} %metric.1) | copy-start | bytes 786436
  8.2 25.9 %copy-start.3 = (f32[64,64]{1,0:T(8,128)S(1)}, f32[64,64]{1,0:T(8,128)}, u32[]{:S(2)}) copy-start(f32[64,64]{1,0:T(8,128)} %modulation.1) | copy-start | bytes 49156
  8.2 12.2 %collective-permute-start.5 = (bf16[3,16,32,128]{3,2,1,0:T(8,128)(2,1)}, bf16[3,16,32,128]{3,2,1,0:T(8,128)(2,1)S(1)}, u32[]{:S(2)}, u32[]{:S(2)}) collective-permute-start(bf16[3,16,32,128]{3,2,1,0:T(8,128)(2,1)} %get-tuple-element.47), channel_id=1, source_target_pairs={{0,2},{1,3},{2,0},{3,1},{4,6},{5,7},{6,4},{7,5},{8,10},{9,11},{10,... | collective-permute-start | bytes 1179656 | tf_op jit(solution)/shard_map/ppermute | solution.py:584
  9.7 18.1 %collective-permute-start.4 = (bf16[3,16,32,128]{3,2,1,0:T(8,128)(2,1)}, bf16[3,16,32,128]{3,2,1,0:T(8,128)(2,1)S(1)}, u32[]{:S(2)}, u32[]{:S(2)}) collective-permute-start(bf16[3,16,32,128]{3,2,1,0:T(8,128)(2,1)} %get-tuple-element.48), channel_id=1, source_target_pairs={{0,2},{1,3},{2,0},{3,1},{4,6},{5,7},{6,4},{7,5},{8,10},{9,11},{10,... | collective-permute-start | bytes 1179656 | tf_op jit(solution)/shard_map/ppermute | solution.py:584
  11.9 20.6 %collective-permute-start = (bf16[3,2,18,16,128]{4,3,2,1,0:T(8,128)(2,1)}, bf16[3,2,18,16,128]{4,3,2,1,0:T(8,128)(2,1)S(1)}, u32[]{:S(2)}, u32[]{:S(2)}) collective-permute-start(bf16[3,2,18,16,128]{4,3,2,1,0:T(8,128)(2,1)} %get-tuple-element.31), channel_id=1, source_target_pairs={{0,1},{1,0},{2,3},{3,2},{4,5},{5,4},{6,7},{7,6},{8,9},{9,8},{10,11... | collective-permute-start | bytes 1327112 | tf_op jit(solution)/shard_map/ppermute | solution.py:588
  20.4 16.9 %collective-permute-start.9 = (bf16[3,16,32,128]{3,2,1,0:T(8,128)(2,1)S(1)}, bf16[3,16,32,128]{3,2,1,0:T(8,128)(2,1)S(1)}, u32[]{:S(2)}, u32[]{:S(2)}) collective-permute-start(bf16[3,16,32,128]{3,2,1,0:T(8,128)(2,1)S(1)} %collective-permute-done.5.refs_1_), channel_id=1, source_target_pairs={{4,8},{12,16},{20,24},{8,4},{16,12},{24,20},{5,9},{13,17},{21,25},... | collective-permute-start | bytes 1179656 | tf_op jit(solution)/shard_map/ppermute | solution.py:594
  27.8 14.1 %collective-permute-start.10 = (bf16[3,16,32,128]{3,2,1,0:T(8,128)(2,1)S(1)}, bf16[3,16,32,128]{3,2,1,0:T(8,128)(2,1)S(1)}, u32[]{:S(2)}, u32[]{:S(2)}) collective-permute-start(bf16[3,16,32,128]{3,2,1,0:T(8,128)(2,1)S(1)} %collective-permute-done.4.refs_0_), channel_id=1, source_target_pairs={{0,4},{8,12},{16,20},{24,28},{4,0},{12,8},{20,16},{28,24},{1,5},{9... | collective-permute-start | bytes 1179656 | tf_op jit(solution)/shard_map/ppermute | solution.py:594
  31.8 2.3 %collective-permute-start.7 = (bf16[3,16,16,128]{3,2,1,0:T(8,128)(2,1)S(1)}, bf16[3,16,16,128]{3,2,1,0:T(8,128)(2,1)S(1)}, u32[]{:S(2)}, u32[]{:S(2)}) collective-permute-start(bf16[3,16,16,128]{3,2,1,0:T(8,128)(2,1)S(1)} %constant_dynamic-slice_fusion), channel_id=1, source_target_pairs={{0,1},{1,0},{2,3},{3,2},{4,5},{5,4},{6,7},{7,6},{8,9},{9,8},{10,11... | collective-permute-start | bytes 589832 | tf_op jit(solution)/shard_map/ppermute | solution.py:588
  31.9 2.1 %collective-permute-start.6 = (bf16[3,16,16,128]{3,2,1,0:T(8,128)(2,1)S(1)}, bf16[3,16,16,128]{3,2,1,0:T(8,128)(2,1)S(1)}, u32[]{:S(2)}, u32[]{:S(2)}) collective-permute-start(bf16[3,16,16,128]{3,2,1,0:T(8,128)(2,1)S(1)} %constant_dynamic-slice_fusion.1), channel_id=1, source_target_pairs={{0,1},{1,0},{2,3},{3,2},{4,5},{5,4},{6,7},{7,6},{8,9},{9,8},{10,11... | collective-permute-start | bytes 589832 | tf_op jit(solution)/shard_map/ppermute | solution.py:588
  32.5 4.8 %collective-permute-start.8 = (bf16[3,4,32,128]{3,2,1,0:T(8,128)(2,1)S(1)}, bf16[3,4,32,128]{3,2,1,0:T(8,128)(2,1)S(1)}, u32[]{:S(2)}, u32[]{:S(2)}) collective-permute-start(bf16[3,4,32,128]{3,2,1,0:T(8,128)(2,1)S(1)} %bitcast.5), channel_id=1, source_target_pairs={{0,2},{1,3},{2,0},{3,1},{4,6},{5,7},{6,4},{7,5},{8,10},{9,11},{10,... | collective-permute-start | bytes 294920 | tf_op jit(solution)/shard_map/ppermute | solution.py:584
  43.3 5.6 %collective-permute-start.13 = (f32[32,128]{1,0:T(8,128)S(1)}, f32[32,128]{1,0:T(8,128)S(1)}, u32[]{:S(2)}, u32[]{:S(2)}) collective-permute-start(f32[32,128]{1,0:T(8,128)S(1)} %get-tuple-element.42), channel_id=1, source_target_pairs={{0,24},{4,28},{8,16},{12,20},{16,8},{20,12},{24,0},{28,4},{1,25},{... | collective-permute-start | bytes 49160 | tf_op jit(solution)/shard_map/ppermute | solution.py:606
  46.8 4.6 %collective-permute-start.12 = (f32[32,128]{1,0:T(8,128)S(1)}, f32[32,128]{1,0:T(8,128)S(1)}, u32[]{:S(2)}, u32[]{:S(2)}) collective-permute-start(f32[32,128]{1,0:T(8,128)S(1)} %get-tuple-element.42), channel_id=1, source_target_pairs={{0,16},{4,20},{8,24},{12,28},{16,0},{20,4},{24,8},{28,12},{1,17},{... | collective-permute-start | bytes 49160 | tf_op jit(solution)/shard_map/ppermute | solution.py:606
  46.8 4.6 %collective-permute-start.11 = (f32[32,128]{1,0:T(8,128)S(1)}, f32[32,128]{1,0:T(8,128)S(1)}, u32[]{:S(2)}, u32[]{:S(2)}) collective-permute-start(f32[32,128]{1,0:T(8,128)S(1)} %get-tuple-element.42), channel_id=1, source_target_pairs={{0,8},{4,12},{8,0},{12,4},{16,24},{20,28},{24,16},{28,20},{1,9},{5... | collective-permute-start | bytes 49160 | tf_op jit(solution)/shard_map/ppermute | solution.py:606
  51.5 3.8 %collective-permute-start.14 = (f32[32,128]{1,0:T(8,128)S(1)}, f32[32,128]{1,0:T(8,128)S(1)}, u32[]{:S(2)}, u32[]{:S(2)}) collective-permute-start(f32[32,128]{1,0:T(8,128)S(1)} %add_add_fusion.1), channel_id=1, source_target_pairs={{0,4},{4,0},{8,12},{12,8},{16,20},{20,16},{24,28},{28,24},{1,5},{5... | collective-permute-start | bytes 49160 | tf_op jit(solution)/shard_map/ppermute | solution.py:606
  55.3 3.3 %collective-permute-start.17 = (f32[32,128]{1,0:T(8,128)S(1)}, f32[32,128]{1,0:T(8,128)S(1)}, u32[]{:S(2)}, u32[]{:S(2)}) collective-permute-start(f32[32,128]{1,0:T(8,128)S(1)} %add.29), channel_id=1, source_target_pairs={{0,3},{1,2},{2,1},{3,0},{4,7},{5,6},{6,5},{7,4},{8,11},{9,10},{10,... | collective-permute-start | bytes 49160 | tf_op jit(solution)/shard_map/ppermute | solution.py:606
  55.3 3.8 %collective-permute-start.16 = (f32[32,128]{1,0:T(8,128)S(1)}, f32[32,128]{1,0:T(8,128)S(1)}, u32[]{:S(2)}, u32[]{:S(2)}) collective-permute-start(f32[32,128]{1,0:T(8,128)S(1)} %add.29), channel_id=1, source_target_pairs={{0,2},{1,3},{2,0},{3,1},{4,6},{5,7},{6,4},{7,5},{8,10},{9,11},{10,... | collective-permute-start | bytes 49160 | tf_op jit(solution)/shard_map/ppermute | solution.py:606
  56.9 2.2 %collective-permute-start.15 = (f32[32,128]{1,0:T(8,128)S(1)}, f32[32,128]{1,0:T(8,128)S(1)}, u32[]{:S(2)}, u32[]{:S(2)}) collective-permute-start(f32[32,128]{1,0:T(8,128)S(1)} %add.29), channel_id=1, source_target_pairs={{0,1},{1,0},{2,3},{3,2},{4,5},{5,4},{6,7},{7,6},{8,9},{9,8},{10,11... | collective-permute-start | bytes 49160 | tf_op jit(solution)/shard_map/ppermute | solution.py:606

commit v8 on v7

--- a/solution.py
+++ b/solution.py
@@ -126,7 +126,7 @@
             ],
             out_specs=specs,
             out_shape=[jax.ShapeDtypeStruct(item, kind) for item in shapes],
-            scratch_shapes=[pltpu.VMEM((snaps * (width + 1), depth), jnp.float32)],
+            scratch_shapes=[pltpu.VMEM(((snaps + 1) * (width + 1), depth), jnp.float32)],
             compiler_params=params,
             name=name,
         )(here)
@@ -141,7 +141,7 @@
         out_shape=[jax.ShapeDtypeStruct((comps, item, snaps, depth), kind) for item in lengths],
         scratch_shapes=[
             pltpu.VMEM((planes * comps, snaps, span, depth), kind),
-            pltpu.VMEM((snaps * (span + 1), depth), jnp.float32),
+            pltpu.VMEM(((snaps + 1) * (span + 1), depth), jnp.float32),
             pltpu.VMEM(large.shape, kind),
             pltpu.VMEM(large.shape, jnp.float32),
             pltpu.SemaphoreType.DMA((planes * comps + 1,)),
@@ -506,7 +506,7 @@
     pieces, (out, slots, sems) = refs[:-3], refs[-3:]
     everyone = 2 * gram.shape[0]
     comps, cols, depth = pieces[0].shape[0], pieces[0].shape[2], pieces[0].shape[4]
-    pitch = slots.shape[1] // everyone
+    pitch = slots.shape[1] // (everyone + 1)
 
     def dot(a, b):
         (a_top, a_rest), (b_top, b_rest) = split(a), split(b)
@@ -544,10 +544,10 @@
                         slots[slot, pl.ds(first + sub, everyone, stride=pitch), :] = mixed[
                             :, sub * depth : (sub + 1) * depth
                         ]
-                source = slots.reshape(slots.shape[0], everyone, pitch, depth)
+                source = slots.reshape(slots.shape[0], everyone + 1, pitch, depth)
                 copies.append(
                     pltpu.make_async_copy(
-                        source.at[slot, :, pl.ds(0, cols)],
+                        source.at[slot, pl.ds(0, everyone), pl.ds(0, cols)],
                         out.at[:, comp, plane],
                         sems.at[slot],
                     )
@@ -570,7 +570,7 @@
         out_specs=pl.BlockSpec(memory_space=pl.ANY),
         out_shape=jax.ShapeDtypeStruct((everyone, comps, planes, cols, depth), jnp.float32),
         scratch_shapes=[
-            pltpu.VMEM((comps * planes, everyone * pitch, depth), jnp.float32),
+            pltpu.VMEM((comps * planes, (everyone + 1) * pitch, depth), jnp.float32),
             pltpu.SemaphoreType.DMA((comps * planes,)),
         ],
         compiler_params=pltpu.CompilerParams(vmem_limit_bytes=VMEM_BYTES),

time: 63.2 us -> 63.2 us (level)
  no operation moved by 1% of the time
where the time goes in v8:
time: 63.2 us; the launch traced here: 63 us
  waiting for transfers between devices  26.6 us (42%)
  starting transfers between devices  20.3 us (32%)
  Pallas kernels  12.5 us (20%)
  local copies, waits for them, and re-layouts  3.3 us (5%)
    ppermute x3, waiting for transfers between devices, to_chip(): return lax.ppermute(array, 'snap', pairs)  15.3 us
    ppermute x7, waiting for transfers between devices, all_sum(): lax.ppermute(value, axis, [(i, i ^ k) for i in range(lax.axis_size(axis))])  8.39 us
    ppermute x4, starting transfers between devices, to_pair(): return lax.ppermute(array, 'slab', pairs + [(j, i) for i, j in pairs])  8.18 us
    ppermute x7, starting transfers between devices, all_sum(): lax.ppermute(value, axis, [(i, i ^ k) for i in range(lax.axis_size(axis))])  7.43 us
    pallas_call x1, Pallas kernels, whiten(): pl.pallas_call(functools.partial(whiten_kernel, count), in_specs=[whole]...  3.89 us
    ppermute x3, starting transfers between devices, to_chip(): return lax.ppermute(array, 'snap', pairs)  3.58 us
    pallas_call x2, Pallas kernels, stage(): pl.pallas_call(kernel, in_specs=[whole] * len(wholes) + [pl.BlockSpec(mem...  3.07 us
    ppermute x4, waiting for transfers between devices, to_pair(): return lax.ppermute(array, 'slab', pairs + [(j, i) for i, j in pairs])  2.86 us
  transfers between devices with their start and end apart: 18, of which 9 were waited for; matrix products, arithmetic and copies ran while one was open for 3% of the time, Pallas kernels for 11%

profile of v8, /device:TPU:0, one launch (start us, length us, event | category | flops | bytes accessed | tf_op | source)
XLA Modules:
  0.0 63.0 jit_solution(14412732596550640525)
XLA Ops:
  0.0 1.4 %copy-done = bf16[16,3,2,64,128]{4,3,2,1,0:T(8,128)(2,1)S(1)} copy-done((bf16[16,3,2,64,128]{4,3,2,1,0:T(8,128)(2,1)S(1)}, bf16[16,3,2,64,128]{4,3,2,1,0:T(8,128)(2,1)}, u32[]{:S(2)}) %copy-start) | copy-done | bytes 1572888
  1.4 0.5 pack_other.1
  2.0 0.5 collective-permute-start.2
  2.5 0.6 pack_own.1
  3.1 2.8 %collective-permute-start.1 = (bf16[3,33,16,128]{3,2,1,0:T(8,128)(2,1)S(1)}, bf16[3,33,16,128]{3,2,1,0:T(8,128)(2,1)S(1)}, u32[]{:S(2)}, u32[]{:S(2)}) collective-permute-start(bf16[3,33,16,128]{3,2,1,0:T(8,128)(2,1)S(1)} %get-tuple-element.26.refs_0_), channel_id=1, source_target_pairs={{0,4},{8,12},{16,20},{24,28},{4,0},{12,8},{20,16},{28,24},{1,5},{9... | collective-permute-start | bytes 1216520 | tf_op jit(solution)/shard_map/ppermute | solution.py:594
  5.9 0.5 pack_mine.1
  6.4 0.0 collective-permute-done.2
  6.4 0.1 pad_maximum_fusion
  6.5 0.0 copy-start.4
  6.5 0.7 %collective-permute-start.3 = (bf16[3,33,16,128]{3,2,1,0:T(8,128)(2,1)S(1)}, bf16[3,33,16,128]{3,2,1,0:T(8,128)(2,1)S(1)}, u32[]{:S(2)}, u32[]{:S(2)}) collective-permute-start(bf16[3,33,16,128]{3,2,1,0:T(8,128)(2,1)S(1)} %get-tuple-element.32.refs_1_), channel_id=1, source_target_pairs={{4,8},{12,16},{20,24},{8,4},{16,12},{24,20},{5,9},{13,17},{21,25},... | collective-permute-start | bytes 1216520 | tf_op jit(solution)/shard_map/ppermute | solution.py:594
  7.2 1.0 %slice_bitcast_fusion = (bf16[3,16,32,128]{3,2,1,0:T(8,128)(2,1)}, bf16[3,16,32,128]{3,2,1,0:T(8,128)(2,1)}) fusion(bf16[3,2,18,32,128]{4,3,2,0,1:T(8,128)(2,1)S(1)} %pad_maximum_fusion), kind=kLoop, calls=%fused_computation.1 | loop fusion | bytes 1572864 | tf_op jit(solution)/shard_map/squeeze | solution.py:632
  8.2 1.5 %collective-permute-start.5 = (bf16[3,16,32,128]{3,2,1,0:T(8,128)(2,1)}, bf16[3,16,32,128]{3,2,1,0:T(8,128)(2,1)S(1)}, u32[]{:S(2)}, u32[]{:S(2)}) collective-permute-start(bf16[3,16,32,128]{3,2,1,0:T(8,128)(2,1)} %get-tuple-element.47), channel_id=1, source_target_pairs={{0,2},{1,3},{2,0},{3,1},{4,6},{5,7},{6,4},{7,5},{8,10},{9,11},{10,... | collective-permute-start | bytes 1179656 | tf_op jit(solution)/shard_map/ppermute | solution.py:584
  9.7 0.5 collective-permute-start.4
  10.2 1.7 %pack_near.1 = (bf16[3,4,16,128]{3,2,1,0:T(8,128)(2,1)S(1)}, bf16[3,2,18,16,128]{4,3,2,1,0:T(8,128)(2,1)}) custom-call(bf16[16,3,2,64,128]{4,3,2,1,0:T(8,128)(2,1)S(1)} %copy-done), custom_call_target="tpu_custom_call" | custom-call | tf_op jit(solution)/shard_map/pack_near/pallas_call | solution.py:121
  11.9 0.0 collective-permute-start
  11.9 0.8 %fusion = (bf16[3,2,1,32,128]{4,3,2,0,1:T(8,128)(2,1)S(1)}, bf16[3,2,1,32,128]{4,3,2,0,1:T(8,128)(2,1)S(1)}) fusion(bf16[3,2,18,32,128]{4,3,2,0,1:T(8,128)(2,1)} %copy-done.4), kind=kLoop, calls=%fused_computation.8 | loop fusion | bytes 196608 | tf_op jit(solution)/shard_map/slice | solution.py:633
  12.7 7.7 %collective-permute-done.5.refs_1_ = bf16[3,16,32,128]{3,2,1,0:T(8,128)(2,1)S(1)} collective-permute-done((bf16[3,16,32,128]{3,2,1,0:T(8,128)(2,1)}, bf16[3,16,32,128]{3,2,1,0:T(8,128)(2,1)S(1)}, u32[]{:S(2)}, u32[]{:S(2)}) %collective-permute-start.5) | collective-permute-done | bytes 393248 | tf_op jit(solution)/shard_map/ppermute | solution.py:584
  20.4 0.7 %collective-permute-start.9 = (bf16[3,16,32,128]{3,2,1,0:T(8,128)(2,1)S(1)}, bf16[3,16,32,128]{3,2,1,0:T(8,128)(2,1)S(1)}, u32[]{:S(2)}, u32[]{:S(2)}) collective-permute-start(bf16[3,16,32,128]{3,2,1,0:T(8,128)(2,1)S(1)} %collective-permute-done.5.refs_1_), channel_id=1, source_target_pairs={{4,8},{12,16},{20,24},{8,4},{16,12},{24,20},{5,9},{13,17},{21,25},... | collective-permute-start | bytes 1179656 | tf_op jit(solution)/shard_map/ppermute | solution.py:594
  21.1 6.8 %collective-permute-done.4.refs_0_ = bf16[3,16,32,128]{3,2,1,0:T(8,128)(2,1)S(1)} collective-permute-done((bf16[3,16,32,128]{3,2,1,0:T(8,128)(2,1)}, bf16[3,16,32,128]{3,2,1,0:T(8,128)(2,1)S(1)}, u32[]{:S(2)}, u32[]{:S(2)}) %collective-permute-start.4) | collective-permute-done | bytes 393248 | tf_op jit(solution)/shard_map/ppermute | solution.py:584
  27.8 4.0 %collective-permute-start.10 = (bf16[3,16,32,128]{3,2,1,0:T(8,128)(2,1)S(1)}, bf16[3,16,32,128]{3,2,1,0:T(8,128)(2,1)S(1)}, u32[]{:S(2)}, u32[]{:S(2)}) collective-permute-start(bf16[3,16,32,128]{3,2,1,0:T(8,128)(2,1)S(1)} %collective-permute-done.4.refs_0_), channel_id=1, source_target_pairs={{0,4},{8,12},{16,20},{24,28},{4,0},{12,8},{20,16},{28,24},{1,5},{9... | collective-permute-start | bytes 1179656 | tf_op jit(solution)/shard_map/ppermute | solution.py:594
  31.8 0.0 collective-permute-done.1.refs_4_
  31.8 0.0 collective-permute-done.3.refs_5_
  31.8 0.1 collective-permute-start.7
  31.9 0.5 collective-permute-start.6
  32.5 0.0 collective-permute-done.refs_3_
  32.5 1.6 %collective-permute-start.8 = (bf16[3,4,32,128]{3,2,1,0:T(8,128)(2,1)S(1)}, bf16[3,4,32,128]{3,2,1,0:T(8,128)(2,1)S(1)}, u32[]{:S(2)}, u32[]{:S(2)}) collective-permute-start(bf16[3,4,32,128]{3,2,1,0:T(8,128)(2,1)S(1)} %bitcast.5), channel_id=1, source_target_pairs={{0,2},{1,3},{2,0},{3,1},{4,6},{5,7},{6,4},{7,5},{8,10},{9,11},{10,... | collective-permute-start | bytes 294920 | tf_op jit(solution)/shard_map/ppermute | solution.py:584
  34.1 0.0 collective-permute-done.7.refs_7_
  34.1 0.0 collective-permute-done.6.refs_6_
  34.1 2.3 %near_stage.1 = (bf16[3,2,16,2,2,16,128]{6,5,4,3,2,1,0:T(8,128)(2,1)S(1)}, f32[2,11,16,128]{3,2,1,0:T(8,128)S(1)}, f32[18,64,128]{2,1,0:T(8,128)S(1)}) custom-call(f32[64,64]{1,0:T(8,128)S(1)} %copy-done.3, f32[4,2,64,128]{3,2,1,0:T(8,128)S(1)} %copy-done.2, bf16[3,2,64,128]{3,2,1,0:T(8,128)(2,1)S(1)} %copy-done.1, ...), custom_call_target="tpu_custom_call" | custom-call | bytes 8388608 | tf_op jit(solution)/shard_map/near_stage/pallas_call | solution.py:324
  36.4 0.9 %collective-permute-done.8.refs_2_ = bf16[3,4,32,128]{3,2,1,0:T(8,128)(2,1)S(1)} collective-permute-done((bf16[3,4,32,128]{3,2,1,0:T(8,128)(2,1)S(1)}, bf16[3,4,32,128]{3,2,1,0:T(8,128)(2,1)S(1)}, u32[]{:S(2)}, u32[]{:S(2)}) %collective-permute-start.8) | collective-permute-done | bytes 98336 | tf_op jit(solution)/shard_map/ppermute | solution.py:584
  37.3 0.0 collective-permute-done.9.refs_3_
  37.3 1.7 %far_stage.1 = (bf16[3,1,16,128,128]{4,3,2,1,0:T(8,128)(2,1)S(1)}, f32[32,128]{1,0:T(8,128)S(1)}, f32[3,1,16,32,128]{4,3,2,1,0:T(8,128)S(1)}) custom-call(f32[2,11,16,128]{3,2,1,0:T(8,128)S(1)} %get-tuple-element.36.coef, f32[18,64,128]{2,1,0:T(8,128)S(1)} %get-tuple-element.38.amplitude, bf16[3,2,16,2,2,16,128]{6,5,4,3,2,1,0:T(8,128)(2,1)S(1)} %get-tuple-element.37.early, ...), custom_call_target="tpu_custom_call" | custom-call | bytes 8388608 | tf_op jit(solution)/shard_map/far_stage/pallas_call | solution.py:451
  39.1 2.9 %collective-permute-done.10.refs_0_ = bf16[3,16,32,128]{3,2,1,0:T(8,128)(2,1)S(1)} collective-permute-done((bf16[3,16,32,128]{3,2,1,0:T(8,128)(2,1)S(1)}, bf16[3,16,32,128]{3,2,1,0:T(8,128)(2,1)S(1)}, u32[]{:S(2)}, u32[]{:S(2)}) %collective-permute-start.10) | collective-permute-done | bytes 393248 | tf_op jit(solution)/shard_map/ppermute | solution.py:594
  41.9 1.3 %last_stage.1 = (bf16[3,1,16,128,128]{4,3,2,1,0:T(8,128)(2,1)S(1)}, f32[32,128]{1,0:T(8,128)S(1)}) custom-call(f32[2,11,16,128]{3,2,1,0:T(8,128)S(1)} %get-tuple-element.36.coef, bf16[3,2,16,2,2,16,128]{6,5,4,3,2,1,0:T(8,128)(2,1)S(1)} %get-tuple-element.37.early, f32[32,128]{1,0:T(8,128)S(1)} %get-tuple-element.40.before, ...), custom_call_target="tpu_custom_call" | custom-call | bytes 8388608 | tf_op jit(solution)/shard_map/last_stage/pallas_call | solution.py:451
  43.3 3.6 %collective-permute-start.13 = (f32[32,128]{1,0:T(8,128)S(1)}, f32[32,128]{1,0:T(8,128)S(1)}, u32[]{:S(2)}, u32[]{:S(2)}) collective-permute-start(f32[32,128]{1,0:T(8,128)S(1)} %get-tuple-element.42), channel_id=1, source_target_pairs={{0,24},{4,28},{8,16},{12,20},{16,8},{20,12},{24,0},{28,4},{1,25},{... | collective-permute-start | bytes 49160 | tf_op jit(solution)/shard_map/ppermute | solution.py:606
  46.8 0.0 collective-permute-start.12
  46.8 0.9 %collective-permute-start.11 = (f32[32,128]{1,0:T(8,128)S(1)}, f32[32,128]{1,0:T(8,128)S(1)}, u32[]{:S(2)}, u32[]{:S(2)}) collective-permute-start(f32[32,128]{1,0:T(8,128)S(1)} %get-tuple-element.42), channel_id=1, source_target_pairs={{0,8},{4,12},{8,0},{12,4},{16,24},{20,28},{24,16},{28,20},{1,9},{5... | collective-permute-start | bytes 49160 | tf_op jit(solution)/shard_map/ppermute | solution.py:606
  47.7 1.1 %collective-permute-done.13 = f32[32,128]{1,0:T(8,128)S(1)} collective-permute-done((f32[32,128]{1,0:T(8,128)S(1)}, f32[32,128]{1,0:T(8,128)S(1)}, u32[]{:S(2)}, u32[]{:S(2)}) %collective-permute-start.13) | collective-permute-done | bytes 16416 | tf_op jit(solution)/shard_map/ppermute | solution.py:606
  48.9 2.6 %collective-permute-done.12 = f32[32,128]{1,0:T(8,128)S(1)} collective-permute-done((f32[32,128]{1,0:T(8,128)S(1)}, f32[32,128]{1,0:T(8,128)S(1)}, u32[]{:S(2)}, u32[]{:S(2)}) %collective-permute-start.12) | collective-permute-done | bytes 16416 | tf_op jit(solution)/shard_map/ppermute | solution.py:606
  51.5 1.1 %collective-permute-start.14 = (f32[32,128]{1,0:T(8,128)S(1)}, f32[32,128]{1,0:T(8,128)S(1)}, u32[]{:S(2)}, u32[]{:S(2)}) collective-permute-start(f32[32,128]{1,0:T(8,128)S(1)} %add_add_fusion.1), channel_id=1, source_target_pairs={{0,4},{4,0},{8,12},{12,8},{16,20},{20,16},{24,28},{28,24},{1,5},{5... | collective-permute-start | bytes 49160 | tf_op jit(solution)/shard_map/ppermute | solution.py:606
  52.6 2.7 %collective-permute-done.14 = f32[32,128]{1,0:T(8,128)S(1)} collective-permute-done((f32[32,128]{1,0:T(8,128)S(1)}, f32[32,128]{1,0:T(8,128)S(1)}, u32[]{:S(2)}, u32[]{:S(2)}) %collective-permute-start.14) | collective-permute-done | bytes 16416 | tf_op jit(solution)/shard_map/ppermute | solution.py:606
  55.3 0.0 collective-permute-start.17
  55.3 1.5 %collective-permute-start.16 = (f32[32,128]{1,0:T(8,128)S(1)}, f32[32,128]{1,0:T(8,128)S(1)}, u32[]{:S(2)}, u32[]{:S(2)}) collective-permute-start(f32[32,128]{1,0:T(8,128)S(1)} %add.29), channel_id=1, source_target_pairs={{0,2},{1,3},{2,0},{3,1},{4,6},{5,7},{6,4},{7,5},{8,10},{9,11},{10,... | collective-permute-start | bytes 49160 | tf_op jit(solution)/shard_map/ppermute | solution.py:606
  56.8 0.3 collective-permute-start.15
  57.2 1.4 %collective-permute-done.17 = f32[32,128]{1,0:T(8,128)S(1)} collective-permute-done((f32[32,128]{1,0:T(8,128)S(1)}, f32[32,128]{1,0:T(8,128)S(1)}, u32[]{:S(2)}, u32[]{:S(2)}) %collective-permute-start.17) | collective-permute-done | bytes 16416 | tf_op jit(solution)/shard_map/ppermute | solution.py:606
  58.6 0.5 collective-permute-done.16
  59.1 0.0 collective-permute-done.15
  59.1 3.9 %whiten.1 = f32[64,3,2,16,128]{4,3,2,1,0:T(8,128)} custom-call(f32[32,128]{1,0:T(8,128)S(1)} %add_add_fusion.gram, bf16[3,1,16,128,128]{4,3,2,1,0:T(8,128)(2,1)S(1)} %get-tuple-element.43.refs_0_, bf16[3,1,16,128,128]{4,3,2,1,0:T(8,128)(2,1)S(1)} %get-tuple-element.44.refs_1_), custom_call_target="tpu_custom_call" | custom-call | tf_op jit(solution)/shard_map/whiten/pallas_call | solution.py:567
  (17 shorter events, 0.1 us)
Async XLA Ops:
  0.0 1.4 %copy-start = (bf16[16,3,2,64,128]{4,3,2,1,0:T(8,128)(2,1)S(1)}, bf16[16,3,2,64,128]{4,3,2,1,0:T(8,128)(2,1)}, u32[]{:S(2)}) copy-start(bf16[16,3,2,64,128]{4,3,2,1,0:T(8,128)(2,1)} %flow.4) | copy-start | bytes 4718596
  1.4 1.1 %copy-start.1 = (bf16[3,2,64,128]{3,2,1,0:T(8,128)(2,1)S(1)}, bf16[3,2,64,128]{3,2,1,0:T(8,128)(2,1)}, u32[]{:S(2)}) copy-start(bf16[3,2,64,128]{3,2,1,0:T(8,128)(2,1)} %large.3) | copy-start | bytes 294916
  2.0 4.4 %collective-permute-start.2 = (bf16[3,2,18,16,128]{4,3,2,0,1:T(8,128)(2,1)S(1)}, bf16[3,2,18,16,128]{4,3,2,0,1:T(8,128)(2,1)S(1)}, u32[]{:S(2)}, u32[]{:S(2)}) collective-permute-start(bf16[3,2,18,16,128]{4,3,2,0,1:T(8,128)(2,1)S(1)} %copy.7), channel_id=1, source_target_pairs={{0,1},{1,0},{2,3},{3,2},{4,5},{5,4},{6,7},{7,6},{8,9},{9,8},{10,11... | collective-permute-start | bytes 1327112 | tf_op jit(solution)/shard_map/ppermute | solution.py:588
  3.1 28.7 %collective-permute-start.1 = (bf16[3,33,16,128]{3,2,1,0:T(8,128)(2,1)S(1)}, bf16[3,33,16,128]{3,2,1,0:T(8,128)(2,1)S(1)}, u32[]{:S(2)}, u32[]{:S(2)}) collective-permute-start(bf16[3,33,16,128]{3,2,1,0:T(8,128)(2,1)S(1)} %get-tuple-element.26.refs_0_), channel_id=1, source_target_pairs={{0,4},{8,12},{16,20},{24,28},{4,0},{12,8},{20,16},{28,24},{1,5},{9... | collective-permute-start | bytes 1216520 | tf_op jit(solution)/shard_map/ppermute | solution.py:594
  6.5 3.2 %copy-start.4 = (bf16[3,2,18,32,128]{4,3,2,0,1:T(8,128)(2,1)}, bf16[3,2,18,32,128]{4,3,2,0,1:T(8,128)(2,1)S(1)}, u32[]{:S(2)}) copy-start(bf16[3,2,18,32,128]{4,3,2,0,1:T(8,128)(2,1)S(1)} %pad_maximum_fusion) | copy-start | bytes 2654212
  6.5 25.3 %collective-permute-start.3 = (bf16[3,33,16,128]{3,2,1,0:T(8,128)(2,1)S(1)}, bf16[3,33,16,128]{3,2,1,0:T(8,128)(2,1)S(1)}, u32[]{:S(2)}, u32[]{:S(2)}) collective-permute-start(bf16[3,33,16,128]{3,2,1,0:T(8,128)(2,1)S(1)} %get-tuple-element.32.refs_1_), channel_id=1, source_target_pairs={{4,8},{12,16},{20,24},{8,4},{16,12},{24,20},{5,9},{13,17},{21,25},... | collective-permute-start | bytes 1216520 | tf_op jit(solution)/shard_map/ppermute | solution.py:594
  8.2 25.9 %copy-start.2 = (f32[4,2,64,128]{3,2,1,0:T(8,128)S(1)}, f32[4,2,64,128]{3,2,1,0:T(8,128)}, u32[]{:S(2)}) copy-start(f32[4,2,64,128]{3,2,1,0:T(8,128)} %metric.1) | copy-start | bytes 786436
  8.2 25.9 %copy-start.3 = (f32[64,64]{1,0:T(8,128)S(1)}, f32[64,64]{1,0:T(8,128)}, u32[]{:S(2)}) copy-start(f32[64,64]{1,0:T(8,128)} %modulation.1) | copy-start | bytes 49156
  8.2 12.2 %collective-permute-start.5 = (bf16[3,16,32,128]{3,2,1,0:T(8,128)(2,1)}, bf16[3,16,32,128]{3,2,1,0:T(8,128)(2,1)S(1)}, u32[]{:S(2)}, u32[]{:S(2)}) collective-permute-start(bf16[3,16,32,128]{3,2,1,0:T(8,128)(2,1)} %get-tuple-element.47), channel_id=1, source_target_pairs={{0,2},{1,3},{2,0},{3,1},{4,6},{5,7},{6,4},{7,5},{8,10},{9,11},{10,... | collective-permute-start | bytes 1179656 | tf_op jit(solution)/shard_map/ppermute | solution.py:584
  9.7 18.1 %collective-permute-start.4 = (bf16[3,16,32,128]{3,2,1,0:T(8,128)(2,1)}, bf16[3,16,32,128]{3,2,1,0:T(8,128)(2,1)S(1)}, u32[]{:S(2)}, u32[]{:S(2)}) collective-permute-start(bf16[3,16,32,128]{3,2,1,0:T(8,128)(2,1)} %get-tuple-element.48), channel_id=1, source_target_pairs={{0,2},{1,3},{2,0},{3,1},{4,6},{5,7},{6,4},{7,5},{8,10},{9,11},{10,... | collective-permute-start | bytes 1179656 | tf_op jit(solution)/shard_map/ppermute | solution.py:584
  11.9 20.6 %collective-permute-start = (bf16[3,2,18,16,128]{4,3,2,1,0:T(8,128)(2,1)}, bf16[3,2,18,16,128]{4,3,2,1,0:T(8,128)(2,1)S(1)}, u32[]{:S(2)}, u32[]{:S(2)}) collective-permute-start(bf16[3,2,18,16,128]{4,3,2,1,0:T(8,128)(2,1)} %get-tuple-element.31), channel_id=1, source_target_pairs={{0,1},{1,0},{2,3},{3,2},{4,5},{5,4},{6,7},{7,6},{8,9},{9,8},{10,11... | collective-permute-start | bytes 1327112 | tf_op jit(solution)/shard_map/ppermute | solution.py:588
  20.4 16.9 %collective-permute-start.9 = (bf16[3,16,32,128]{3,2,1,0:T(8,128)(2,1)S(1)}, bf16[3,16,32,128]{3,2,1,0:T(8,128)(2,1)S(1)}, u32[]{:S(2)}, u32[]{:S(2)}) collective-permute-start(bf16[3,16,32,128]{3,2,1,0:T(8,128)(2,1)S(1)} %collective-permute-done.5.refs_1_), channel_id=1, source_target_pairs={{4,8},{12,16},{20,24},{8,4},{16,12},{24,20},{5,9},{13,17},{21,25},... | collective-permute-start | bytes 1179656 | tf_op jit(solution)/shard_map/ppermute | solution.py:594
  27.8 14.1 %collective-permute-start.10 = (bf16[3,16,32,128]{3,2,1,0:T(8,128)(2,1)S(1)}, bf16[3,16,32,128]{3,2,1,0:T(8,128)(2,1)S(1)}, u32[]{:S(2)}, u32[]{:S(2)}) collective-permute-start(bf16[3,16,32,128]{3,2,1,0:T(8,128)(2,1)S(1)} %collective-permute-done.4.refs_0_), channel_id=1, source_target_pairs={{0,4},{8,12},{16,20},{24,28},{4,0},{12,8},{20,16},{28,24},{1,5},{9... | collective-permute-start | bytes 1179656 | tf_op jit(solution)/shard_map/ppermute | solution.py:594
  31.8 2.3 %collective-permute-start.7 = (bf16[3,16,16,128]{3,2,1,0:T(8,128)(2,1)S(1)}, bf16[3,16,16,128]{3,2,1,0:T(8,128)(2,1)S(1)}, u32[]{:S(2)}, u32[]{:S(2)}) collective-permute-start(bf16[3,16,16,128]{3,2,1,0:T(8,128)(2,1)S(1)} %constant_dynamic-slice_fusion), channel_id=1, source_target_pairs={{0,1},{1,0},{2,3},{3,2},{4,5},{5,4},{6,7},{7,6},{8,9},{9,8},{10,11... | collective-permute-start | bytes 589832 | tf_op jit(solution)/shard_map/ppermute | solution.py:588
  31.9 2.1 %collective-permute-start.6 = (bf16[3,16,16,128]{3,2,1,0:T(8,128)(2,1)S(1)}, bf16[3,16,16,128]{3,2,1,0:T(8,128)(2,1)S(1)}, u32[]{:S(2)}, u32[]{:S(2)}) collective-permute-start(bf16[3,16,16,128]{3,2,1,0:T(8,128)(2,1)S(1)} %constant_dynamic-slice_fusion.1), channel_id=1, source_target_pairs={{0,1},{1,0},{2,3},{3,2},{4,5},{5,4},{6,7},{7,6},{8,9},{9,8},{10,11... | collective-permute-start | bytes 589832 | tf_op jit(solution)/shard_map/ppermute | solution.py:588
  32.5 4.8 %collective-permute-start.8 = (bf16[3,4,32,128]{3,2,1,0:T(8,128)(2,1)S(1)}, bf16[3,4,32,128]{3,2,1,0:T(8,128)(2,1)S(1)}, u32[]{:S(2)}, u32[]{:S(2)}) collective-permute-start(bf16[3,4,32,128]{3,2,1,0:T(8,128)(2,1)S(1)} %bitcast.5), channel_id=1, source_target_pairs={{0,2},{1,3},{2,0},{3,1},{4,6},{5,7},{6,4},{7,5},{8,10},{9,11},{10,... | collective-permute-start | bytes 294920 | tf_op jit(solution)/shard_map/ppermute | solution.py:584
  43.3 5.6 %collective-permute-start.13 = (f32[32,128]{1,0:T(8,128)S(1)}, f32[32,128]{1,0:T(8,128)S(1)}, u32[]{:S(2)}, u32[]{:S(2)}) collective-permute-start(f32[32,128]{1,0:T(8,128)S(1)} %get-tuple-element.42), channel_id=1, source_target_pairs={{0,24},{4,28},{8,16},{12,20},{16,8},{20,12},{24,0},{28,4},{1,25},{... | collective-permute-start | bytes 49160 | tf_op jit(solution)/shard_map/ppermute | solution.py:606
  46.8 4.6 %collective-permute-start.12 = (f32[32,128]{1,0:T(8,128)S(1)}, f32[32,128]{1,0:T(8,128)S(1)}, u32[]{:S(2)}, u32[]{:S(2)}) collective-permute-start(f32[32,128]{1,0:T(8,128)S(1)} %get-tuple-element.42), channel_id=1, source_target_pairs={{0,16},{4,20},{8,24},{12,28},{16,0},{20,4},{24,8},{28,12},{1,17},{... | collective-permute-start | bytes 49160 | tf_op jit(solution)/shard_map/ppermute | solution.py:606
  46.8 4.6 %collective-permute-start.11 = (f32[32,128]{1,0:T(8,128)S(1)}, f32[32,128]{1,0:T(8,128)S(1)}, u32[]{:S(2)}, u32[]{:S(2)}) collective-permute-start(f32[32,128]{1,0:T(8,128)S(1)} %get-tuple-element.42), channel_id=1, source_target_pairs={{0,8},{4,12},{8,0},{12,4},{16,24},{20,28},{24,16},{28,20},{1,9},{5... | collective-permute-start | bytes 49160 | tf_op jit(solution)/shard_map/ppermute | solution.py:606
  51.5 3.8 %collective-permute-start.14 = (f32[32,128]{1,0:T(8,128)S(1)}, f32[32,128]{1,0:T(8,128)S(1)}, u32[]{:S(2)}, u32[]{:S(2)}) collective-permute-start(f32[32,128]{1,0:T(8,128)S(1)} %add_add_fusion.1), channel_id=1, source_target_pairs={{0,4},{4,0},{8,12},{12,8},{16,20},{20,16},{24,28},{28,24},{1,5},{5... | collective-permute-start | bytes 49160 | tf_op jit(solution)/shard_map/ppermute | solution.py:606
  55.3 3.3 %collective-permute-start.17 = (f32[32,128]{1,0:T(8,128)S(1)}, f32[32,128]{1,0:T(8,128)S(1)}, u32[]{:S(2)}, u32[]{:S(2)}) collective-permute-start(f32[32,128]{1,0:T(8,128)S(1)} %add.29), channel_id=1, source_target_pairs={{0,3},{1,2},{2,1},{3,0},{4,7},{5,6},{6,5},{7,4},{8,11},{9,10},{10,... | collective-permute-start | bytes 49160 | tf_op jit(solution)/shard_map/ppermute | solution.py:606
  55.3 3.8 %collective-permute-start.16 = (f32[32,128]{1,0:T(8,128)S(1)}, f32[32,128]{1,0:T(8,128)S(1)}, u32[]{:S(2)}, u32[]{:S(2)}) collective-permute-start(f32[32,128]{1,0:T(8,128)S(1)} %add.29), channel_id=1, source_target_pairs={{0,2},{1,3},{2,0},{3,1},{4,6},{5,7},{6,4},{7,5},{8,10},{9,11},{10,... | collective-permute-start | bytes 49160 | tf_op jit(solution)/shard_map/ppermute | solution.py:606
  56.8 2.3 %collective-permute-start.15 = (f32[32,128]{1,0:T(8,128)S(1)}, f32[32,128]{1,0:T(8,128)S(1)}, u32[]{:S(2)}, u32[]{:S(2)}) collective-permute-start(f32[32,128]{1,0:T(8,128)S(1)} %add.29), channel_id=1, source_target_pairs={{0,1},{1,0},{2,3},{3,2},{4,5},{5,4},{6,7},{7,6},{8,9},{9,8},{10,11... | collective-permute-start | bytes 49160 | tf_op jit(solution)/shard_map/ppermute | solution.py:606
